TPU v7x, 32 devices: a whole 2x2x4 slice. The times are simulated.
32 devices in a mesh: dp: 4 (over x, core), sp: 4 (over z), blk: 2 (over y).
Axes of the slice: x: 2, y: 2, z: 4, core: 2. Of those that a mesh axis runs over, the one named last changes fastest.
Arguments:
- inputs: bfloat16 [8192, 1024], P(('dp', 'sp', 'blk')), may hold values from -6 to 6
- w_qkv: bfloat16 [1024, 3072], P(('dp', 'sp', 'blk')), may hold values from -0.1875 to 0.1875
- w_dense: bfloat16 [1024, 1024], P(('dp', 'sp', 'blk')), may hold values from -0.75 to 0.75
- w_in: bfloat16 [1024, 4096], P(('dp', 'sp', 'blk')), may hold values from -0.1875 to 0.1875
- w_out: bfloat16 [4096, 1024], P(('dp', 'sp', 'blk')), may hold values from -0.09375 to 0.09375
- norm_gains: bfloat16 [2, 1024], P(None, ('dp', 'sp', 'blk')), may hold values from 0.5 to 1.5
- biases: bfloat16 [6, 1024], P(None, ('dp', 'sp', 'blk')), may hold values from -3 to 3
- in_bias: bfloat16 [4096], P(('dp', 'sp', 'blk')), may hold values from -3 to 3
- alibi_slopes: float32 [16], replicated, may hold values from 0.00024414062 to 0.1
- upstream: bfloat16 [8192, 1024], P(('dp', 'sp', 'blk')), may hold values from -6 to 6
Outputs:
- output: bfloat16 [8192, 1024], P(('dp', 'sp', 'blk'))
- grad_inputs: float32 [8192, 1024], P(('dp', 'sp', 'blk'))
- grad_w_qkv: float32 [1024, 3072], P(('dp', 'sp', 'blk'))
- grad_w_dense: float32 [1024, 1024], P(('dp', 'sp', 'blk'))
- grad_w_in: float32 [1024, 4096], P(('dp', 'sp', 'blk'))
- grad_w_out: float32 [4096, 1024], P(('dp', 'sp', 'blk'))
- grad_norm_gains: float32 [2, 1024], P(None, ('dp', 'sp', 'blk'))
- grad_biases: float32 [6, 1024], P(None, ('dp', 'sp', 'blk'))
- grad_in_bias: float32 [4096], P(('dp', 'sp', 'blk'))
All inputs are finite; a program needn't handle non-finite values.
Results may differ from a plain program's by a relative error of at most 0.0096.
Values may be sent and summed in bfloat16 or wider, within the bound.
No kernel may reach another device: no remote copies, remote signals or barrier semaphores. Data moves between devices by JAX's collectives and lax.ppermute only.
A program may use at most 192 MiB of HBM per device.

v0:
```python
import math

import jax
import jax.numpy as jnp
from jax import lax
from jax.sharding import PartitionSpec as P

H = 16


def norm_rows(features, gain_row, offset):
    row_mean = jnp.mean(features, axis=-1, keepdims=True)
    centered = features - row_mean
    variance = jnp.mean(centered * centered, axis=-1, keepdims=True)
    return centered * lax.rsqrt(variance + 1e-05) * gain_row + offset


def head_scores(query_rows, row_places, key_rows, key_places, slopes, score_scale):
    scores = (
        jnp.einsum("qhe,khe->hqk", query_rows, key_rows, preferred_element_type=jnp.float32)
        * score_scale
    )
    distance = (row_places[:, None] - key_places[None, :]).astype(jnp.float32)
    scores = scores - slopes[:, None, None] * distance[None]
    return jnp.where((distance >= 0)[None], scores, -1e30)


def on_device(
    inputs, w_qkv, w_dense, w_in, w_out, norm_gains, biases, in_bias, alibi_slopes, upstream
):
    gathered = (
        lax.all_gather(w_qkv, ("dp", "sp", "blk"), axis=0, tiled=True),
        lax.all_gather(w_dense, ("dp", "sp", "blk"), axis=0, tiled=True),
        lax.all_gather(w_in, ("dp", "sp", "blk"), axis=0, tiled=True),
        lax.all_gather(w_out, ("dp", "sp", "blk"), axis=0, tiled=True),
        lax.all_gather(norm_gains, ("dp", "sp", "blk"), axis=1, tiled=True),
        lax.all_gather(biases, ("dp", "sp", "blk"), axis=1, tiled=True),
        lax.all_gather(in_bias, ("dp", "sp", "blk"), axis=0, tiled=True),
    )
    qkv_full, dense_full, in_full, out_full, gains_full, offsets_full, in_bias_full = gathered
    gains_row = gains_full.astype(jnp.float32)
    offsets = offsets_full.astype(jnp.float32)
    in_offset = in_bias_full.astype(jnp.float32)
    tok_rows = inputs.shape[0]
    model_width = inputs.shape[1]
    head_dim = model_width // H
    score_scale = 1.0 / math.sqrt(head_dim)
    sp_count = lax.axis_size("sp")
    cycle_count = lax.axis_size("blk")
    local_rows = sp_count * tok_rows
    key_count = cycle_count * local_rows
    cycle_place = lax.axis_index("blk")
    row_index = jnp.arange(local_rows, dtype=jnp.int32)
    row_places = (
        row_index // tok_rows * cycle_count + cycle_place
    ) * tok_rows + row_index % tok_rows
    key_index = jnp.arange(key_count, dtype=jnp.int32)
    key_rest = key_index % local_rows
    key_places = (
        key_rest // tok_rows * cycle_count + key_index // local_rows
    ) * tok_rows + key_rest % tok_rows
    rows_in = inputs.astype(jnp.float32)
    normed_one = norm_rows(rows_in, gains_row[0], offsets[0]).astype(jnp.bfloat16)
    projected = jnp.dot(normed_one, qkv_full, preferred_element_type=jnp.float32)
    query_tok = (projected[:, :model_width] + offsets[1]).astype(jnp.bfloat16)
    key_tok = projected[:, model_width : 2 * model_width].astype(jnp.bfloat16)
    value_tok = (projected[:, 2 * model_width :] + offsets[2]).astype(jnp.bfloat16)
    query_heads, key_heads, value_heads = (
        lax.all_to_all(query_tok, "sp", split_axis=1, concat_axis=0, tiled=True),
        lax.all_to_all(key_tok, "sp", split_axis=1, concat_axis=0, tiled=True),
        lax.all_to_all(value_tok, "sp", split_axis=1, concat_axis=0, tiled=True),
    )
    local_heads = query_heads.shape[1] // head_dim
    key_group, value_group = (
        lax.all_gather(key_heads, "blk", axis=0, tiled=True),
        lax.all_gather(value_heads, "blk", axis=0, tiled=True),
    )
    query_rows = query_heads.reshape(local_rows, local_heads, head_dim)
    key_rows = key_group.reshape(key_count, local_heads, head_dim)
    value_rows = value_group.reshape(key_count, local_heads, head_dim)
    slopes = lax.dynamic_slice_in_dim(alibi_slopes, lax.axis_index("sp") * local_heads, local_heads)
    block_rows = min(512, local_rows)
    firsts = jnp.arange(local_rows // block_rows, dtype=jnp.int32) * block_rows

    def forward_block(first_row):
        chosen = lax.dynamic_slice_in_dim(query_rows, first_row, block_rows, 0)
        places = lax.dynamic_slice_in_dim(row_places, first_row, block_rows, 0)
        scores = head_scores(chosen, places, key_rows, key_places, slopes, score_scale)
        row_top = jnp.max(scores, axis=-1, keepdims=True)
        exponent = jnp.exp(scores - row_top)
        row_total = jnp.sum(exponent, axis=-1, keepdims=True)
        soft_weights = (exponent / row_total).astype(jnp.bfloat16)
        context = jnp.einsum(
            "hqk,khe->qhe", soft_weights, value_rows, preferred_element_type=jnp.float32
        )
        return (context.astype(jnp.bfloat16), row_top, row_total)

    contexts, row_tops, row_totals = lax.map(forward_block, firsts)
    context_heads = contexts.reshape(local_rows, local_heads * head_dim)
    context_tok = lax.all_to_all(context_heads, "sp", split_axis=0, concat_axis=1, tiled=True)
    attended = jnp.dot(context_tok, dense_full, preferred_element_type=jnp.float32) + offsets[3]
    middle = rows_in + attended
    normed_two = norm_rows(middle, gains_row[1], offsets[4]).astype(jnp.bfloat16)
    hidden_pre = jnp.dot(normed_two, in_full, preferred_element_type=jnp.float32) + in_offset
    hidden = jax.nn.gelu(hidden_pre).astype(jnp.bfloat16)
    branch = jnp.dot(hidden, out_full, preferred_element_type=jnp.float32) + offsets[5]
    output = (middle + branch).astype(jnp.bfloat16)
    gathered = (
        lax.all_gather(w_qkv, ("dp", "sp", "blk"), axis=0, tiled=True),
        lax.all_gather(w_dense, ("dp", "sp", "blk"), axis=0, tiled=True),
        lax.all_gather(w_in, ("dp", "sp", "blk"), axis=0, tiled=True),
        lax.all_gather(w_out, ("dp", "sp", "blk"), axis=0, tiled=True),
        lax.all_gather(norm_gains, ("dp", "sp", "blk"), axis=1, tiled=True),
        lax.all_gather(biases, ("dp", "sp", "blk"), axis=1, tiled=True),
        lax.all_gather(in_bias, ("dp", "sp", "blk"), axis=0, tiled=True),
    )
    qkv_full, dense_full, in_full, out_full, gains_full, offsets_full, in_bias_full = gathered
    gains_row = gains_full.astype(jnp.float32)
    offsets = offsets_full.astype(jnp.float32)
    grad_top = upstream.astype(jnp.float32)
    grad_w_out = jnp.einsum("tf,td->fd", hidden, upstream, preferred_element_type=jnp.float32)
    grad_out_bias = jnp.sum(grad_top, axis=0)
    grad_hidden = jnp.einsum("td,fd->tf", upstream, out_full, preferred_element_type=jnp.float32)
    _, gelu_pull = jax.vjp(jax.nn.gelu, hidden_pre)
    grad_pre = gelu_pull(grad_hidden)[0].astype(jnp.bfloat16)
    grad_w_in = jnp.einsum("td,tf->df", normed_two, grad_pre, preferred_element_type=jnp.float32)
    grad_in_bias = jnp.sum(grad_pre.astype(jnp.float32), axis=0)
    grad_normed_two = jnp.einsum("tf,df->td", grad_pre, in_full, preferred_element_type=jnp.float32)
    _, second_pull = jax.vjp(norm_rows, middle, gains_row[1], offsets[4])
    grad_mid_part, grad_gain_two, grad_shift_two = second_pull(grad_normed_two)
    grad_middle = grad_top + grad_mid_part
    grad_att = grad_middle.astype(jnp.bfloat16)
    grad_w_dense = jnp.einsum(
        "td,te->de", context_tok, grad_att, preferred_element_type=jnp.float32
    )
    grad_dense_bias = jnp.sum(grad_att.astype(jnp.float32), axis=0)
    grad_context = jnp.einsum(
        "te,de->td", grad_att, dense_full, preferred_element_type=jnp.float32
    ).astype(jnp.bfloat16)
    grad_context_heads = lax.all_to_all(grad_context, "sp", split_axis=1, concat_axis=0, tiled=True)
    grad_context_rows = grad_context_heads.reshape(local_rows, local_heads, head_dim)

    def backward_step(running, step_item):
        grad_keys, grad_values = running
        first_row, row_top, row_total = step_item
        chosen = lax.dynamic_slice_in_dim(query_rows, first_row, block_rows, 0)
        places = lax.dynamic_slice_in_dim(row_places, first_row, block_rows, 0)
        grad_rows = lax.dynamic_slice_in_dim(grad_context_rows, first_row, block_rows, 0)
        scores = head_scores(chosen, places, key_rows, key_places, slopes, score_scale)
        soft_weights = jnp.exp(scores - row_top) / row_total
        grad_values = grad_values + jnp.einsum(
            "hqk,qhe->khe",
            soft_weights.astype(jnp.bfloat16),
            grad_rows,
            preferred_element_type=jnp.float32,
        )
        grad_probs = jnp.einsum(
            "qhe,khe->hqk", grad_rows, value_rows, preferred_element_type=jnp.float32
        )
        grad_scores = (
            soft_weights * (grad_probs - jnp.sum(soft_weights * grad_probs, axis=-1, keepdims=True))
        ).astype(jnp.bfloat16)
        grad_query = (
            jnp.einsum("hqk,khe->qhe", grad_scores, key_rows, preferred_element_type=jnp.float32)
            * score_scale
        )
        grad_keys = (
            grad_keys
            + jnp.einsum("hqk,qhe->khe", grad_scores, chosen, preferred_element_type=jnp.float32)
            * score_scale
        )
        return ((grad_keys, grad_values), grad_query.astype(jnp.bfloat16))

    empty = jnp.zeros((key_count, local_heads, head_dim), jnp.float32)
    (grad_keys_all, grad_values_all), grad_queries = lax.scan(
        backward_step, (empty, empty), (firsts, row_tops, row_totals)
    )
    grad_keys_own, grad_values_own = (
        lax.psum_scatter(
            grad_keys_all.reshape(key_count, local_heads * head_dim),
            "blk",
            scatter_dimension=0,
            tiled=True,
        ),
        lax.psum_scatter(
            grad_values_all.reshape(key_count, local_heads * head_dim),
            "blk",
            scatter_dimension=0,
            tiled=True,
        ),
    )
    grad_query_heads = grad_queries.reshape(local_rows, local_heads * head_dim)
    grad_query_tok, grad_key_tok, grad_value_tok = (
        lax.all_to_all(grad_query_heads, "sp", split_axis=0, concat_axis=1, tiled=True),
        lax.all_to_all(
            grad_keys_own.astype(jnp.bfloat16), "sp", split_axis=0, concat_axis=1, tiled=True
        ),
        lax.all_to_all(
            grad_values_own.astype(jnp.bfloat16), "sp", split_axis=0, concat_axis=1, tiled=True
        ),
    )
    grad_projected = jnp.concatenate([grad_query_tok, grad_key_tok, grad_value_tok], axis=1)
    grad_w_qkv = jnp.einsum(
        "td,tc->dc", normed_one, grad_projected, preferred_element_type=jnp.float32
    )
    grad_query_bias = jnp.sum(grad_query_tok.astype(jnp.float32), axis=0)
    grad_value_bias = jnp.sum(grad_value_tok.astype(jnp.float32), axis=0)
    grad_normed_one = jnp.einsum(
        "tc,dc->td", grad_projected, qkv_full, preferred_element_type=jnp.float32
    )
    _, first_pull = jax.vjp(norm_rows, rows_in, gains_row[0], offsets[0])
    grad_rows_part, grad_gain_one, grad_shift_one = first_pull(grad_normed_one)
    grad_inputs = grad_middle + grad_rows_part
    grad_gains_local = jnp.stack([grad_gain_one, grad_gain_two], axis=0)
    grad_biases_local = jnp.stack(
        [
            grad_shift_one,
            grad_query_bias,
            grad_value_bias,
            grad_dense_bias,
            grad_shift_two,
            grad_out_bias,
        ],
        axis=0,
    )
    summed = (
        lax.psum_scatter(grad_w_qkv, ("dp", "sp", "blk"), scatter_dimension=0, tiled=True),
        lax.psum_scatter(grad_w_dense, ("dp", "sp", "blk"), scatter_dimension=0, tiled=True),
        lax.psum_scatter(grad_w_in, ("dp", "sp", "blk"), scatter_dimension=0, tiled=True),
        lax.psum_scatter(grad_w_out, ("dp", "sp", "blk"), scatter_dimension=0, tiled=True),
        lax.psum_scatter(grad_gains_local, ("dp", "sp", "blk"), scatter_dimension=1, tiled=True),
        lax.psum_scatter(grad_biases_local, ("dp", "sp", "blk"), scatter_dimension=1, tiled=True),
        lax.psum_scatter(grad_in_bias, ("dp", "sp", "blk"), scatter_dimension=0, tiled=True),
    )
    return (
        output,
        grad_inputs,
        summed[0],
        summed[1],
        summed[2],
        summed[3],
        summed[4],
        summed[5],
        summed[6],
    )


def solution(mesh):
    in_specs = (
        P(("dp", "sp", "blk"), None),
        P(("dp", "sp", "blk"), None),
        P(("dp", "sp", "blk"), None),
        P(("dp", "sp", "blk"), None),
        P(("dp", "sp", "blk"), None),
        P(None, ("dp", "sp", "blk")),
        P(None, ("dp", "sp", "blk")),
        P(("dp", "sp", "blk")),
        P(),
        P(("dp", "sp", "blk"), None),
    )
    out_specs = (
        P(("dp", "sp", "blk"), None),
        P(("dp", "sp", "blk"), None),
        P(("dp", "sp", "blk"), None),
        P(("dp", "sp", "blk"), None),
        P(("dp", "sp", "blk"), None),
        P(("dp", "sp", "blk"), None),
        P(None, ("dp", "sp", "blk")),
        P(None, ("dp", "sp", "blk")),
        P(("dp", "sp", "blk")),
    )
    return jax.shard_map(
        on_device, mesh=mesh, in_specs=in_specs, out_specs=out_specs, check_vma=False
    )
```

profile of v0, /device:TPU:0, one launch (start us, length us, event | category | flops | bytes accessed | tf_op | source)
XLA Modules:
  0.0 1970.5 jit_solution(8163006601729356469)
XLA Ops:
  8.0 69.8 %all-gather = bf16[32,32,2]{1,2,0:T(2,128)(2,1)S(1)} all-gather(bf16[1,32,2]{1,2,0:T(2,128)(2,1)} %bitcast.227), channel_id=1, replica_groups=mesh['dp'=4,'sp'=4,'blk'=2] {'dp','sp','blk'}, dimensions={0}, use_global_device_ids=true | all-gather | bytes 4224 | tf_op jit(solution)/shard_map/all_gather | solution.py:36
  77.8 63.9 %all-gather.1 = bf16[32,32,6]{1,2,0:T(8,128)(2,1)S(1)} all-gather(bf16[1,32,6]{1,2,0:T(8,128)(2,1)} %bitcast.226), channel_id=1, replica_groups=mesh['dp'=4,'sp'=4,'blk'=2] {'dp','sp','blk'}, dimensions={0}, use_global_device_ids=true | all-gather | bytes 12672 | tf_op jit(solution)/shard_map/all_gather | solution.py:37
  150.7 14.4 all_to_all.146
  166.3 15.3 all_to_all.147
  188.8 11.9 all-to-all-done
  211.6 53.9 %while.30 = (s32[]{:T(128)}, bf16[2,512,4,64]{1,3,2,0:T(8,128)(2,1)S(1)}, f32[2,4,512,1]{2,1,3,0:T(4,128)S(1)}, f32[2,4,512,1]{2,1,3,0:T(4,128)S(1)}, s32[2]{0:T...) while((s32[]{:T(128)}, ...), condition=%wide.region_5.6_spmd.clone, body=%wide.region_2.5_spmd.clone.sunk | while | flops 1154680832 | bytes 90809072 | solution.py:98
  271.8 73.8 %all-gather.2 = bf16[32,1,128]{2,1,0:T(2,128)(2,1)S(1)} all-gather(bf16[1,1,128]{2,1,0:T(2,128)(2,1)S(1)} %bitcast.228), channel_id=1, replica_groups=mesh['dp'=4,'sp'=4,'blk'=2] {'dp','sp','blk'}, dimensions={0}, use_global_device_ids=true | all-gather | bytes 8448 | tf_op jit(solution)/shard_map/all_gather | solution.py:38
  357.1 71.0 %all-gather.18.cloned.1.call-done = bf16[1024,4096]{1,0:T(8,128)(2,1)} async-done(((bf16[32,4096]{1,0:T(8,128)(2,1)}), bf16[1024,4096]{1,0:T(8,128)(2,1)}) %all-gather.18.cloned.1.call-update) | async-done | bytes 8388624 | tf_op jit(solution)/shard_map/all_gather | solution.py:34
  428.1 12.0 convert_reduce_fusion
  450.7 15.1 all-to-all-done.4
  467.3 114.0 %while.31 = (s32[]{:T(128)}, f32[2048,4,64]{0,2,1:T(8,128)}, f32[2048,4,64]{0,2,1:T(8,128)}, bf16[2,512,4,64]{1,3,2,0:T(8,128)(2,1)}, s32[2]{0:T(128)S(1)}, /*in...) while((s32[]{:T(128)}, f32[2048,4,64]{0,2,1:T(8,128)}, ...), condition=%wide.region_12.13_spmd.clone, body=%wide.region_10.12_spmd.clone.sunk | while | flops 2742882304 | bytes 216367376 | solution.py:175
  481.0 15.2 multiply_reduce_fusion.5
  496.2 11.5 multiply_convert_fusion.5
  536.6 15.2 multiply_reduce_fusion.5
  587.5 24.0 %reduce-scatter.13.cloned.1.call-done = f32[1024,256]{0,1:T(8,128)} async-done(((f32[2048,256]{0,1:T(8,128)}), f32[1024,256]{0,1:T(8,128)}) %reduce-scatter.13.cloned.1.call-update) | async-done | bytes 1048592 | tf_op jit(solution)/shard_map/reduce_scatter | solution.py:179
  618.5 27.3 %reduce-scatter.15.cloned.1.call-done = f32[1024,256]{0,1:T(8,128)} async-done(((f32[2048,256]{0,1:T(8,128)}), f32[1024,256]{0,1:T(8,128)}) %reduce-scatter.15.cloned.1.call-update) | async-done | bytes 1048592 | tf_op jit(solution)/shard_map/reduce_scatter | solution.py:185
  653.1 14.0 all-to-all-done.7
  710.0 37.0 %all-reduce = f32[4096]{0:T(1024)S(1)} all-reduce(f32[4096]{0:T(1024)S(1)} %copy-done.37), channel_id=10, replica_groups=mesh['dp'=4,'sp'=4,'blk'=2] {'dp','sp','blk'}, use_global_device_ids=true, to_apply=%region_32.33.clone | all-reduce | flops 4096 | bytes 32768
  755.8 52.2 %reduce-scatter.25.cloned.1.call-done = f32[32,2]{1,0:T(8,128)} async-done(((f32[1024,2]{1,0:T(8,128)}), f32[32,2]{1,0:T(8,128)}) %reduce-scatter.25.cloned.1.call-update) | async-done | bytes 272
  809.3 131.4 %reduce-scatter.27.cloned.1.call-done = f32[32,6]{1,0:T(8,128)} async-done(((f32[1024,6]{1,0:T(8,128)}), f32[32,6]{1,0:T(8,128)}) %reduce-scatter.27.cloned.1.call-update) | async-done | bytes 784
  942.2 141.9 %reduce-scatter.19.cloned.1.call-done = f32[32,1024]{1,0:T(8,128)} async-done(((f32[1024,1024]{1,0:T(8,128)}), f32[32,1024]{1,0:T(8,128)}) %reduce-scatter.19.cloned.1.call-update) | async-done | bytes 131088 | tf_op jit(solution)/shard_map/reduce_scatter | solution.py:228
  1084.1 159.3 %reduce-scatter.17.cloned.1.call-done = f32[32,3072]{1,0:T(8,128)} async-done(((f32[1024,3072]{1,0:T(8,128)}), f32[32,3072]{1,0:T(8,128)}) %reduce-scatter.17.cloned.1.call-update) | async-done | bytes 393232 | tf_op jit(solution)/shard_map/reduce_scatter | solution.py:227
  1243.5 360.1 %reduce-scatter.23.cloned.1.call-done = f32[128,1024]{1,0:T(8,128)} async-done(((f32[4096,1024]{1,0:T(8,128)}), f32[128,1024]{1,0:T(8,128)}) %reduce-scatter.23.cloned.1.call-update) | async-done | bytes 524304 | tf_op jit(solution)/shard_map/reduce_scatter | solution.py:230
  1603.6 360.2 %reduce-scatter.21.cloned.1.call-done = f32[32,4096]{1,0:T(8,128)} async-done(((f32[1024,4096]{1,0:T(8,128)}), f32[32,4096]{1,0:T(8,128)}) %reduce-scatter.21.cloned.1.call-update) | async-done | bytes 524304 | tf_op jit(solution)/shard_map/reduce_scatter | solution.py:229
  (258 shorter events, 249.6 us)
Async XLA Ops:
  7.2 138.5 %all-gather.10.cloned.1.call-start = ((), (), s32[]{:S(2)}) async-start(), calls=%async_computation.16 | async-start | bytes 6488064 | tf_op jit(solution)/shard_map/all_gather | solution.py:32
  7.9 194.3 %all-gather.12.cloned.1.call-start = ((), (), s32[]{:S(2)}) async-start(), calls=%async_computation.17 | async-start | bytes 1572864 | tf_op jit(solution)/shard_map/all_gather | solution.py:75
  165.1 44.2 %all-gather.14.cloned.1.call-start = ((), (), s32[]{:S(2)}) async-start(), calls=%async_computation.18 | async-start | bytes 1572864 | tf_op jit(solution)/shard_map/all_gather | solution.py:76
  181.6 164.0 %all-gather.16.cloned.1.call-start = ((), (), s32[]{:S(2)}) async-start(), calls=%async_computation.19 | async-start | bytes 2162688 | tf_op jit(solution)/shard_map/all_gather | solution.py:33
  182.2 167.2 %all-gather.20.cloned.1.call-start = ((), (), s32[]{:S(2)}) async-start(), calls=%async_computation.21 | async-start | bytes 8650752 | tf_op jit(solution)/shard_map/all_gather | solution.py:35
  184.6 16.1 all-to-all-start
  188.1 240.0 %all-gather.18.cloned.1.call-start = ((), (), s32[]{:S(2)}) async-start(), calls=%async_computation.20 | async-start | bytes 8650752 | tf_op jit(solution)/shard_map/all_gather | solution.py:34
  266.1 83.3 %copy-start.10 = (bf16[256,1024]{1,0:T(8,128)(2,1)S(1)}, bf16[256,1024]{1,0:T(8,128)(2,1)}, u32[]{:S(2)}) copy-start(bf16[256,1024]{1,0:T(8,128)(2,1)} %param.23) | copy-start | bytes 1572868
  267.2 78.4 %all-to-all-start.3 = ((bf16[4,256,256]{1,2,0:T(8,128)(2,1)}), bf16[4,256,256]{1,2,0:T(8,128)(2,1)S(1)}, u32[]{:S(2)}, u32[]{:S(2)}) async-start(bf16[4,256,256]{1,2,0:T(8,128)(2,1)} %copy.116), calls=%async_computation.3 | async-start | bytes 1048576 | tf_op jit(solution)/shard_map/all_to_all | solution.py:100
  348.3 95.1 %copy-start.4 = (f32[256,1024]{1,0:T(8,128)}, f32[256,1024]{1,0:T(8,128)S(1)}, u32[]{:S(2)}) copy-start(f32[256,1024]{1,0:T(8,128)S(1)} %get-tuple-element.340) | copy-start | bytes 3145732
  348.3 95.0 %copy-start.30 = (f32[256]{0:T(256)}, f32[256]{0:T(256)S(1)}, u32[]{:S(2)}) copy-start(f32[256]{0:T(256)S(1)} %broadcast_multiply_fusion) | copy-start | bytes 3076
  348.6 94.8 %copy-start.34 = (f32[256]{0:T(256)}, f32[256]{0:T(256)S(1)}, u32[]{:S(2)}) copy-start(f32[256]{0:T(256)S(1)} %fusion.110) | copy-start | bytes 3076
  447.2 18.6 all-to-all-start.4
  450.6 160.9 %reduce-scatter.13.cloned.1.call-start = ((), (), s32[]{:S(2)}) async-start(), calls=%async_computation.22 | async-start | bytes 3145728 | tf_op jit(solution)/shard_map/reduce_scatter | solution.py:179
  581.4 64.3 %reduce-scatter.15.cloned.1.call-start = ((), (), s32[]{:S(2)}) async-start(), calls=%async_computation.23 | async-start | bytes 3145728 | tf_op jit(solution)/shard_map/reduce_scatter | solution.py:185
  584.0 29.8 %all-to-all-start.5 = ((bf16[4,256,256]{1,2,0:T(8,128)(2,1)}), bf16[4,256,256]{1,2,0:T(8,128)(2,1)S(1)}, u32[]{:S(2)}, u32[]{:S(2)}) async-start(bf16[4,256,256]{1,2,0:T(8,128)(2,1)} %copy.120), calls=%async_computation.5 | async-start | bytes 1048576 | tf_op jit(solution)/shard_map/all_to_all | solution.py:194
  613.9 34.1 %all-to-all-start.6 = ((bf16[4,256,256]{2,1,0:T(8,128)(2,1)}), bf16[4,256,256]{2,1,0:T(8,128)(2,1)S(1)}, u32[]{:S(2)}, u32[]{:S(2)}) async-start(bf16[4,256,256]{2,1,0:T(8,128)(2,1)} %bitcast.29), calls=%async_computation.7 | async-start | bytes 1048576 | tf_op jit(solution)/shard_map/all_to_all | solution.py:195
  648.0 19.1 all-to-all-start.7
  652.6 155.3 %reduce-scatter.25.cloned.1.call-start = ((), (), s32[]{:S(2)}) async-start(), calls=%async_computation.28 | async-start | bytes 540672
  675.6 265.1 %reduce-scatter.27.cloned.1.call-start = ((), (), s32[]{:S(2)}) async-start(), calls=%async_computation.29 | async-start | bytes 540672
  676.9 407.2 %reduce-scatter.19.cloned.1.call-start = ((), (), s32[]{:S(2)}) async-start(), calls=%async_computation.25 | async-start | bytes 4325376 | tf_op jit(solution)/shard_map/reduce_scatter | solution.py:228
  680.7 562.7 %reduce-scatter.17.cloned.1.call-start = ((), (), s32[]{:S(2)}) async-start(), calls=%async_computation.24 | async-start | bytes 12976128 | tf_op jit(solution)/shard_map/reduce_scatter | solution.py:227
  688.3 915.3 %reduce-scatter.23.cloned.1.call-start = ((), (), s32[]{:S(2)}) async-start(), calls=%async_computation.27 | async-start | bytes 17301504 | tf_op jit(solution)/shard_map/reduce_scatter | solution.py:230
  699.2 1264.6 %reduce-scatter.21.cloned.1.call-start = ((), (), s32[]{:S(2)}) async-start(), calls=%async_computation.26 | async-start | bytes 17301504 | tf_op jit(solution)/shard_map/reduce_scatter | solution.py:229
  (46 other events, 715.9 us)
Sparse Core Ops, SparseCore 0:
  10.9 72.2 all-gather.9
  165.2 21.1 all-gather.11
  188.0 21.2 all-gather.13
  212.2 56.5 all-gather.15
  271.6 77.7 all-gather.19
  352.2 75.8 all-gather.17
  581.5 29.9 reduce-scatter.12
  613.9 31.8 reduce-scatter.14
  675.8 132.1 reduce-scatter.24
  810.2 130.5 reduce-scatter.26
  943.6 140.4 reduce-scatter.18
  1090.6 152.8 reduce-scatter.16
  1246.4 357.1 reduce-scatter.22
  1606.4 357.3 reduce-scatter.20
where the time goes:
time: 1980 us; the launch traced here: 1970 us
  waiting for transfers between devices  1380 us (70%)
  blocking collectives  274 us (14%)
  matrix products  182 us (9%)
  other arithmetic  49.5 us (2%)
  local copies, waits for them, and re-layouts  38.3 us (2%)
  starting transfers between devices  24.9 us (1%)
    reduce_scatter x1, waiting for transfers between devices, on_device(): lax.psum_scatter(grad_w_in, ('dp', 'sp', 'blk'), scatter_dimension=0, til...  360 us
    reduce_scatter x1, waiting for transfers between devices, on_device(): lax.psum_scatter(grad_w_out, ('dp', 'sp', 'blk'), scatter_dimension=0, ti...  360 us
    unnamed x16, waiting for transfers between devices  187 us
    reduce_scatter x1, waiting for transfers between devices, on_device(): lax.psum_scatter(grad_w_qkv, ('dp', 'sp', 'blk'), scatter_dimension=0, ti...  159 us
    reduce_scatter x1, waiting for transfers between devices, on_device(): lax.psum_scatter(grad_w_dense, ('dp', 'sp', 'blk'), scatter_dimension=0,...  142 us
    all_gather x1, blocking collectives, on_device(): lax.all_gather(in_bias, ('dp', 'sp', 'blk'), axis=0, tiled=True)  73.8 us
    all_gather x1, waiting for transfers between devices, on_device(): lax.all_gather(w_in, ('dp', 'sp', 'blk'), axis=0, tiled=True)  71 us
    all_gather x1, blocking collectives, on_device(): lax.all_gather(norm_gains, ('dp', 'sp', 'blk'), axis=1, tiled=True)  69.8 us
  transfers between devices with their start and end apart: 20, of which 14 were waited for; matrix products, arithmetic and copies ran while one was open for 6% of the time, Pallas kernels for 0%

commit v1 on v0

v1 whole, which is shorter than its diff:
```python
import functools
import math

import jax
import jax.numpy as jnp
from jax import lax
from jax.experimental import pallas as pl
from jax.experimental.pallas import tpu as pltpu
from jax.sharding import PartitionSpec as P

H = 16
ALL = ("dp", "sp", "blk")
SEQ_AXES = ("sp", "blk")
F32 = jnp.float32
BF16 = jnp.bfloat16
LOG2E = 1.4426950408889634


def norm_rows(features, gain_row, offset):
    row_mean = jnp.mean(features, axis=-1, keepdims=True)
    centered = features - row_mean
    variance = jnp.mean(centered * centered, axis=-1, keepdims=True)
    return centered * lax.rsqrt(variance + 1e-05) * gain_row + offset


def dot_nn(a, b):
    return lax.dot_general(a, b, (((1,), (0,)), ((), ())), preferred_element_type=F32)


def dot_nt(a, b):
    return lax.dot_general(a, b, (((1,), (1,)), ((), ())), preferred_element_type=F32)


def dot_tn(a, b):
    return lax.dot_general(a, b, (((0,), (0,)), ((), ())), preferred_element_type=F32)


def exchange(value, bit):
    count = lax.axis_size("dp")
    return lax.ppermute(value, "dp", [(i, i ^ bit) for i in range(count)])


def gather_dp(value):
    pieces = {0: value}
    bit = lax.axis_size("dp") // 2
    while bit:
        for place in list(pieces):
            pieces[place | bit] = exchange(pieces[place], bit)
        bit //= 2
    return [pieces[place] for place in range(len(pieces))]


def swap_dp(pieces):
    return [pieces[0]] + [exchange(pieces[place], place) for place in range(1, len(pieces))]


def sum_dp(pieces):
    pieces = dict(enumerate(pieces))
    count, bit = len(pieces), 1
    while bit < count:
        for place in range(0, count, 2 * bit):
            arrived = exchange(pieces[place + bit].astype(BF16), bit)
            pieces[place] = pieces[place].astype(F32) + arrived.astype(F32)
        bit *= 2
    return pieces[0]


def one_head(rows, head, head_dim):
    lane = lax.broadcasted_iota(jnp.int32, rows.shape, 1)
    inside = (lane >= head * head_dim) & (lane < (head + 1) * head_dim)
    return jnp.where(inside, rows, jnp.zeros_like(rows))


def score_tile(keys, query_head, scale, slope, key_first, query_first, masked):
    scores = dot_nt(keys, query_head) * scale
    key_row = lax.broadcasted_iota(jnp.int32, (keys.shape[0], 1), 0)
    ahead = key_first - query_first
    scores = scores + (key_row.astype(F32) * slope + ahead.astype(F32) * slope)
    if masked:
        key_place = lax.broadcasted_iota(jnp.int32, scores.shape, 0) + ahead
        query_place = lax.broadcasted_iota(jnp.int32, scores.shape, 1)
        scores = jnp.where(key_place <= query_place, scores, -1e30)
    return scores


def forward_kernel(heads, head_dim, block, slopes_ref, qkv_ref, ctx_ref, ctx_t_ref, lse_ref, value_t_ref):
    width = heads * head_dim
    step = pl.program_id(0)
    scale = LOG2E / math.sqrt(head_dim)

    @pl.when(step == 0)
    def _():
        value_t_ref[...] = qkv_ref[:, 2 * width :].astype(F32).T.astype(BF16)

    first = pl.multiple_of(step * block, block)
    rows = qkv_ref[pl.ds(first, block), 0:width]
    queries = [one_head(rows, head, head_dim) for head in range(heads)]
    slopes = [slopes_ref[head] * LOG2E for head in range(heads)]

    def tile(index, running, masked):
        key_first = pl.multiple_of(index * block, block)
        keys = qkv_ref[pl.ds(key_first, block), width : 2 * width]
        values = value_t_ref[:, pl.ds(key_first, block)]
        after = []
        for head in range(heads):
            top, total, context = running[head]
            scores = score_tile(keys, queries[head], scale, slopes[head], key_first, first, masked)
            new_top = jnp.maximum(top, jnp.max(scores, axis=0, keepdims=True))
            exponent = jnp.exp2(scores - new_top)
            shrink = jnp.exp2(top - new_top)
            total = total * shrink + jnp.sum(exponent, axis=0, keepdims=True)
            part = dot_nn(values[head * head_dim : (head + 1) * head_dim], exponent.astype(BF16))
            after.append((new_top, total, context * shrink + part))
        return tuple(after)

    start = tuple(
        (jnp.full((1, block), -1e30, F32), jnp.zeros((1, block), F32), jnp.zeros((head_dim, block), F32))
        for _ in range(heads)
    )
    running = lax.fori_loop(0, step, lambda index, held: tile(index, held, False), start)
    running = tile(step, running, True)
    contexts = []
    for head in range(heads):
        top, total, context = running[head]
        context = context * (1.0 / total)
        ctx_t_ref[head * head_dim : (head + 1) * head_dim, pl.ds(first, block)] = context
        lse_ref[head : head + 1, pl.ds(first, block)] = top + jnp.log2(total)
        contexts.append(context)
    ctx_ref[pl.ds(first, block), :] = jnp.concatenate(contexts, axis=0).T.astype(BF16)


def backward_kernel(
    heads, head_dim, block, slopes_ref, qkv_ref, grad_ref, ctx_t_ref, lse_ref, out_ref, key_t_ref, grad_key_ref, grad_value_ref
):
    width = heads * head_dim
    step = pl.program_id(0)
    scale = LOG2E / math.sqrt(head_dim)
    unit = 1.0 / math.sqrt(head_dim)

    @pl.when(step == 0)
    def _():
        key_t_ref[...] = qkv_ref[:, width : 2 * width].astype(F32).T.astype(BF16)
        grad_key_ref[...] = jnp.zeros_like(grad_key_ref)
        grad_value_ref[...] = jnp.zeros_like(grad_value_ref)

    first = pl.multiple_of(step * block, block)
    rows = qkv_ref[pl.ds(first, block), 0:width]
    grad_rows = grad_ref[pl.ds(first, block), :]
    queries = [one_head(rows, head, head_dim) for head in range(heads)]
    grads = [one_head(grad_rows, head, head_dim) for head in range(heads)]
    product = grad_rows.astype(F32).T * ctx_t_ref[:, pl.ds(first, block)]
    deltas = [
        jnp.sum(product[head * head_dim : (head + 1) * head_dim], axis=0, keepdims=True)
        for head in range(heads)
    ]
    lses = [lse_ref[head : head + 1, pl.ds(first, block)] for head in range(heads)]
    slopes = [slopes_ref[head] * LOG2E for head in range(heads)]

    def tile(index, running, masked):
        key_first = pl.multiple_of(index * block, block)
        keys = qkv_ref[pl.ds(key_first, block), width : 2 * width]
        values = qkv_ref[pl.ds(key_first, block), 2 * width :]
        keys_t = key_t_ref[:, pl.ds(key_first, block)]
        grad_key = grad_key_ref[pl.ds(key_first, block), :]
        grad_value = grad_value_ref[pl.ds(key_first, block), :]
        after = []
        for head in range(heads):
            scores = score_tile(keys, queries[head], scale, slopes[head], key_first, first, masked)
            weights = jnp.exp2(scores - lses[head])
            grad_weights = dot_nt(values, grads[head])
            grad_scores = (weights * (grad_weights - deltas[head])).astype(BF16)
            grad_value = grad_value + dot_nn(weights.astype(BF16), grads[head])
            grad_key = grad_key + dot_nn(grad_scores, queries[head])
            head_rows = keys_t[head * head_dim : (head + 1) * head_dim]
            after.append(running[head] + dot_nn(head_rows, grad_scores))
        grad_key_ref[pl.ds(key_first, block), :] = grad_key
        grad_value_ref[pl.ds(key_first, block), :] = grad_value
        return tuple(after)

    start = tuple(jnp.zeros((head_dim, block), F32) for _ in range(heads))
    running = lax.fori_loop(0, step, lambda index, held: tile(index, held, False), start)
    running = tile(step, running, True)
    grad_query = jnp.concatenate(running, axis=0) * unit
    out_ref[pl.ds(first, block), 0:width] = grad_query.T.astype(BF16)

    @pl.when(step == pl.num_programs(0) - 1)
    def _():
        out_ref[:, width : 2 * width] = (grad_key_ref[...] * unit).astype(BF16)
        out_ref[:, 2 * width :] = grad_value_ref[...].astype(BF16)


def whole(count):
    return [pl.BlockSpec(memory_space=pltpu.VMEM)] * count


def attend_forward(slopes, qkv, heads, block):
    length, width = qkv.shape[0], qkv.shape[1] // 3
    head_dim = width // heads
    pairs = heads * length * length
    return pl.pallas_call(
        functools.partial(forward_kernel, heads, head_dim, block),
        grid=(length // block,),
        out_shape=(
            jax.ShapeDtypeStruct((length, width), BF16),
            jax.ShapeDtypeStruct((width, length), F32),
            jax.ShapeDtypeStruct((heads, length), F32),
        ),
        in_specs=[pl.BlockSpec(memory_space=pltpu.SMEM)] + whole(1),
        out_specs=tuple(whole(3)),
        scratch_shapes=[pltpu.VMEM((width, length), BF16)],
        compiler_params=pltpu.CompilerParams(vmem_limit_bytes=40 << 20),
        cost_estimate=pl.CostEstimate(
            flops=4 * pairs * head_dim, bytes_accessed=6 * length * width, transcendentals=pairs
        ),
        name="attend_forward",
    )(slopes, qkv)


def attend_backward(slopes, qkv, grad, ctx_t, lse, heads, block):
    length, width = qkv.shape[0], qkv.shape[1] // 3
    head_dim = width // heads
    pairs = heads * length * length
    return pl.pallas_call(
        functools.partial(backward_kernel, heads, head_dim, block),
        grid=(length // block,),
        out_shape=jax.ShapeDtypeStruct((length, 3 * width), BF16),
        in_specs=[pl.BlockSpec(memory_space=pltpu.SMEM)] + whole(4),
        out_specs=whole(1)[0],
        scratch_shapes=[
            pltpu.VMEM((width, length), BF16),
            pltpu.VMEM((length, width), F32),
            pltpu.VMEM((length, width), F32),
        ],
        compiler_params=pltpu.CompilerParams(vmem_limit_bytes=40 << 20),
        cost_estimate=pl.CostEstimate(
            flops=10 * pairs * head_dim, bytes_accessed=12 * length * width, transcendentals=pairs
        ),
        name="attend_backward",
    )(slopes, qkv, grad, ctx_t, lse)


def split_scores(query_rows, row_places, key_rows, key_places, slopes, score_scale):
    scores = jnp.einsum("qhe,khe->hqk", query_rows, key_rows, preferred_element_type=F32) * score_scale
    distance = (row_places[:, None] - key_places[None, :]).astype(F32)
    scores = scores - slopes[:, None, None] * distance[None]
    return jnp.where((distance >= 0)[None], scores, -1e30)


def split_setup(qkv, heads, rows_each):
    local, width = qkv.shape[0], qkv.shape[1] // 3
    shape = (heads, width // heads)
    parts, mine = lax.axis_size("blk"), lax.axis_index("blk")
    held = lax.all_gather(qkv[:, width:], "blk", axis=0, tiled=False)
    held = held.reshape(parts, local // rows_each, rows_each, 2 * width).transpose(1, 0, 2, 3)
    held = held.reshape(parts * local, 2 * width)
    index = jnp.arange(local, dtype=jnp.int32)
    places = (index // rows_each * parts + mine) * rows_each + index % rows_each
    block = min(512, local)
    return (
        qkv[:, :width].reshape((local // block, block) + shape),
        held[:, :width].reshape((parts * local,) + shape),
        held[:, width:].reshape((parts * local,) + shape),
        places.reshape(local // block, block),
        jnp.arange(parts * local, dtype=jnp.int32),
        1.0 / math.sqrt(width // heads),
    )


def split_forward(slopes, qkv, heads, rows_each):
    queries, keys, values, places, key_places, scale = split_setup(qkv, heads, rows_each)

    def one_block(item):
        chosen, block_places = item
        scores = split_scores(chosen, block_places, keys, key_places, slopes, scale)
        top = jnp.max(scores, axis=-1, keepdims=True)
        exponent = jnp.exp(scores - top)
        total = jnp.sum(exponent, axis=-1, keepdims=True)
        weights = (exponent / total).astype(BF16)
        context = jnp.einsum("hqk,khe->qhe", weights, values, preferred_element_type=F32)
        return context.astype(BF16), top, total

    contexts, tops, totals = lax.map(one_block, (queries, places))
    return contexts.reshape(qkv.shape[0], -1), tops, totals


def split_backward(slopes, qkv, grad, tops, totals, heads, rows_each):
    queries, keys, values, places, key_places, scale = split_setup(qkv, heads, rows_each)
    grads = grad.reshape(queries.shape)

    def one_block(running, item):
        grad_keys, grad_values = running
        chosen, block_places, grad_rows, top, total = item
        scores = split_scores(chosen, block_places, keys, key_places, slopes, scale)
        weights = jnp.exp(scores - top) / total
        grad_values = grad_values + jnp.einsum(
            "hqk,qhe->khe", weights.astype(BF16), grad_rows, preferred_element_type=F32
        )
        grad_probs = jnp.einsum("qhe,khe->hqk", grad_rows, values, preferred_element_type=F32)
        grad_scores = (
            weights * (grad_probs - jnp.sum(weights * grad_probs, axis=-1, keepdims=True))
        ).astype(BF16)
        grad_query = jnp.einsum("hqk,khe->qhe", grad_scores, keys, preferred_element_type=F32) * scale
        grad_keys = (
            grad_keys
            + jnp.einsum("hqk,qhe->khe", grad_scores, chosen, preferred_element_type=F32) * scale
        )
        return (grad_keys, grad_values), grad_query.astype(BF16)

    empty = jnp.zeros(keys.shape, F32)
    (grad_keys, grad_values), grad_queries = lax.scan(
        one_block, (empty, empty), (queries, places, grads, tops, totals)
    )
    local, width = grad.shape
    both = jnp.concatenate([grad_keys.reshape(-1, width), grad_values.reshape(-1, width)], axis=1)
    parts = lax.axis_size("blk")
    both = both.reshape(local // rows_each, parts, rows_each, 2 * width).transpose(1, 0, 2, 3)
    own = lax.psum_scatter(both, "blk", scatter_dimension=0, tiled=False)
    own = own.reshape(local, 2 * width).astype(BF16)
    return jnp.concatenate([grad_queries.reshape(local, width), own], axis=1)


def on_device(
    inputs, w_qkv, w_dense, w_in, w_out, norm_gains, biases, in_bias, alibi_slopes, upstream
):
    dp_count, sp_count, blk_count = (lax.axis_size(axis) for axis in ALL)
    dp_place = lax.axis_index("dp")
    ring = sp_count * blk_count
    devices = dp_count * ring
    rows, width = inputs.shape
    slice_rows = w_qkv.shape[0]
    inner = in_bias.shape[0] * devices // dp_count
    head_dim = width // H
    dp_heads = H // dp_count
    dp_width = dp_heads * head_dim

    whole_pairs = ring % dp_count == 0 and dp_heads % max(1, ring // dp_count) == 0
    pair_axes = SEQ_AXES if whole_pairs else ("sp",)
    owners = ring if whole_pairs else sp_count
    groups = owners // dp_count
    pair_heads = dp_heads // groups
    pair_width = pair_heads * head_dim

    def spread(pieces):
        columns = pieces.shape[-1]
        sent = pieces.transpose(0, 2, 1, 3).reshape(owners * rows, columns)
        return lax.all_to_all(sent, pair_axes, split_axis=0, concat_axis=0, tiled=True)

    def collect(held):
        columns = held.shape[-1]
        got = lax.all_to_all(held, pair_axes, split_axis=0, concat_axis=0, tiled=True)
        return got.reshape(dp_count, groups, rows, columns).transpose(0, 2, 1, 3)

    tokens = jnp.concatenate(gather_dp(inputs), axis=0)
    grad_tokens = jnp.concatenate(gather_dp(upstream), axis=0)
    small = jnp.concatenate([norm_gains.reshape(-1), biases.reshape(-1), in_bias])
    small = lax.all_to_all(
        jnp.broadcast_to(small[None], (devices, small.shape[0])), ALL, split_axis=0, concat_axis=0, tiled=True
    )
    gain_size, bias_size = norm_gains.size, biases.size
    gains_row = small[:, :gain_size].reshape(devices, 2, -1).transpose(1, 0, 2).reshape(2, width).astype(F32)
    offsets = small[:, gain_size : gain_size + bias_size].reshape(devices, 6, -1)
    offsets = offsets.transpose(1, 0, 2).reshape(6, width).astype(F32)
    in_offset = lax.dynamic_slice_in_dim(
        small[:, gain_size + bias_size :].reshape(-1), dp_place * inner, inner
    ).astype(F32)

    def columns_weight(pieces):
        columns = pieces.shape[-1]
        swapped = lax.all_to_all(pieces, "dp", split_axis=0, concat_axis=0, tiled=True)
        gathered = lax.all_gather(swapped, SEQ_AXES, axis=0, tiled=False)
        return gathered.transpose(1, 0, 2, 3).reshape(width, columns)

    def columns_gradient(grad):
        columns = grad.shape[-1]
        sent = grad.astype(BF16).reshape(dp_count, ring, slice_rows, columns).transpose(1, 0, 2, 3)
        summed = lax.psum_scatter(sent, SEQ_AXES, scatter_dimension=0, tiled=False)
        return lax.all_to_all(summed, "dp", split_axis=0, concat_axis=0, tiled=True)

    qkv_split = w_qkv.reshape(slice_rows, 3, dp_count, groups, pair_width).transpose(2, 0, 3, 1, 4)
    qkv_weight = columns_weight(qkv_split.reshape(dp_count, slice_rows, 3 * dp_width))
    dense_part = lax.all_gather(w_dense, SEQ_AXES, axis=0, tiled=True)
    in_weight = columns_weight(w_in.reshape(slice_rows, dp_count, inner).transpose(1, 0, 2))
    out_weight = lax.all_gather(w_out, SEQ_AXES, axis=0, tiled=True)
    dense_weight = jnp.concatenate(gather_dp(dense_part), axis=0)

    rows_in = inputs.astype(F32)
    normed_one = norm_rows(tokens.astype(F32), gains_row[0], offsets[0]).astype(BF16)
    own_offset = lax.dynamic_slice_in_dim(offsets, dp_place * dp_width, dp_width, 1)
    own_offset = own_offset.reshape(6, groups, pair_width)
    qkv_offset = jnp.stack([own_offset[1], jnp.zeros_like(own_offset[1]), own_offset[2]], axis=1).reshape(-1)
    projected = (dot_nn(normed_one, qkv_weight) + qkv_offset).astype(BF16)
    qkv = spread(projected.reshape(dp_count, rows, groups, 3 * pair_width))
    group = lax.axis_index(pair_axes) % groups
    slopes = lax.dynamic_slice_in_dim(alibi_slopes, dp_place * dp_heads + group * pair_heads, pair_heads)
    if whole_pairs:
        block = min(512, ring * rows)
        context, *kept = attend_forward(slopes, qkv, pair_heads, block)
    else:
        context, *kept = split_forward(slopes, qkv, pair_heads, rows)
    context_tok = collect(context).reshape(dp_count, rows, dp_width)
    context_tok = jnp.concatenate(swap_dp([context_tok[k] for k in range(dp_count)]), axis=1)
    middle = rows_in + (dot_nn(context_tok, dense_weight) + offsets[3])
    normed_two = norm_rows(middle, gains_row[1], offsets[4]).astype(BF16)
    normed_two_all = jnp.concatenate(gather_dp(normed_two), axis=0)
    hidden_pre = dot_nn(normed_two_all, in_weight) + in_offset
    hidden, gelu_pull = jax.vjp(jax.nn.gelu, hidden_pre)
    hidden = hidden.astype(BF16)

    grad_top = upstream.astype(F32)
    grad_pre = gelu_pull(dot_nt(grad_tokens, out_weight))[0].astype(BF16)
    grad_normed_two = sum_dp(list(dot_nt(grad_pre, in_weight).reshape(dp_count, rows, width)))
    _, second_pull = jax.vjp(norm_rows, middle, gains_row[1], offsets[4])
    grad_mid_part, grad_gain_two, grad_shift_two = second_pull(grad_normed_two)
    grad_middle = grad_top + grad_mid_part
    grad_att = grad_middle.astype(BF16)
    grad_context = dot_nt(grad_att, dense_weight).astype(BF16)
    grad_context = swap_dp([grad_context[:, k * dp_width : (k + 1) * dp_width] for k in range(dp_count)])
    grad_held = spread(jnp.stack(grad_context).reshape(dp_count, rows, groups, pair_width))

    branch = sum_dp(list(dot_nn(hidden, out_weight).reshape(dp_count, rows, width)))
    output = (middle + (branch + offsets[5])).astype(BF16)
    grad_w_out = lax.psum_scatter(
        dot_tn(hidden, grad_tokens).astype(BF16), SEQ_AXES, scatter_dimension=0, tiled=True
    ).astype(F32)
    grad_w_in = columns_gradient(dot_tn(normed_two_all, grad_pre))
    grad_w_in = grad_w_in.transpose(1, 0, 2).reshape(slice_rows, -1).astype(F32)
    grad_dense = sum_dp(list(dot_tn(context_tok, grad_att).reshape(dp_count, dp_width, width)))
    grad_w_dense = lax.psum_scatter(
        grad_dense.astype(BF16), SEQ_AXES, scatter_dimension=0, tiled=True
    ).astype(F32)

    if whole_pairs:
        grad_qkv = attend_backward(slopes, qkv, grad_held, *kept, pair_heads, block)
    else:
        grad_qkv = split_backward(slopes, qkv, grad_held, *kept, pair_heads, rows)
    grad_projected = collect(grad_qkv).reshape(dp_count * rows, 3 * dp_width)
    grad_w_qkv = columns_gradient(dot_tn(normed_one, grad_projected))
    grad_w_qkv = grad_w_qkv.reshape(dp_count, slice_rows, groups, 3, pair_width).transpose(1, 3, 0, 2, 4)
    grad_w_qkv = grad_w_qkv.reshape(slice_rows, 3 * width).astype(F32)
    grad_normed_one = sum_dp(list(dot_nt(grad_projected, qkv_weight).reshape(dp_count, rows, width)))
    _, first_pull = jax.vjp(norm_rows, rows_in, gains_row[0], offsets[0])
    grad_rows_part, grad_gain_one, grad_shift_one = first_pull(grad_normed_one)
    grad_inputs = grad_middle + grad_rows_part

    own_sums = jnp.sum(grad_projected.astype(F32), axis=0).reshape(groups, 3, pair_width)

    def placed(part, size):
        return lax.dynamic_update_slice_in_dim(jnp.zeros(size, F32), part, dp_place * part.shape[0], 0)

    grad_vectors = jnp.stack(
        [
            grad_gain_one,
            grad_gain_two,
            grad_shift_one,
            placed(own_sums[:, 0].reshape(-1), width),
            placed(own_sums[:, 2].reshape(-1), width),
            jnp.sum(grad_att.astype(F32), axis=0),
            grad_shift_two,
            jnp.sum(grad_top, axis=0),
        ]
    )
    grad_in_part = placed(jnp.sum(grad_pre.astype(F32), axis=0), inner * dp_count)
    parts = jnp.concatenate(
        [
            grad_vectors.reshape(8, devices, -1).transpose(1, 0, 2).reshape(devices, -1),
            grad_in_part.reshape(devices, -1),
        ],
        axis=1,
    )
    parts = lax.all_to_all(parts, ALL, split_axis=0, concat_axis=0, tiled=True)
    summed = jnp.sum(parts, axis=0)
    vectors = summed[: gain_size + bias_size].reshape(8, -1)
    return (
        output,
        grad_inputs,
        grad_w_qkv,
        grad_w_dense,
        grad_w_in,
        grad_w_out,
        vectors[:2],
        vectors[2:],
        summed[gain_size + bias_size :],
    )


def solution(mesh):
    rows, columns, vector = P(ALL, None), P(None, ALL), P(ALL)
    in_specs = (rows, rows, rows, rows, rows, columns, columns, vector, P(), rows)
    out_specs = (rows, rows, rows, rows, rows, rows, columns, columns, vector)
    return jax.shard_map(
        on_device, mesh=mesh, in_specs=in_specs, out_specs=out_specs, check_vma=False
    )
```

time: 1980 us -> 705 us (0.36)
  waiting for transfers between devices: 1380 us -> 381 us
  blocking collectives: 274 us -> 80.4 us
  matrix products: 182 us -> 52.3 us
  Pallas kernels: 0 us -> 30.6 us
  local copies, waits for them, and re-layouts: 38.3 us -> 60.3 us
  starting transfers between devices: 24.9 us -> 45.9 us
    reduce_scatter x6 -> x3, waiting for transfers between devices: 1070 us -> 155 us  [the longest x1 69 us: on_device(): lax.psum_scatter(dot_tn(hidden, grad_tokens).astype(BF16), SEQ_AXES, scat...]
    all_gather x3 -> x1, blocking collectives: 207 us -> 41.9 us  [on_device(): dense_part = lax.all_gather(w_dense, SEQ_AXES, axis=0, tiled=True)]
    unnamed x16 -> x8, waiting for transfers between devices: 187 us -> 31.5 us
    dot_general x26 -> x12, matrix products: 182 us -> 52.3 us  [the longest x4 18.7 us: dot_nn(): lax.dot_general(a, b, (((1,), (0,)), ((), ())), preferred_element_type=F32)]
    ppermute x0 -> x30, waiting for transfers between devices: none -> 74.3 us  [exchange(): return lax.ppermute(value, 'dp', [(i, i ^ bit) for i in range(count)])]
    all_to_all x6 -> x7, waiting for transfers between devices: 41 us -> 102 us  [the longest x2 52.2 us: collect(): lax.all_to_all(held, pair_axes, split_axis=0, concat_axis=0, tiled=True)]
    all_gather x6 -> x3, waiting for transfers between devices: 76.7 us -> 18.3 us  [the longest x2 18.3 us: columns_weight(): gathered = lax.all_gather(swapped, SEQ_AXES, axis=0, tiled=False)]
    unnamed x1 -> x0, blocking collectives: 37 us -> none
  transfers between devices with their start and end apart: 20 -> 44, of which waited for: 14 -> 19; matrix products, arithmetic and copies ran while one was open for 6% -> 16% of each run, Pallas kernels for 0% -> 2%
where the time goes in v1:
time: 705 us; the launch traced here: 696 us
  waiting for transfers between devices  381 us (54%)
  blocking collectives  80.4 us (11%)
  local copies, waits for them, and re-layouts  60.3 us (9%)
  matrix products  52.3 us (7%)
  starting transfers between devices  45.9 us (7%)
  Pallas kernels  30.6 us (4%)
  other arithmetic  30.3 us (4%)
  between operations  15.4 us (2%)
    ppermute x30, waiting for transfers between devices, exchange(): return lax.ppermute(value, 'dp', [(i, i ^ bit) for i in range(count)])  74.3 us
    reduce_scatter x1, waiting for transfers between devices, on_device(): lax.psum_scatter(dot_tn(hidden, grad_tokens).astype(BF16), SEQ_AXES, scat...  69 us
    reduce_scatter x1, waiting for transfers between devices, on_device(): lax.psum_scatter(grad_dense.astype(BF16), SEQ_AXES, scatter_dimension=0,...  60.2 us
    all_to_all x2, waiting for transfers between devices, collect(): lax.all_to_all(held, pair_axes, split_axis=0, concat_axis=0, tiled=True)  52.2 us
    all_to_all x1, waiting for transfers between devices, spread(): lax.all_to_all(sent, pair_axes, split_axis=0, concat_axis=0, tiled=True)  44.4 us
    all_gather x1, blocking collectives, on_device(): dense_part = lax.all_gather(w_dense, SEQ_AXES, axis=0, tiled=True)  41.9 us
    unnamed x8, waiting for transfers between devices  31.5 us
    reduce_scatter x1, waiting for transfers between devices, columns_gradient(): summed = lax.psum_scatter(sent, SEQ_AXES, scatter_dimension=0, tiled=False)  26.2 us
  transfers between devices with their start and end apart: 44, of which 19 were waited for; matrix products, arithmetic and copies ran while one was open for 16% of the time, Pallas kernels for 2%

profile of v1, /device:TPU:0, one launch (start us, length us, event | category | flops | bytes accessed | tf_op | source)
XLA Modules:
  0.0 696.2 jit_solution(6877791265428945950)
XLA Ops:
  8.6 9.4 %all_to_all.78 = bf16[4,32,768]{2,1,0:T(8,128)(2,1)} all-to-all(bf16[4,32,768]{2,1,0:T(8,128)(2,1)S(1)} %reshape.302), channel_id=1, replica_groups=mesh['dp'=4,'sp'=4,'blk'=2] {'dp'}, dimensions={0} | all-to-all | bytes 393216 | tf_op jit(solution)/shard_map/all_to_all | solution.py:369
  22.8 6.4 all-to-all-start
  44.7 18.3 %all-gather.8.cloned.1.call-done = bf16[32,32,768]{2,1,0:T(8,128)(2,1)} async-done(((bf16[4,32,768]{2,1,0:T(8,128)(2,1)}), bf16[32,32,768]{2,1,0:T(8,128)(2,1)}) %all-gather.8.cloned.1.call-update) | async-done | bytes 1572880 | tf_op jit(solution)/shard_map/all_gather | solution.py:370
  80.3 44.4 %all-to-all-done.2 = bf16[8,256,384]{2,1,0:T(8,128)(2,1)S(1)} async-done(((bf16[8,256,384]{2,1,0:T(8,128)(2,1)}), bf16[8,256,384]{2,1,0:T(8,128)(2,1)S(1)}, u32[]{:S(2)}, u32[]{:S(2)}) %all-to-all-start.2) | async-done | bytes 1572896 | tf_op jit(solution)/shard_map/all_to_all | solution.py:346
  124.7 12.9 %attend_forward.1 = (bf16[2048,128]{1,0:T(8,128)(2,1)}, f32[128,2048]{1,0:T(8,128)S(1)}, f32[2,2048]{1,0:T(2,128)S(1)}) custom-call(f32[2]{0:T(128)S(1)} %dynamic_slice.9.slopes_ref, bf16[2048,384]{1,0:T(8,128)(2,1)S(1)} %bitcast.95), custom_call_target="tpu_custom_call" | custom-call | flops 2147483648 | bytes 1572864 | tf_op jit(solution)/shard_map/attend_forward/pallas_call | solution.py:200
  141.8 41.9 %all_gather.20 = bf16[256,1024]{1,0:T(8,128)(2,1)} all-gather(bf16[32,1024]{1,0:T(8,128)(2,1)S(1)} %copy-done.27), channel_id=1, replica_groups=mesh['dp'=4,'sp'=4,'blk'=2] {'sp','blk'}, dimensions={0}, use_global_device_ids=true | all-gather | bytes 589824 | tf_op jit(solution)/shard_map/all_gather | solution.py:381
  185.7 12.0 %collective-permute-done.7 = bf16[256,1024]{1,0:T(8,128)(2,1)} collective-permute-done((bf16[256,1024]{1,0:T(8,128)(2,1)}, bf16[256,1024]{1,0:T(8,128)(2,1)}, u32[]{:S(2)}, u32[]{:S(2)}) %collective-permute-start.7) | collective-permute-done | bytes 524320 | tf_op jit(solution)/shard_map/ppermute | solution.py:40
  223.0 10.2 %collective-permute-done.10 = bf16[256,1024]{1,0:T(8,128)(2,1)} collective-permute-done((bf16[256,1024]{1,0:T(8,128)(2,1)}, bf16[256,1024]{1,0:T(8,128)(2,1)}, u32[]{:S(2)}, u32[]{:S(2)}) %collective-permute-start.10) | collective-permute-done | bytes 524320 | tf_op jit(solution)/shard_map/ppermute | solution.py:40
  241.0 5.8 fusion.34
  246.8 8.4 %convert_reduce_fusion.1 = (f32[1024]{0:T(1024)S(1)}, bf16[1024,1024]{1,0:T(8,128)(2,1)S(1)}) fusion(f32[1024,1024]{1,0:T(8,128)} %fusion.34, f32[1024]{0:T(1024)S(1)} %dynamic-slice_convert_fusion, bf16[1024,1024]{1,0:T(8,128)(2,1)} %constant_dynamic-update-slice_fusion.4, bf16[1024,1024]{1,0:T(8,128)(2,1)} %all-gather.6.cloned.1.call-done), kind=kOutput, calls=%fused_computation.17 | convolution fusion | flops 2171599872 | bytes 10493952 | tf_op jit(solution)/shard_map/dot_general | solution.py:31
  270.7 11.0 %collective-permute-done.20 = bf16[256,1024]{1,0:T(8,128)(2,1)} collective-permute-done((bf16[256,1024]{1,0:T(8,128)(2,1)}, bf16[256,1024]{1,0:T(8,128)(2,1)}, u32[]{:S(2)}, u32[]{:S(2)}) %collective-permute-start.20) | collective-permute-done | bytes 524320 | tf_op jit(solution)/shard_map/ppermute | solution.py:40
  284.2 8.3 %collective-permute-done.14 = bf16[256,1024]{1,0:T(8,128)(2,1)S(1)} collective-permute-done((bf16[256,1024]{1,0:T(8,128)(2,1)S(1)}, bf16[256,1024]{1,0:T(8,128)(2,1)S(1)}, u32[]{:S(2)}, u32[]{:S(2)}) %collective-permute-start.14) | collective-permute-done | bytes 524320 | tf_op jit(solution)/shard_map/ppermute | solution.py:40
  313.7 17.5 %all_to_all.79 = bf16[8,256,128]{2,1,0:T(8,128)(2,1)S(1)} all-to-all(bf16[8,256,128]{2,1,0:T(8,128)(2,1)S(1)} %bitcast.110), channel_id=1, replica_groups=mesh['dp'=4,'sp'=4,'blk'=2] {'sp','blk'}, dimensions={0} | all-to-all | bytes 1048576 | tf_op jit(solution)/shard_map/all_to_all | solution.py:346
  331.1 17.7 %attend_backward.1 = bf16[2048,384]{1,0:T(8,128)(2,1)} custom-call(f32[2]{0:T(128)S(1)} %dynamic_slice.9.slopes_ref, bf16[2048,384]{1,0:T(8,128)(2,1)S(1)} %bitcast.96, bf16[2048,128]{1,0:T(8,128)(2,1)S(1)} %bitcast.97, f32[128,2048]{1,0:T(8,128)S(1)} %get-tuple-element.13.ctx_t_ref, f32[2,2048]{1,0:T(2,128)S(1)} %get-tuple-element.14.lse_ref), custom_call_target="tpu_custom_call" | custom-call | flops 5368709120 | bytes 3145728 | tf_op jit(solution)/shard_map/attend_backward/pallas_call | solution.py:223
  352.5 6.0 convolution_convert_fusion.1
  358.8 52.2 %all-to-all-done.6 = bf16[8,256,384]{2,1,0:T(8,128)(2,1)S(1)} async-done(((bf16[8,256,384]{2,1,0:T(8,128)(2,1)}), bf16[8,256,384]{2,1,0:T(8,128)(2,1)S(1)}, u32[]{:S(2)}, u32[]{:S(2)}) %all-to-all-start.6) | async-done | bytes 1572896 | tf_op jit(solution)/shard_map/all_to_all | solution.py:350
  420.6 13.0 %collective-permute-done.29 = bf16[256,1024]{1,0:T(8,128)(2,1)S(1)} collective-permute-done((bf16[256,1024]{1,0:T(8,128)(2,1)S(1)}, bf16[256,1024]{1,0:T(8,128)(2,1)S(1)}, u32[]{:S(2)}, u32[]{:S(2)}) %collective-permute-start.29) | collective-permute-done | bytes 524320 | tf_op jit(solution)/shard_map/ppermute | solution.py:40
  434.8 7.5 %convolution_convert_fusion = bf16[1024,1024]{1,0:T(8,128)(2,1)} fusion(bf16[1024,1024]{1,0:T(8,128)(2,1)} %constant_dynamic-update-slice_fusion.4, f32[1024,1024]{1,0:T(8,128)} %fusion.34, f32[1024]{0:T(1024)S(1)} %dynamic-slice_convert_fusion), kind=kOutput, calls=%fused_computation.23 | convolution fusion | flops 2159017984 | bytes 8392704 | tf_op jit(solution)/shard_map/dot_general | solution.py:35
  450.1 30.7 %all-reduce.3.cloned.1.call-done = bf16[8,4,32,1024]{3,2,0,1:T(8,128)(2,1)} async-done(((bf16[8,4,32,1024]{3,2,0,1:T(8,128)(2,1)}), bf16[8,4,32,1024]{3,2,0,1:T(8,128)(2,1)}) %all-reduce.3.cloned.1.call-update) | async-done | bytes 2097168
  494.6 10.4 %collective-permute-done.26 = bf16[256,1024]{1,0:T(8,128)(2,1)} collective-permute-done((bf16[256,1024]{1,0:T(8,128)(2,1)}, bf16[256,1024]{1,0:T(8,128)(2,1)}, u32[]{:S(2)}, u32[]{:S(2)}) %collective-permute-start.26) | collective-permute-done | bytes 524320 | tf_op jit(solution)/shard_map/ppermute | solution.py:40
  510.9 11.6 %all_to_all.80 = f32[32,1,384]{2,1,0:T(1,128)S(1)} all-to-all(f32[32,1,384]{2,1,0:T(1,128)S(1)} %copy.87), channel_id=1, replica_groups=mesh['dp'=4,'sp'=4,'blk'=2] {'dp','sp','blk'}, dimensions={0} | all-to-all | bytes 98304 | tf_op jit(solution)/shard_map/all_to_all | solution.py:470
  522.5 26.2 %reduce-scatter.7.cloned.1.call-done = bf16[1,4,32,768]{3,2,1,0:T(8,128)(2,1)} async-done(((bf16[8,4,32,768]{3,2,1,0:T(8,128)(2,1)}), bf16[1,4,32,768]{3,2,1,0:T(8,128)(2,1)}) %reduce-scatter.7.cloned.1.call-update) | async-done | bytes 196624 | tf_op jit(solution)/shard_map/reduce_scatter | solution.py:376
  553.0 60.2 %reduce-scatter.9.cloned.1.call-done = bf16[32,1024]{1,0:T(8,128)(2,1)} async-done(((bf16[256,1024]{1,0:T(8,128)(2,1)}), bf16[32,1024]{1,0:T(8,128)(2,1)}) %reduce-scatter.9.cloned.1.call-update) | async-done | bytes 65552 | tf_op jit(solution)/shard_map/reduce_scatter | solution.py:428
  614.7 69.0 %reduce-scatter.11.cloned.1.call-done = bf16[128,1024]{1,0:T(8,128)(2,1)} async-done(((bf16[1024,1024]{1,0:T(8,128)(2,1)}), bf16[128,1024]{1,0:T(8,128)(2,1)}) %reduce-scatter.11.cloned.1.call-update) | async-done | bytes 262160 | tf_op jit(solution)/shard_map/reduce_scatter | solution.py:422
  (280 shorter events, 169.8 us)
Async XLA Ops:
  7.2 55.8 %all-gather.8.cloned.1.call-start = ((), (), s32[]{:S(2)}) async-start(), calls=%async_computation.17 | async-start | bytes 1769472 | tf_op jit(solution)/shard_map/all_gather | solution.py:370
  18.1 22.0 %collective-permute-start.1 = (bf16[256,1024]{1,0:T(8,128)(2,1)}, bf16[256,1024]{1,0:T(8,128)(2,1)S(1)}, u32[]{:S(2)}, u32[]{:S(2)}) collective-permute-start(bf16[256,1024]{1,0:T(8,128)(2,1)} %param.10), channel_id=1, source_target_pairs={{0,16},{8,24},{16,0},{24,8},{1,17},{9,25},{17,1},{25,9},{2,18},{10... | collective-permute-start | bytes 1572872 | tf_op jit(solution)/shard_map/ppermute | solution.py:40
  36.5 39.4 %all-to-all-start.4 = ((bf16[4,32,1024]{2,1,0:T(8,128)(2,1)}), bf16[4,32,1024]{2,1,0:T(8,128)(2,1)S(1)}, u32[]{:S(2)}, u32[]{:S(2)}) async-start(bf16[4,32,1024]{2,1,0:T(8,128)(2,1)} %copy.80), calls=%async_computation.4 | async-start | bytes 524288 | tf_op jit(solution)/shard_map/all_to_all | solution.py:369
  75.8 48.9 %all-to-all-start.2 = ((bf16[8,256,384]{2,1,0:T(8,128)(2,1)}), bf16[8,256,384]{2,1,0:T(8,128)(2,1)S(1)}, u32[]{:S(2)}, u32[]{:S(2)}) async-start(bf16[8,256,384]{2,1,0:T(8,128)(2,1)} %bitcast.101), calls=%async_computation.2 | async-start | bytes 3145728 | tf_op jit(solution)/shard_map/all_to_all | solution.py:346
  79.4 158.3 %all-gather.10.cloned.1.call-start = ((), (), s32[]{:S(2)}) async-start(), calls=%async_computation.18 | async-start | bytes 2359296 | tf_op jit(solution)/shard_map/all_gather | solution.py:370
  137.6 64.2 %all-to-all-start.3 = ((bf16[8,256,128]{2,1,0:T(8,128)(2,1)}), bf16[8,256,128]{2,1,0:T(8,128)(2,1)}, u32[]{:S(2)}, u32[]{:S(2)}) async-start(bf16[8,256,128]{2,1,0:T(8,128)(2,1)} %bitcast.13), calls=%async_computation.3 | async-start | bytes 1048576 | tf_op jit(solution)/shard_map/all_to_all | solution.py:350
  141.7 105.0 %all-gather.6.cloned.1.call-start = ((), (), s32[]{:S(2)}) async-start(), calls=%async_computation.13 | async-start | bytes 2359296 | tf_op jit(solution)/shard_map/all_gather | solution.py:383
  185.1 14.7 %collective-permute-start.6 = (bf16[256,1024]{1,0:T(8,128)(2,1)}, bf16[256,1024]{1,0:T(8,128)(2,1)}, u32[]{:S(2)}, u32[]{:S(2)}) collective-permute-start(bf16[256,1024]{1,0:T(8,128)(2,1)} %all_gather.20), channel_id=1, source_target_pairs={{0,8},{8,0},{16,24},{24,16},{1,9},{9,1},{17,25},{25,17},{2,10},{10... | collective-permute-start | bytes 1572872 | tf_op jit(solution)/shard_map/ppermute | solution.py:40
  185.1 37.3 %collective-permute-start.16 = (bf16[256,1024]{1,0:T(8,128)(2,1)}, bf16[256,1024]{1,0:T(8,128)(2,1)}, u32[]{:S(2)}, u32[]{:S(2)}) collective-permute-start(bf16[256,1024]{1,0:T(8,128)(2,1)} %param.19), channel_id=1, source_target_pairs={{0,16},{8,24},{16,0},{24,8},{1,17},{9,25},{17,1},{25,9},{2,18},{10... | collective-permute-start | bytes 1572872 | tf_op jit(solution)/shard_map/ppermute | solution.py:40
  218.9 14.2 %collective-permute-start.10 = (bf16[256,1024]{1,0:T(8,128)(2,1)}, bf16[256,1024]{1,0:T(8,128)(2,1)}, u32[]{:S(2)}, u32[]{:S(2)}) collective-permute-start(bf16[256,1024]{1,0:T(8,128)(2,1)} %add_convert_fusion.1), channel_id=1, source_target_pairs={{0,16},{8,24},{16,0},{24,8},{1,17},{9,25},{17,1},{25,9},{2,18},{10... | collective-permute-start | bytes 1572872 | tf_op jit(solution)/shard_map/ppermute | solution.py:40
  222.5 14.5 %collective-permute-start.17 = (bf16[256,1024]{1,0:T(8,128)(2,1)}, bf16[256,1024]{1,0:T(8,128)(2,1)S(1)}, u32[]{:S(2)}, u32[]{:S(2)}) collective-permute-start(bf16[256,1024]{1,0:T(8,128)(2,1)} %collective-permute-done.16), channel_id=1, source_target_pairs={{0,8},{8,0},{16,24},{24,16},{1,9},{9,1},{17,25},{25,17},{2,10},{10... | collective-permute-start | bytes 1572872 | tf_op jit(solution)/shard_map/ppermute | solution.py:40
  223.0 16.6 %collective-permute-start.9 = (bf16[256,1024]{1,0:T(8,128)(2,1)}, bf16[256,1024]{1,0:T(8,128)(2,1)}, u32[]{:S(2)}, u32[]{:S(2)}) collective-permute-start(bf16[256,1024]{1,0:T(8,128)(2,1)} %add_convert_fusion.1), channel_id=1, source_target_pairs={{0,8},{8,0},{16,24},{24,16},{1,9},{9,1},{17,25},{25,17},{2,10},{10... | collective-permute-start | bytes 1572872 | tf_op jit(solution)/shard_map/ppermute | solution.py:40
  266.7 15.0 %collective-permute-start.20 = (bf16[256,1024]{1,0:T(8,128)(2,1)}, bf16[256,1024]{1,0:T(8,128)(2,1)}, u32[]{:S(2)}, u32[]{:S(2)}) collective-permute-start(bf16[256,1024]{1,0:T(8,128)(2,1)} %fusion.26), channel_id=1, source_target_pairs={{0,16},{8,24},{16,0},{24,8},{1,17},{9,25},{17,1},{25,9},{2,18},{10... | collective-permute-start | bytes 1572872 | tf_op jit(solution)/shard_map/ppermute | solution.py:40
  268.0 16.2 %collective-permute-start.12 = (bf16[256,1024]{1,0:T(8,128)(2,1)}, bf16[256,1024]{1,0:T(8,128)(2,1)S(1)}, u32[]{:S(2)}, u32[]{:S(2)}) collective-permute-start(bf16[256,1024]{1,0:T(8,128)(2,1)} %get-tuple-element.43), channel_id=1, source_target_pairs={{0,8},{8,0},{16,24},{24,16},{1,9},{9,1},{17,25},{25,17},{2,10},{10... | collective-permute-start | bytes 1572872 | tf_op jit(solution)/shard_map/ppermute | solution.py:40
  269.8 22.7 %collective-permute-start.14 = (bf16[256,1024]{1,0:T(8,128)(2,1)S(1)}, bf16[256,1024]{1,0:T(8,128)(2,1)S(1)}, u32[]{:S(2)}, u32[]{:S(2)}) collective-permute-start(bf16[256,1024]{1,0:T(8,128)(2,1)S(1)} %fusion.28), channel_id=1, source_target_pairs={{0,16},{8,24},{16,0},{24,8},{1,17},{9,25},{17,1},{25,9},{2,18},{10... | collective-permute-start | bytes 1572872 | tf_op jit(solution)/shard_map/ppermute | solution.py:40
  348.9 62.2 %all-to-all-start.6 = ((bf16[8,256,384]{2,1,0:T(8,128)(2,1)}), bf16[8,256,384]{2,1,0:T(8,128)(2,1)S(1)}, u32[]{:S(2)}, u32[]{:S(2)}) async-start(bf16[8,256,384]{2,1,0:T(8,128)(2,1)} %bitcast.29), calls=%async_computation.6 | async-start | bytes 3145728 | tf_op jit(solution)/shard_map/all_to_all | solution.py:350
  352.5 128.4 %all-reduce.3.cloned.1.call-start = ((), (), s32[]{:S(2)}) async-start(), calls=%async_computation.19 | async-start | bytes 4194304
  358.5 190.2 %reduce-scatter.7.cloned.1.call-start = ((), (), s32[]{:S(2)}) async-start(), calls=%async_computation.14 | async-start | bytes 1769472 | tf_op jit(solution)/shard_map/reduce_scatter | solution.py:376
  416.6 196.6 %reduce-scatter.9.cloned.1.call-start = ((), (), s32[]{:S(2)}) async-start(), calls=%async_computation.15 | async-start | bytes 589824 | tf_op jit(solution)/shard_map/reduce_scatter | solution.py:428
  434.7 249.0 %reduce-scatter.11.cloned.1.call-start = ((), (), s32[]{:S(2)}) async-start(), calls=%async_computation.16 | async-start | bytes 2359296 | tf_op jit(solution)/shard_map/reduce_scatter | solution.py:422
  448.8 38.6 %collective-permute-start.25 = (bf16[256,1024]{1,0:T(8,128)(2,1)S(1)}, bf16[256,1024]{1,0:T(8,128)(2,1)S(1)}, u32[]{:S(2)}, u32[]{:S(2)}) collective-permute-start(bf16[256,1024]{1,0:T(8,128)(2,1)S(1)} %get-tuple-element.40), channel_id=1, source_target_pairs={{0,8},{8,0},{16,24},{24,16},{1,9},{9,1},{17,25},{25,17},{2,10},{10... | collective-permute-start | bytes 1572872 | tf_op jit(solution)/shard_map/ppermute | solution.py:40
  483.2 27.7 %all-to-all-start.8 = ((bf16[4,32,1024]{2,1,0:T(8,128)(2,1)}), bf16[4,32,1024]{2,1,0:T(8,128)(2,1)S(1)}, u32[]{:S(2)}, u32[]{:S(2)}) async-start(bf16[4,32,1024]{2,1,0:T(8,128)(2,1)} %dynamic-slice_bitcast_fusion), calls=%async_computation.10 | async-start | bytes 524288 | tf_op jit(solution)/shard_map/all_to_all | solution.py:377
  490.6 14.4 %collective-permute-start.26 = (bf16[256,1024]{1,0:T(8,128)(2,1)}, bf16[256,1024]{1,0:T(8,128)(2,1)}, u32[]{:S(2)}, u32[]{:S(2)}) collective-permute-start(bf16[256,1024]{1,0:T(8,128)(2,1)} %fusion.24), channel_id=1, source_target_pairs={{0,16},{8,24},{16,0},{24,8},{1,17},{9,25},{17,1},{25,9},{2,18},{10... | collective-permute-start | bytes 1572872 | tf_op jit(solution)/shard_map/ppermute | solution.py:40
  548.8 138.7 %all-to-all-start.7 = ((bf16[4,32,768]{2,1,0:T(8,128)(2,1)}), bf16[4,32,768]{2,1,0:T(8,128)(2,1)S(1)}, u32[]{:S(2)}, u32[]{:S(2)}) async-start(bf16[4,32,768]{2,1,0:T(8,128)(2,1)} %bitcast.125), calls=%async_computation.8 | async-start | bytes 393216 | tf_op jit(solution)/shard_map/all_to_all | solution.py:377
  (53 other events, 526.1 us)
Sparse Core Ops, SparseCore 0:
  18.2 44.7 all-gather.7
  83.0 66.3 all-gather.9
  185.8 47.7 all-gather.5
  358.7 122.1 all-reduce.2
  484.1 64.5 reduce-scatter.6
  552.3 60.8 reduce-scatter.8
  616.8 66.8 reduce-scatter.10

commit v2 on v1

--- a/solution.py
+++ b/solution.py
@@ -35,9 +35,9 @@
     return lax.dot_general(a, b, (((0,), (0,)), ((), ())), preferred_element_type=F32)
 
 
-def exchange(value, bit):
-    count = lax.axis_size("dp")
-    return lax.ppermute(value, "dp", [(i, i ^ bit) for i in range(count)])
+def exchange(value, bit, axis="dp"):
+    count = lax.axis_size(axis)
+    return lax.ppermute(value, axis, [(i, i ^ bit) for i in range(count)])
 
 
 def gather_dp(value):
@@ -63,6 +63,32 @@
             pieces[place] = pieces[place].astype(F32) + arrived.astype(F32)
         bit *= 2
     return pieces[0]
+
+
+def to_places_dp(pieces):
+    mine = lax.axis_index("dp")
+    placed = pieces
+    for place in range(1, pieces.shape[0]):
+        other = mine ^ place
+        arrived = exchange(lax.dynamic_index_in_dim(pieces, other, 0), place)
+        placed = lax.dynamic_update_slice_in_dim(placed, arrived, other, 0)
+    return placed
+
+
+def sum_sequence(parts):
+    held = parts.reshape((lax.axis_size("sp"), lax.axis_size("blk")) + parts.shape[1:])
+    for axis, level in (("blk", 1), ("sp", 0)):
+        place, bit = lax.axis_index(axis), 1
+        while bit < lax.axis_size(axis):
+            shape = held.shape
+            halves = held.reshape(shape[:level] + (shape[level] // 2, 2) + shape[level + 1 :])
+            side = place // bit % 2
+            sent = lax.dynamic_index_in_dim(halves, 1 - side, level + 1, keepdims=False)
+            kept = lax.dynamic_index_in_dim(halves, side, level + 1, keepdims=False)
+            arrived = exchange(sent.astype(BF16), bit, axis)
+            held = (kept.astype(F32) + arrived.astype(F32)).astype(BF16)
+            bit *= 2
+    return held.reshape(parts.shape[1:])
 
 
 def one_head(rows, head, head_dim):
@@ -364,23 +390,30 @@
         small[:, gain_size + bias_size :].reshape(-1), dp_place * inner, inner
     ).astype(F32)
 
-    def columns_weight(pieces):
-        columns = pieces.shape[-1]
-        swapped = lax.all_to_all(pieces, "dp", split_axis=0, concat_axis=0, tiled=True)
-        gathered = lax.all_gather(swapped, SEQ_AXES, axis=0, tiled=False)
+    def my_columns(pieces):
+        return lax.all_to_all(pieces, "dp", split_axis=0, concat_axis=0, tiled=True)
+
+    def all_rows(gathered):
+        columns = gathered.shape[-1]
+        gathered = gathered.reshape(ring, dp_count, slice_rows, columns)
         return gathered.transpose(1, 0, 2, 3).reshape(width, columns)
 
     def columns_gradient(grad):
         columns = grad.shape[-1]
-        sent = grad.astype(BF16).reshape(dp_count, ring, slice_rows, columns).transpose(1, 0, 2, 3)
-        summed = lax.psum_scatter(sent, SEQ_AXES, scatter_dimension=0, tiled=False)
-        return lax.all_to_all(summed, "dp", split_axis=0, concat_axis=0, tiled=True)
+        parts = grad.astype(BF16).reshape(dp_count, ring, slice_rows, columns).transpose(1, 0, 2, 3)
+        return to_places_dp(sum_sequence(parts))
 
     qkv_split = w_qkv.reshape(slice_rows, 3, dp_count, groups, pair_width).transpose(2, 0, 3, 1, 4)
-    qkv_weight = columns_weight(qkv_split.reshape(dp_count, slice_rows, 3 * dp_width))
-    dense_part = lax.all_gather(w_dense, SEQ_AXES, axis=0, tiled=True)
-    in_weight = columns_weight(w_in.reshape(slice_rows, dp_count, inner).transpose(1, 0, 2))
-    out_weight = lax.all_gather(w_out, SEQ_AXES, axis=0, tiled=True)
+    qkv_part = my_columns(qkv_split.reshape(dp_count, slice_rows, 3 * dp_width))
+    qkv_weight = all_rows(lax.all_gather(qkv_part, SEQ_AXES, axis=0, tiled=False))
+    in_part = my_columns(w_in.reshape(slice_rows, dp_count, inner).transpose(1, 0, 2))
+    in_part = in_part.reshape(-1, width)
+    in_rows, out_rows = in_part.shape[0], w_out.shape[0]
+    rest = jnp.concatenate([in_part, w_out, w_dense], axis=0)
+    rest = lax.all_gather(rest, SEQ_AXES, axis=0, tiled=False)
+    in_weight = all_rows(rest[:, :in_rows].reshape(ring, dp_count * slice_rows, inner))
+    out_weight = rest[:, in_rows : in_rows + out_rows].reshape(inner, width)
+    dense_part = rest[:, in_rows + out_rows :].reshape(dp_width, width)
     dense_weight = jnp.concatenate(gather_dp(dense_part), axis=0)
 
     rows_in = inputs.astype(F32)
@@ -419,15 +452,12 @@
 
     branch = sum_dp(list(dot_nn(hidden, out_weight).reshape(dp_count, rows, width)))
     output = (middle + (branch + offsets[5])).astype(BF16)
-    grad_w_out = lax.psum_scatter(
-        dot_tn(hidden, grad_tokens).astype(BF16), SEQ_AXES, scatter_dimension=0, tiled=True
-    ).astype(F32)
+    grad_out = dot_tn(hidden, grad_tokens).astype(BF16)
+    grad_w_out = sum_sequence(grad_out.reshape(ring, -1, width)).astype(F32)
     grad_w_in = columns_gradient(dot_tn(normed_two_all, grad_pre))
     grad_w_in = grad_w_in.transpose(1, 0, 2).reshape(slice_rows, -1).astype(F32)
     grad_dense = sum_dp(list(dot_tn(context_tok, grad_att).reshape(dp_count, dp_width, width)))
-    grad_w_dense = lax.psum_scatter(
-        grad_dense.astype(BF16), SEQ_AXES, scatter_dimension=0, tiled=True
-    ).astype(F32)
+    grad_w_dense = sum_sequence(grad_dense.reshape(ring, -1, width)).astype(F32)
 
     if whole_pairs:
         grad_qkv = attend_backward(slopes, qkv, grad_held, *kept, pair_heads, block)

time: 705 us -> 498 us (0.71)
  waiting for transfers between devices: 381 us -> 233 us
  blocking collectives: 80.4 us -> 17.9 us
  starting transfers between devices: 45.9 us -> 66.8 us
  matrix products: 52.3 us -> 40.4 us
    reduce_scatter x3 -> x0, waiting for transfers between devices: 155 us -> none  [the longest x1 69 us: on_device(): lax.psum_scatter(dot_tn(hidden, grad_tokens).astype(BF16), SEQ_AXES, scat...]
    ppermute x30 -> x48, waiting for transfers between devices: 74.3 us -> 129 us  [exchange(): return lax.ppermute(value, axis, [(i, i ^ bit) for i in range(count)])]
    all_to_all x2, waiting for transfers between devices: 52.2 us -> 0.01 us  [collect(): lax.all_to_all(held, pair_axes, split_axis=0, concat_axis=0, tiled=True)]
    all_gather x1 -> x0, blocking collectives: 41.9 us -> none  [on_device(): dense_part = lax.all_gather(w_dense, SEQ_AXES, axis=0, tiled=True)]
    all_to_all x1 -> x2, waiting for transfers between devices: 44.4 us -> 79.2 us  [spread(): lax.all_to_all(sent, pair_axes, split_axis=0, concat_axis=0, tiled=True)]
    unnamed x8 -> x2, waiting for transfers between devices: 31.5 us -> 0.03 us
    ppermute x30 -> x48, starting transfers between devices: 17.2 us -> 41.3 us  [exchange(): return lax.ppermute(value, axis, [(i, i ^ bit) for i in range(count)])]
    all_to_all x3 -> x2, blocking collectives: 38.5 us -> 17.9 us  [my_columns(): return lax.all_to_all(pieces, 'dp', split_axis=0, concat_axis=0, tiled=True)]
  transfers between devices with their start and end apart: 44 -> 56, of which waited for: 19 -> 24; matrix products, arithmetic and copies ran while one was open for 16% -> 21% of each run, Pallas kernels for 2% -> 6%
where the time goes in v2:
time: 498 us; the launch traced here: 488 us
  waiting for transfers between devices  233 us (47%)
  starting transfers between devices  66.8 us (13%)
  local copies, waits for them, and re-layouts  53.6 us (11%)
  matrix products  40.4 us (8%)
  Pallas kernels  30.6 us (6%)
  other arithmetic  30 us (6%)
  blocking collectives  17.9 us (4%)
  between operations  15.9 us (3%)
    ppermute x48, waiting for transfers between devices, exchange(): return lax.ppermute(value, axis, [(i, i ^ bit) for i in range(count)])  129 us
    all_to_all x2, waiting for transfers between devices, spread(): lax.all_to_all(sent, pair_axes, split_axis=0, concat_axis=0, tiled=True)  79.2 us
    ppermute x48, starting transfers between devices, exchange(): return lax.ppermute(value, axis, [(i, i ^ bit) for i in range(count)])  41.3 us
    all_to_all x2, blocking collectives, my_columns(): return lax.all_to_all(pieces, 'dp', split_axis=0, concat_axis=0, tiled=True)  17.9 us
    pallas_call x1, Pallas kernels, attend_backward(): pl.pallas_call(functools.partial(backward_kernel, heads, head_dim, block)...  17.7 us
    dot_general x4, matrix products, dot_nn(): lax.dot_general(a, b, (((1,), (0,)), ((), ())), preferred_element_type=F32)  14.1 us
    dot_general x4, matrix products, dot_nt(): lax.dot_general(a, b, (((1,), (1,)), ((), ())), preferred_element_type=F32)  13.6 us
    pallas_call x1, Pallas kernels, attend_forward(): pl.pallas_call(functools.partial(forward_kernel, heads, head_dim, block),...  12.9 us
  transfers between devices with their start and end apart: 56, of which 24 were waited for; matrix products, arithmetic and copies ran while one was open for 21% of the time, Pallas kernels for 6%

profile of v2, /device:TPU:0, one launch (start us, length us, event | category | flops | bytes accessed | tf_op | source)
XLA Modules:
  0.0 488.3 jit_solution(15031962625410191071)
XLA Ops:
  8.6 9.4 %all_to_all.68 = bf16[4,32,768]{2,1,0:T(8,128)(2,1)} all-to-all(bf16[4,32,768]{2,1,0:T(8,128)(2,1)S(1)} %reshape.483), channel_id=1, replica_groups=mesh['dp'=4,'sp'=4,'blk'=2] {'dp'}, dimensions={0} | all-to-all | bytes 393216 | tf_op jit(solution)/shard_map/all_to_all | solution.py:394
  19.1 8.4 %all_to_all.69 = bf16[4,32,1024]{2,1,0:T(8,128)(2,1)S(1)} all-to-all(bf16[4,32,1024]{2,1,0:T(8,128)(2,1)S(1)} %bitcast.213), channel_id=1, replica_groups=mesh['dp'=4,'sp'=4,'blk'=2] {'dp'}, dimensions={0} | all-to-all | bytes 524288 | tf_op jit(solution)/shard_map/all_to_all | solution.py:394
  32.2 6.4 %all-to-all-start = ((bf16[32,2,192]{2,1,0:T(2,128)(2,1)}), bf16[32,2,192]{2,1,0:T(2,128)(2,1)S(1)}, u32[]{:S(2)}, u32[]{:S(2)}) async-start(bf16[32,2,192]{2,1,0:T(2,128)(2,1)} %reshape.570), calls=%async_computation | async-start | bytes 65536 | tf_op jit(solution)/shard_map/all_to_all | solution.py:382
  39.0 6.8 %all-to-all-done = bf16[32,2,192]{2,1,0:T(2,128)(2,1)S(1)} async-done(((bf16[32,2,192]{2,1,0:T(2,128)(2,1)}), bf16[32,2,192]{2,1,0:T(2,128)(2,1)S(1)}, u32[]{:S(2)}, u32[]{:S(2)}) %all-to-all-start) | async-done | bytes 24608 | tf_op jit(solution)/shard_map/all_to_all | solution.py:382
  50.5 12.7 %all-gather.5.cloned.1.call-done = bf16[32,32,768]{2,1,0:T(8,128)(2,1)} async-done(((bf16[4,32,768]{2,1,0:T(8,128)(2,1)}), bf16[32,32,768]{2,1,0:T(8,128)(2,1)}) %all-gather.5.cloned.1.call-update) | async-done | bytes 1572880 | tf_op jit(solution)/shard_map/all_gather | solution.py:408
  66.0 5.3 %add_convert_fusion = bf16[1024,768]{1,0:T(8,128)(2,1)} fusion(bf16[1024,768]{1,0:T(8,128)(2,1)S(1)} %bitcast.205, f32[768]{0:T(1024)S(1)} %add.305, f32[1024]{0:T(1024)S(1)} %add.301, f32[1024]{0:T(1024)S(1)} %mul.196, f32[1024]{0:T(1024)S(1)} %add_rsqrt_fusion, f32[1024]{0:T(1024)S(1)} %broadcast_multiply_fusion, ...), kind=kOutput, calls=%fused_computation.20 | convolution fusion | flops 1625817088 | bytes 5262336 | tf_op jit(solution)/shard_map/dot_general | solution.py:27
  79.9 69.8 %all-to-all-done.2 = bf16[8,256,384]{2,1,0:T(8,128)(2,1)S(1)} async-done(((bf16[8,256,384]{2,1,0:T(8,128)(2,1)}), bf16[8,256,384]{2,1,0:T(8,128)(2,1)S(1)}, u32[]{:S(2)}, u32[]{:S(2)}) %all-to-all-start.2) | async-done | bytes 1572896 | tf_op jit(solution)/shard_map/all_to_all | solution.py:372
  149.7 12.9 %attend_forward.1 = (bf16[2048,128]{1,0:T(8,128)(2,1)}, f32[128,2048]{1,0:T(8,128)S(1)}, f32[2,2048]{1,0:T(2,128)S(1)}) custom-call(f32[2]{0:T(128)S(1)} %dynamic_slice.109.slopes_ref, bf16[2048,384]{1,0:T(8,128)(2,1)S(1)} %bitcast.171), custom_call_target="tpu_custom_call" | custom-call | flops 2147483648 | bytes 1572864 | tf_op jit(solution)/shard_map/attend_forward/pallas_call | solution.py:226
  162.6 4.6 all-to-all-start.3
  175.5 10.7 %collective-permute-done.7 = bf16[256,1024]{1,0:T(8,128)(2,1)} collective-permute-done((bf16[256,1024]{1,0:T(8,128)(2,1)}, bf16[256,1024]{1,0:T(8,128)(2,1)}, u32[]{:S(2)}, u32[]{:S(2)}) %collective-permute-start.7) | collective-permute-done | bytes 524320 | tf_op jit(solution)/shard_map/ppermute | solution.py:40
  205.9 8.4 %collective-permute-done.16 = bf16[256,1024]{1,0:T(8,128)(2,1)} collective-permute-done((bf16[256,1024]{1,0:T(8,128)(2,1)}, bf16[256,1024]{1,0:T(8,128)(2,1)}, u32[]{:S(2)}, u32[]{:S(2)}) %collective-permute-start.16) | collective-permute-done | bytes 524320 | tf_op jit(solution)/shard_map/ppermute | solution.py:40
  216.7 7.3 %collective-permute-done.10 = bf16[256,1024]{1,0:T(8,128)(2,1)} collective-permute-done((bf16[256,1024]{1,0:T(8,128)(2,1)S(1)}, bf16[256,1024]{1,0:T(8,128)(2,1)}, u32[]{:S(2)}, u32[]{:S(2)}) %collective-permute-start.10) | collective-permute-done | bytes 524320 | tf_op jit(solution)/shard_map/ppermute | solution.py:40
  236.0 5.3 %convert_reduce_fusion.1 = (f32[1024]{0:T(1024)S(1)}, bf16[1024,1024]{1,0:T(8,128)(2,1)S(1)}) fusion(f32[1024,1024]{1,0:T(8,128)S(1)} %fusion.40, f32[1024]{0:T(1024)S(1)} %dynamic-slice_convert_fusion, bf16[1024,1024]{1,0:T(8,128)(2,1)S(1)} %copy-done.23, bf16[1024,1024]{1,0:T(8,128)(2,1)S(1)} %bitcast.203), kind=kOutput, calls=%fused_computation.17 | convolution fusion | flops 2171599872 | bytes 10493952 | tf_op jit(solution)/shard_map/dot_general | solution.py:31
  256.6 17.7 %collective-permute-done.39 = bf16[4,1,4,32,1024]{4,3,2,0,1:T(8,128)(2,1)S(1)} collective-permute-done((bf16[4,1,4,32,1024]{4,3,2,0,1:T(8,128)(2,1)S(1)}, bf16[4,1,4,32,1024]{4,3,2,0,1:T(8,128)(2,1)S(1)}, u32[]{:S(2)}, u32[]{:S(2)}) %collective-permute-start.39) | collective-permute-done | bytes 1048608 | tf_op jit(solution)/shard_map/ppermute | solution.py:40
  278.0 9.5 %collective-permute-done.14 = bf16[256,1024]{1,0:T(8,128)(2,1)S(1)} collective-permute-done((bf16[256,1024]{1,0:T(8,128)(2,1)S(1)}, bf16[256,1024]{1,0:T(8,128)(2,1)S(1)}, u32[]{:S(2)}, u32[]{:S(2)}) %collective-permute-start.14) | collective-permute-done | bytes 524320 | tf_op jit(solution)/shard_map/ppermute | solution.py:40
  319.6 9.4 %all-to-all-done.5 = bf16[8,256,128]{2,1,0:T(8,128)(2,1)S(1)} async-done(((bf16[8,256,128]{2,1,0:T(8,128)(2,1)}), bf16[8,256,128]{2,1,0:T(8,128)(2,1)S(1)}, u32[]{:S(2)}, u32[]{:S(2)}) %all-to-all-start.5) | async-done | bytes 524320 | tf_op jit(solution)/shard_map/all_to_all | solution.py:372
  329.1 17.7 %attend_backward.1 = bf16[2048,384]{1,0:T(8,128)(2,1)} custom-call(f32[2]{0:T(128)S(1)} %dynamic_slice.109.slopes_ref, bf16[2048,384]{1,0:T(8,128)(2,1)S(1)} %bitcast.172, bf16[2048,128]{1,0:T(8,128)(2,1)S(1)} %bitcast.173, f32[128,2048]{1,0:T(8,128)S(1)} %get-tuple-element.13.ctx_t_ref, f32[2,2048]{1,0:T(2,128)S(1)} %get-tuple-element.14.lse_ref), custom_call_target="tpu_custom_call" | custom-call | flops 5368709120 | bytes 3145728 | tf_op jit(solution)/shard_map/attend_backward/pallas_call | solution.py:249
  346.8 4.0 all-to-all-start.6
  360.0 32.5 %collective-permute-done.47 = bf16[1,1,128,1024]{3,2,0,1:T(8,128)(2,1)S(1)} collective-permute-done((bf16[1,1,128,1024]{3,2,0,1:T(8,128)(2,1)S(1)}, bf16[1,1,128,1024]{3,2,0,1:T(8,128)(2,1)S(1)}, u32[]{:S(2)}, u32[]{:S(2)}) %collective-permute-start.47) | collective-permute-done | bytes 262176 | tf_op jit(solution)/shard_map/ppermute | solution.py:40
  392.4 4.7 collective-permute-start.44
  401.5 6.6 %collective-permute-done.36 = bf16[4,1,32,1024]{3,2,0,1:T(8,128)(2,1)S(1)} collective-permute-done((bf16[4,1,32,1024]{3,2,0,1:T(8,128)(2,1)S(1)}, bf16[4,1,32,1024]{3,2,0,1:T(8,128)(2,1)S(1)}, u32[]{:S(2)}, u32[]{:S(2)}) %collective-permute-start.36) | collective-permute-done | bytes 262176 | tf_op jit(solution)/shard_map/ppermute | solution.py:40
  410.0 4.2 collective-permute-done.37
  437.8 8.0 %collective-permute-done.27 = bf16[4,1,4,32,768]{4,3,2,0,1:T(8,128)(2,1)S(1)} collective-permute-done((bf16[4,1,4,32,768]{4,3,2,0,1:T(8,128)(2,1)}, bf16[4,1,4,32,768]{4,3,2,0,1:T(8,128)(2,1)S(1)}, u32[]{:S(2)}, u32[]{:S(2)}) %collective-permute-start.27) | collective-permute-done | bytes 786464 | tf_op jit(solution)/shard_map/ppermute | solution.py:40
  451.5 6.5 %collective-permute-done.28 = bf16[2,1,4,32,768]{4,3,2,0,1:T(8,128)(2,1)S(1)} collective-permute-done((bf16[2,1,4,32,768]{4,3,2,0,1:T(8,128)(2,1)S(1)}, bf16[2,1,4,32,768]{4,3,2,0,1:T(8,128)(2,1)S(1)}, u32[]{:S(2)}, u32[]{:S(2)}) %collective-permute-start.28) | collective-permute-done | bytes 393248 | tf_op jit(solution)/shard_map/ppermute | solution.py:40
  (350 shorter events, 183.6 us)
Async XLA Ops:
  7.2 56.0 %all-gather.5.cloned.1.call-start = ((), (), s32[]{:S(2)}) async-start(), calls=%async_computation.8 | async-start | bytes 1769472 | tf_op jit(solution)/shard_map/all_gather | solution.py:408
  18.1 152.3 %all-gather.7.cloned.1.call-start = ((), (), s32[]{:S(2)}) async-start(), calls=%async_computation.9 | async-start | bytes 5308416 | tf_op jit(solution)/shard_map/all_gather | solution.py:413
  76.2 73.5 %all-to-all-start.2 = ((bf16[8,256,384]{2,1,0:T(8,128)(2,1)}), bf16[8,256,384]{2,1,0:T(8,128)(2,1)S(1)}, u32[]{:S(2)}, u32[]{:S(2)}) async-start(bf16[8,256,384]{2,1,0:T(8,128)(2,1)} %bitcast.179), calls=%async_computation.2 | async-start | bytes 3145728 | tf_op jit(solution)/shard_map/all_to_all | solution.py:372
  162.6 23.7 %all-to-all-start.3 = ((bf16[8,256,128]{2,1,0:T(8,128)(2,1)}), bf16[8,256,128]{2,1,0:T(8,128)(2,1)}, u32[]{:S(2)}, u32[]{:S(2)}) async-start(bf16[8,256,128]{2,1,0:T(8,128)(2,1)} %bitcast.13), calls=%async_computation.3 | async-start | bytes 1048576 | tf_op jit(solution)/shard_map/all_to_all | solution.py:376
  175.5 25.3 %collective-permute-start.6 = (bf16[256,1024]{1,0:T(8,128)(2,1)}, bf16[256,1024]{1,0:T(8,128)(2,1)}, u32[]{:S(2)}, u32[]{:S(2)}) collective-permute-start(bf16[256,1024]{1,0:T(8,128)(2,1)} %bitcast.24), channel_id=1, source_target_pairs={{0,8},{8,0},{16,24},{24,16},{1,9},{9,1},{17,25},{25,17},{2,10},{10... | collective-permute-start | bytes 1572872 | tf_op jit(solution)/shard_map/ppermute | solution.py:40
  248.3 26.0 %collective-permute-start.39 = (bf16[4,1,4,32,1024]{4,3,2,0,1:T(8,128)(2,1)S(1)}, bf16[4,1,4,32,1024]{4,3,2,0,1:T(8,128)(2,1)S(1)}, u32[]{:S(2)}, u32[]{:S(2)}) collective-permute-start(bf16[4,1,4,32,1024]{4,3,2,0,1:T(8,128)(2,1)S(1)} %dynamic-slice_bitcast_fusion.1), channel_id=1, source_target_pairs={{0,1},{1,0},{2,3},{3,2},{4,5},{5,4},{6,7},{7,6},{8,9},{9,8},{10,11... | collective-permute-start | bytes 3145736 | tf_op jit(solution)/shard_map/ppermute | solution.py:40
  251.5 25.9 %collective-permute-start.18 = (bf16[256,1024]{1,0:T(8,128)(2,1)S(1)}, bf16[256,1024]{1,0:T(8,128)(2,1)S(1)}, u32[]{:S(2)}, u32[]{:S(2)}) collective-permute-start(bf16[256,1024]{1,0:T(8,128)(2,1)S(1)} %get-tuple-element.43), channel_id=1, source_target_pairs={{0,8},{8,0},{16,24},{24,16},{1,9},{9,1},{17,25},{25,17},{2,10},{10... | collective-permute-start | bytes 1572872 | tf_op jit(solution)/shard_map/ppermute | solution.py:40
  252.1 25.9 %collective-permute-start.12 = (bf16[256,1024]{1,0:T(8,128)(2,1)S(1)}, bf16[256,1024]{1,0:T(8,128)(2,1)S(1)}, u32[]{:S(2)}, u32[]{:S(2)}) collective-permute-start(bf16[256,1024]{1,0:T(8,128)(2,1)S(1)} %get-tuple-element.45), channel_id=1, source_target_pairs={{0,8},{8,0},{16,24},{24,16},{1,9},{9,1},{17,25},{25,17},{2,10},{10... | collective-permute-start | bytes 1572872 | tf_op jit(solution)/shard_map/ppermute | solution.py:40
  252.6 43.8 %collective-permute-start.45 = (bf16[4,1,128,1024]{3,2,0,1:T(8,128)(2,1)S(1)}, bf16[4,1,128,1024]{3,2,0,1:T(8,128)(2,1)S(1)}, u32[]{:S(2)}, u32[]{:S(2)}) collective-permute-start(bf16[4,1,128,1024]{3,2,0,1:T(8,128)(2,1)S(1)} %dynamic-slice_bitcast_fusion), channel_id=1, source_target_pairs={{0,1},{1,0},{2,3},{3,2},{4,5},{5,4},{6,7},{7,6},{8,9},{9,8},{10,11... | collective-permute-start | bytes 3145736 | tf_op jit(solution)/shard_map/ppermute | solution.py:40
  254.8 22.6 %collective-permute-start.20 = (bf16[256,1024]{1,0:T(8,128)(2,1)S(1)}, bf16[256,1024]{1,0:T(8,128)(2,1)S(1)}, u32[]{:S(2)}, u32[]{:S(2)}) collective-permute-start(bf16[256,1024]{1,0:T(8,128)(2,1)S(1)} %fusion.28), channel_id=1, source_target_pairs={{0,16},{8,24},{16,0},{24,8},{1,17},{9,25},{17,1},{25,9},{2,18},{10... | collective-permute-start | bytes 1572872 | tf_op jit(solution)/shard_map/ppermute | solution.py:40
  277.4 37.2 %collective-permute-start.40 = (bf16[2,1,4,32,1024]{4,3,2,0,1:T(8,128)(2,1)}, bf16[2,1,4,32,1024]{4,3,2,0,1:T(8,128)(2,1)}, u32[]{:S(2)}, u32[]{:S(2)}) collective-permute-start(bf16[2,1,4,32,1024]{4,3,2,0,1:T(8,128)(2,1)} %dynamic-slice_bitcast_fusion.4), channel_id=1, source_target_pairs={{0,2},{2,0},{4,6},{6,4},{1,3},{3,1},{5,7},{7,5},{8,10},{10,8},{12,... | collective-permute-start | bytes 1572872 | tf_op jit(solution)/shard_map/ppermute | solution.py:40
  298.7 52.1 %collective-permute-start.46 = (bf16[2,1,128,1024]{3,2,0,1:T(8,128)(2,1)}, bf16[2,1,128,1024]{3,2,0,1:T(8,128)(2,1)}, u32[]{:S(2)}, u32[]{:S(2)}) collective-permute-start(bf16[2,1,128,1024]{3,2,0,1:T(8,128)(2,1)} %dynamic-slice_bitcast_fusion.3), channel_id=1, source_target_pairs={{0,2},{2,0},{4,6},{6,4},{1,3},{3,1},{5,7},{7,5},{8,10},{10,8},{12,... | collective-permute-start | bytes 1572872 | tf_op jit(solution)/shard_map/ppermute | solution.py:40
  304.1 24.9 %all-to-all-start.5 = ((bf16[8,256,128]{2,1,0:T(8,128)(2,1)}), bf16[8,256,128]{2,1,0:T(8,128)(2,1)S(1)}, u32[]{:S(2)}, u32[]{:S(2)}) async-start(bf16[8,256,128]{2,1,0:T(8,128)(2,1)} %bitcast.200), calls=%async_computation.5 | async-start | bytes 1048576 | tf_op jit(solution)/shard_map/all_to_all | solution.py:372
  312.6 42.6 %collective-permute-start.34 = (bf16[256,1024]{1,0:T(8,128)(2,1)}, bf16[256,1024]{1,0:T(8,128)(2,1)}, u32[]{:S(2)}, u32[]{:S(2)}) collective-permute-start(bf16[256,1024]{1,0:T(8,128)(2,1)} %get-tuple-element.40), channel_id=1, source_target_pairs={{0,8},{8,0},{16,24},{24,16},{1,9},{9,1},{17,25},{25,17},{2,10},{10... | collective-permute-start | bytes 1572872 | tf_op jit(solution)/shard_map/ppermute | solution.py:40
  312.6 85.3 %collective-permute-start.33 = (bf16[256,1024]{1,0:T(8,128)(2,1)}, bf16[256,1024]{1,0:T(8,128)(2,1)}, u32[]{:S(2)}, u32[]{:S(2)}) collective-permute-start(bf16[256,1024]{1,0:T(8,128)(2,1)} %get-tuple-element.39), channel_id=1, source_target_pairs={{0,8},{8,0},{16,24},{24,16},{1,9},{9,1},{17,25},{25,17},{2,10},{10... | collective-permute-start | bytes 1572872 | tf_op jit(solution)/shard_map/ppermute | solution.py:40
  316.8 40.0 %collective-permute-start.41 = (bf16[1,1,4,32,1024]{4,3,2,0,1:T(8,128)(2,1)S(1)}, bf16[1,1,4,32,1024]{4,3,2,0,1:T(8,128)(2,1)}, u32[]{:S(2)}, u32[]{:S(2)}) collective-permute-start(bf16[1,1,4,32,1024]{4,3,2,0,1:T(8,128)(2,1)S(1)} %constant_dynamic-slice_fusion.1), channel_id=1, source_target_pairs={{0,4},{2,6},{4,0},{6,2},{1,5},{3,7},{5,1},{7,3},{8,12},{10,14},{12... | collective-permute-start | bytes 786440 | tf_op jit(solution)/shard_map/ppermute | solution.py:40
  346.8 69.8 %all-to-all-start.6 = ((bf16[8,256,384]{2,1,0:T(8,128)(2,1)}), bf16[8,256,384]{2,1,0:T(8,128)(2,1)S(1)}, u32[]{:S(2)}, u32[]{:S(2)}) async-start(bf16[8,256,384]{2,1,0:T(8,128)(2,1)} %bitcast.33), calls=%async_computation.6 | async-start | bytes 3145728 | tf_op jit(solution)/shard_map/all_to_all | solution.py:376
  352.2 40.2 %collective-permute-start.47 = (bf16[1,1,128,1024]{3,2,0,1:T(8,128)(2,1)S(1)}, bf16[1,1,128,1024]{3,2,0,1:T(8,128)(2,1)S(1)}, u32[]{:S(2)}, u32[]{:S(2)}) collective-permute-start(bf16[1,1,128,1024]{3,2,0,1:T(8,128)(2,1)S(1)} %constant_dynamic-slice_fusion), channel_id=1, source_target_pairs={{0,4},{2,6},{4,0},{6,2},{1,5},{3,7},{5,1},{7,3},{8,12},{10,14},{12... | collective-permute-start | bytes 786440 | tf_op jit(solution)/shard_map/ppermute | solution.py:40
  356.7 41.3 %collective-permute-start.35 = (bf16[256,1024]{1,0:T(8,128)(2,1)S(1)}, bf16[256,1024]{1,0:T(8,128)(2,1)S(1)}, u32[]{:S(2)}, u32[]{:S(2)}) collective-permute-start(bf16[256,1024]{1,0:T(8,128)(2,1)S(1)} %fusion.24), channel_id=1, source_target_pairs={{0,16},{8,24},{16,0},{24,8},{1,17},{9,25},{17,1},{25,9},{2,18},{10... | collective-permute-start | bytes 1572872 | tf_op jit(solution)/shard_map/ppermute | solution.py:40
  357.8 43.5 %collective-permute-start.42 = (bf16[1,32,1024]{2,1,0:T(8,128)(2,1)S(1)}, bf16[1,32,1024]{2,1,0:T(8,128)(2,1)S(1)}, u32[]{:S(2)}, u32[]{:S(2)}) collective-permute-start(bf16[1,32,1024]{2,1,0:T(8,128)(2,1)S(1)} %get-tuple-element.60), channel_id=1, source_target_pairs={{0,8},{8,0},{16,24},{24,16},{1,9},{9,1},{17,25},{25,17},{2,10},{10... | collective-permute-start | bytes 196616 | tf_op jit(solution)/shard_map/ppermute | solution.py:40
  357.9 43.5 %collective-permute-start.43 = (bf16[1,32,1024]{2,1,0:T(8,128)(2,1)S(1)}, bf16[1,32,1024]{2,1,0:T(8,128)(2,1)S(1)}, u32[]{:S(2)}, u32[]{:S(2)}) collective-permute-start(bf16[1,32,1024]{2,1,0:T(8,128)(2,1)S(1)} %get-tuple-element.59), channel_id=1, source_target_pairs={{0,16},{8,24},{16,0},{24,8},{1,17},{9,25},{17,1},{25,9},{2,18},{10... | collective-permute-start | bytes 196616 | tf_op jit(solution)/shard_map/ppermute | solution.py:40
  414.9 54.2 %collective-permute-start.38 = (bf16[1,1,32,1024]{3,2,0,1:T(8,128)(2,1)}, bf16[1,1,32,1024]{3,2,0,1:T(8,128)(2,1)}, u32[]{:S(2)}, u32[]{:S(2)}) collective-permute-start(bf16[1,1,32,1024]{3,2,0,1:T(8,128)(2,1)} %constant_dynamic-slice_fusion.2), channel_id=1, source_target_pairs={{0,4},{2,6},{4,0},{6,2},{1,5},{3,7},{5,1},{7,3},{8,12},{10,14},{12... | collective-permute-start | bytes 196616 | tf_op jit(solution)/shard_map/ppermute | solution.py:40
  426.7 22.4 %collective-permute-start.24 = (bf16[256,1024]{1,0:T(8,128)(2,1)S(1)}, bf16[256,1024]{1,0:T(8,128)(2,1)S(1)}, u32[]{:S(2)}, u32[]{:S(2)}) collective-permute-start(bf16[256,1024]{1,0:T(8,128)(2,1)S(1)} %get-tuple-element.41), channel_id=1, source_target_pairs={{0,8},{8,0},{16,24},{24,16},{1,9},{9,1},{17,25},{25,17},{2,10},{10... | collective-permute-start | bytes 1572872 | tf_op jit(solution)/shard_map/ppermute | solution.py:40
  427.7 21.4 %collective-permute-start.26 = (bf16[256,1024]{1,0:T(8,128)(2,1)S(1)}, bf16[256,1024]{1,0:T(8,128)(2,1)S(1)}, u32[]{:S(2)}, u32[]{:S(2)}) collective-permute-start(bf16[256,1024]{1,0:T(8,128)(2,1)S(1)} %fusion.26), channel_id=1, source_target_pairs={{0,16},{8,24},{16,0},{24,8},{1,17},{9,25},{17,1},{25,9},{2,18},{10... | collective-permute-start | bytes 1572872 | tf_op jit(solution)/shard_map/ppermute | solution.py:40
  (78 other events, 821.4 us)
Sparse Core Ops, SparseCore 0:
  18.2 44.9 all-gather.4
  66.0 104.4 all-gather.6

commit v3 on v2

v3 whole, which is shorter than its diff:
```python
import functools
import math

import jax
import jax.numpy as jnp
from jax import lax
from jax.experimental import pallas as pl
from jax.experimental.pallas import tpu as pltpu
from jax.sharding import PartitionSpec as P

H = 16
DP = ("x", "core")
ALL = ("x", "core", "sp", "blk")
SEQ_AXES = ("sp", "blk")
F32 = jnp.float32
BF16 = jnp.bfloat16
LOG2E = 1.4426950408889634


def norm_rows(features, gain_row, offset):
    row_mean = jnp.mean(features, axis=-1, keepdims=True)
    centered = features - row_mean
    variance = jnp.mean(centered * centered, axis=-1, keepdims=True)
    return centered * lax.rsqrt(variance + 1e-05) * gain_row + offset


def dot_nn(a, b):
    return lax.dot_general(a, b, (((1,), (0,)), ((), ())), preferred_element_type=F32)


def dot_nt(a, b):
    return lax.dot_general(a, b, (((1,), (1,)), ((), ())), preferred_element_type=F32)


def dot_tn(a, b):
    return lax.dot_general(a, b, (((0,), (0,)), ((), ())), preferred_element_type=F32)


def exchange(value, bit, axis=DP):
    count = lax.axis_size(axis)
    return lax.ppermute(value, axis, [(i, i ^ bit) for i in range(count)])


def gather_dp(value):
    pieces = {0: value}
    bit = lax.axis_size(DP) // 2
    while bit:
        for place in list(pieces):
            pieces[place | bit] = exchange(pieces[place], bit)
        bit //= 2
    return [pieces[place] for place in range(len(pieces))]


def sum_bits_first(pieces):
    arrived = [exchange(piece.astype(BF16), 1) for piece in pieces[1::2]]
    return [a.astype(F32) + b.astype(F32) for a, b in zip(pieces[::2], arrived, strict=True)]


def sum_bits_rest(pieces):
    bit = 2
    while len(pieces) > 1:
        arrived = [exchange(piece.astype(BF16), bit) for piece in pieces[1::2]]
        pieces = [a.astype(F32) + b.astype(F32) for a, b in zip(pieces[::2], arrived, strict=True)]
        bit *= 2
    return pieces[0]


def swap_dp(pieces):
    return [pieces[0]] + [exchange(pieces[place], place) for place in range(1, len(pieces))]


def sum_dp(pieces):
    pieces = dict(enumerate(pieces))
    count, bit = len(pieces), 1
    while bit < count:
        for place in range(0, count, 2 * bit):
            arrived = exchange(pieces[place + bit].astype(BF16), bit)
            pieces[place] = pieces[place].astype(F32) + arrived.astype(F32)
        bit *= 2
    return pieces[0]


def to_places_dp(pieces):
    mine = lax.axis_index(DP)
    placed = pieces
    for place in range(1, pieces.shape[0]):
        other = mine ^ place
        arrived = exchange(lax.dynamic_index_in_dim(pieces, other, 0), place)
        placed = lax.dynamic_update_slice_in_dim(placed, arrived, other, 0)
    return placed


def bits_of(axis, first=1):
    bits, bit = [], first
    while bit < lax.axis_size(axis):
        bits.append((axis, bit))
        bit *= 2
    return bits


def side_of(axis, bit):
    return lax.axis_index(axis) // bit % 2


def in_order(mine, other, side, level):
    above = side == 1
    return jnp.stack([jnp.where(above, other, mine), jnp.where(above, mine, other)], axis=level)


def gather_bits(held, bits, level):
    for axis, bit in bits:
        held = in_order(held, exchange(held, bit, axis), side_of(axis, bit), level)
        level += 1
    return held, level


def sum_bits(held, bits, level):
    for axis, bit in bits:
        shape = held.shape
        halves = held.reshape(shape[:level] + (shape[level] // 2, 2) + shape[level + 1 :])
        side = side_of(axis, bit)
        sent = lax.dynamic_index_in_dim(halves, 1 - side, level + 1, keepdims=False)
        kept = lax.dynamic_index_in_dim(halves, side, level + 1, keepdims=False)
        arrived = exchange(sent.astype(BF16), bit, axis)
        held = (kept.astype(F32) + arrived.astype(F32)).astype(BF16)
    return jnp.squeeze(held, level)


def sum_sequence(parts):
    held = parts.reshape((lax.axis_size("sp"), lax.axis_size("blk")) + parts.shape[1:])
    return sum_bits(sum_bits(held, bits_of("blk"), 1), bits_of("sp"), 0)


def gather_group(value, bits):
    pieces = [value]
    for axis, bit in bits:
        pieces = pieces + [exchange(piece, bit, axis) for piece in pieces]
    return pieces


def sum_group(pieces, bits):
    for axis, bit in reversed(bits):
        half = len(pieces) // 2
        arrived = [exchange(piece.astype(BF16), bit, axis) for piece in pieces[half:]]
        pieces = [a.astype(F32) + b.astype(F32) for a, b in zip(pieces[:half], arrived, strict=True)]
    return pieces[0]


def lanes_of(rows, first, count):
    lane = lax.broadcasted_iota(jnp.int32, rows.shape, 1)
    return jnp.where((lane >= first) & (lane < first + count), rows, jnp.zeros_like(rows))


def queries_at_keys(rows, head_dim):
    return lanes_of(jnp.concatenate([rows[:, head_dim:], rows[:, :head_dim]], axis=1), head_dim, head_dim)


def score_tile(keys, queries, scale, slope, key_first, query_first, masked):
    scores = dot_nt(keys, queries) * scale
    key_row = lax.broadcasted_iota(jnp.int32, (keys.shape[0], 1), 0)
    ahead = key_first - query_first
    scores = scores + (key_row.astype(F32) * slope + ahead.astype(F32) * slope)
    if masked:
        key_place = lax.broadcasted_iota(jnp.int32, scores.shape, 0) + ahead
        query_place = lax.broadcasted_iota(jnp.int32, scores.shape, 1)
        scores = jnp.where(key_place <= query_place, scores, -1e30)
    return scores


def forward_kernel(head, last, head_dim, block, slopes_ref, qk_ref, value_ref, *refs):
    earlier, (ctx_t_ref, lse_ref) = refs[:head] if last else (), refs[head if last else 0 :][:2]
    value_t_ref = refs[-1]
    step = pl.program_id(0)
    scale = LOG2E / math.sqrt(head_dim)
    slope = slopes_ref[head] * LOG2E

    @pl.when(step == 0)
    def _():
        values_t = value_ref[...].astype(F32).T.astype(BF16)
        value_t_ref[...] = values_t[head * head_dim : (head + 1) * head_dim]

    firsts = [pl.multiple_of((2 * step + half) * block, block) for half in range(2)]
    queries = [queries_at_keys(qk_ref[pl.ds(first, block), :], head_dim) for first in firsts]

    def tile(index, running, masks):
        key_first = pl.multiple_of(index * block, block)
        keys = qk_ref[pl.ds(key_first, block), :]
        values = value_t_ref[:, pl.ds(key_first, block)]
        after = list(running)
        for half, masked in masks:
            top, total, context = running[half]
            scores = score_tile(keys, queries[half], scale, slope, key_first, firsts[half], masked)
            new_top = jnp.maximum(top, jnp.max(scores, axis=0, keepdims=True))
            exponent = jnp.exp2(scores - new_top)
            shrink = jnp.exp2(top - new_top)
            total = total * shrink + jnp.sum(exponent, axis=0, keepdims=True)
            after[half] = (new_top, total, context * shrink + dot_nn(values, exponent.astype(BF16)))
        return tuple(after)

    start = (
        jnp.full((1, block), -1e30, F32),
        jnp.zeros((1, block), F32),
        jnp.zeros((head_dim, block), F32),
    )
    both = ((0, False), (1, False))
    running = lax.fori_loop(0, 2 * step, lambda index, held: tile(index, held, both), (start, start))
    running = tile(2 * step, running, ((0, True), (1, False)))
    running = tile(2 * step + 1, running, ((1, True),))
    for first, (top, total, context) in zip(firsts, running, strict=True):
        here = pl.ds(first, block)
        context = context * (1.0 / total)
        ctx_t_ref[:, here] = context
        lse_ref[:, here] = top + jnp.log2(total)
        if last:
            heads = [ref[:, here] for ref in earlier] + [context]
            refs[-2][here, :] = jnp.concatenate(heads, axis=0).T.astype(BF16)


def backward_kernel(
    head,
    head_dim,
    block,
    slopes_ref,
    qk_ref,
    value_ref,
    grad_ref,
    ctx_t_ref,
    lse_ref,
    *refs,
):
    key_t_ref, grad_key_ref, grad_sum_ref = refs[-3:]
    width = 2 * head_dim
    later, outs = (refs[:-4], refs[-4:-3]) if head == 0 else ((), refs[:2])
    step = pl.program_id(0)
    scale = LOG2E / math.sqrt(head_dim)
    unit = 1.0 / math.sqrt(head_dim)
    slope = slopes_ref[head] * LOG2E

    @pl.when(step == 0)
    def _():
        key_t_ref[...] = qk_ref[...].astype(F32).T[head_dim:].astype(BF16)
        grad_key_ref[...] = jnp.zeros_like(grad_key_ref)
        grad_sum_ref[...] = jnp.zeros_like(grad_sum_ref)

    firsts, queries, grads, deltas, lses = [], [], [], [], []
    for half in range(2):
        first = pl.multiple_of((2 * step + half) * block, block)
        here = pl.ds(first, block)
        grad_rows = grad_ref[here, :]
        grads_t = grad_rows.astype(F32).T[head * head_dim : (head + 1) * head_dim]
        firsts.append(first)
        queries.append(queries_at_keys(qk_ref[here, :], head_dim))
        grads.append(lanes_of(grad_rows, head * head_dim, head_dim))
        deltas.append(jnp.sum(grads_t * ctx_t_ref[:, here], axis=0, keepdims=True))
        lses.append(lse_ref[:, here])

    def tile(index, running, masks):
        key_first = pl.multiple_of(index * block, block)
        here = pl.ds(key_first, block)
        keys, values, keys_t = qk_ref[here, :], value_ref[here, :], key_t_ref[:, here]
        grad_sum, grad_key = grad_sum_ref[here, :], grad_key_ref[here, :]
        after = list(running)
        for half, masked in masks:
            scores = score_tile(keys, queries[half], scale, slope, key_first, firsts[half], masked)
            weights = jnp.exp2(scores - lses[half])
            grad_weights = dot_nt(values, grads[half])
            grad_scores = (weights * (grad_weights - deltas[half])).astype(BF16)
            grad_sum = grad_sum + dot_nn(weights.astype(BF16), grads[half])
            grad_key = grad_key + dot_nn(grad_scores, queries[half])
            after[half] = running[half] + dot_nn(keys_t, grad_scores)
        grad_sum_ref[here, :] = grad_sum
        grad_key_ref[here, :] = grad_key
        return tuple(after)

    start = jnp.zeros((head_dim, block), F32)
    both = ((0, False), (1, False))
    running = lax.fori_loop(0, 2 * step, lambda index, held: tile(index, held, both), (start, start))
    running = tile(2 * step, running, ((0, True), (1, False)))
    running = tile(2 * step + 1, running, ((1, True),))
    for first, total in zip(firsts, running, strict=True):
        grad_query = jnp.concatenate([total * unit, jnp.zeros_like(total)], axis=0).T
        outs[0][pl.ds(first, block), :width] = grad_query.astype(BF16)

    @pl.when(step == pl.num_programs(0) - 1)
    def _():
        outs[0][:, :width] = outs[0][:, :width] + (grad_key_ref[...] * unit).astype(BF16)
        grad_value = grad_sum_ref[...].astype(BF16)
        if head == 0:
            outs[0][:, width:] = sum((ref[...] for ref in later), grad_value)
        else:
            outs[1][...] = grad_value


def whole(count):
    return [pl.BlockSpec(memory_space=pltpu.VMEM)] * count


def columns_spec(array, width, place):
    return pl.BlockSpec((array.shape[0], width), lambda step: (0, place))


def attend_forward(slopes, qk, first, head, heads, earlier, block):
    length, width = first.shape[0], first.shape[1] // 2
    head_dim = width // heads
    pairs = length * length // 2
    last = head == heads - 1
    taken = tuple(earlier) if last else ()
    out_shape = [jax.ShapeDtypeStruct((head_dim, length), F32), jax.ShapeDtypeStruct((1, length), F32)]
    if last:
        out_shape.append(jax.ShapeDtypeStruct((length, width), BF16))
    return pl.pallas_call(
        functools.partial(forward_kernel, head, last, head_dim, block),
        grid=(length // (2 * block),),
        out_shape=tuple(out_shape),
        in_specs=[
            pl.BlockSpec(memory_space=pltpu.SMEM),
            columns_spec(qk, width, 0),
            columns_spec(first, width, 1),
        ]
        + whole(len(taken)),
        out_specs=tuple(whole(len(out_shape))),
        scratch_shapes=[pltpu.VMEM((head_dim, length), BF16)],
        compiler_params=pltpu.CompilerParams(vmem_limit_bytes=40 << 20),
        cost_estimate=pl.CostEstimate(
            flops=64 * pairs * head_dim, bytes_accessed=16 * length * head_dim, transcendentals=pairs
        ),
        name="attend_forward",
    )(slopes, qk, first, *taken)


def attend_backward(slopes, qk, first, grad, ctx_t, lse, head, heads, later, block):
    length, width = first.shape[0], first.shape[1] // 2
    head_dim = width // heads
    pairs = length * length // 2
    taken = tuple(later) if head == 0 else ()
    out_shape = [jax.ShapeDtypeStruct(first.shape, BF16)]
    if head:
        out_shape = [jax.ShapeDtypeStruct((length, width), BF16)] * 2
    return pl.pallas_call(
        functools.partial(backward_kernel, head, head_dim, block),
        grid=(length // (2 * block),),
        out_shape=tuple(out_shape),
        in_specs=[
            pl.BlockSpec(memory_space=pltpu.SMEM),
            columns_spec(qk, width, 0),
            columns_spec(first, width, 1),
        ]
        + whole(3 + len(taken)),
        out_specs=tuple(whole(len(out_shape))),
        scratch_shapes=[
            pltpu.VMEM((head_dim, length), BF16),
            pltpu.VMEM((length, width), F32),
            pltpu.VMEM((length, width), F32),
        ],
        compiler_params=pltpu.CompilerParams(vmem_limit_bytes=40 << 20),
        cost_estimate=pl.CostEstimate(
            flops=80 * pairs * head_dim, bytes_accessed=32 * length * head_dim, transcendentals=pairs
        ),
        name="attend_backward",
    )(slopes, qk, first, grad, ctx_t, lse, *taken)


def split_scores(query_rows, row_places, key_rows, key_places, slopes, score_scale):
    scores = jnp.einsum("qhe,khe->hqk", query_rows, key_rows, preferred_element_type=F32) * score_scale
    distance = (row_places[:, None] - key_places[None, :]).astype(F32)
    scores = scores - slopes[:, None, None] * distance[None]
    return jnp.where((distance >= 0)[None], scores, -1e30)


def split_setup(qkv, heads, rows_each):
    local, width = qkv.shape[0], qkv.shape[1] // 3
    shape = (heads, width // heads)
    parts, mine = lax.axis_size("blk"), lax.axis_index("blk")
    held = lax.all_gather(qkv[:, width:], "blk", axis=0, tiled=False)
    held = held.reshape(parts, local // rows_each, rows_each, 2 * width).transpose(1, 0, 2, 3)
    held = held.reshape(parts * local, 2 * width)
    index = jnp.arange(local, dtype=jnp.int32)
    places = (index // rows_each * parts + mine) * rows_each + index % rows_each
    block = min(512, local)
    return (
        qkv[:, :width].reshape((local // block, block) + shape),
        held[:, :width].reshape((parts * local,) + shape),
        held[:, width:].reshape((parts * local,) + shape),
        places.reshape(local // block, block),
        jnp.arange(parts * local, dtype=jnp.int32),
        1.0 / math.sqrt(width // heads),
    )


def split_forward(slopes, qkv, heads, rows_each):
    queries, keys, values, places, key_places, scale = split_setup(qkv, heads, rows_each)

    def one_block(item):
        chosen, block_places = item
        scores = split_scores(chosen, block_places, keys, key_places, slopes, scale)
        top = jnp.max(scores, axis=-1, keepdims=True)
        exponent = jnp.exp(scores - top)
        total = jnp.sum(exponent, axis=-1, keepdims=True)
        weights = (exponent / total).astype(BF16)
        context = jnp.einsum("hqk,khe->qhe", weights, values, preferred_element_type=F32)
        return context.astype(BF16), top, total

    contexts, tops, totals = lax.map(one_block, (queries, places))
    return contexts.reshape(qkv.shape[0], -1), tops, totals


def split_backward(slopes, qkv, grad, tops, totals, heads, rows_each):
    queries, keys, values, places, key_places, scale = split_setup(qkv, heads, rows_each)
    grads = grad.reshape(queries.shape)

    def one_block(running, item):
        grad_keys, grad_values = running
        chosen, block_places, grad_rows, top, total = item
        scores = split_scores(chosen, block_places, keys, key_places, slopes, scale)
        weights = jnp.exp(scores - top) / total
        grad_values = grad_values + jnp.einsum(
            "hqk,qhe->khe", weights.astype(BF16), grad_rows, preferred_element_type=F32
        )
        grad_probs = jnp.einsum("qhe,khe->hqk", grad_rows, values, preferred_element_type=F32)
        grad_scores = (
            weights * (grad_probs - jnp.sum(weights * grad_probs, axis=-1, keepdims=True))
        ).astype(BF16)
        grad_query = jnp.einsum("hqk,khe->qhe", grad_scores, keys, preferred_element_type=F32) * scale
        grad_keys = (
            grad_keys
            + jnp.einsum("hqk,qhe->khe", grad_scores, chosen, preferred_element_type=F32) * scale
        )
        return (grad_keys, grad_values), grad_query.astype(BF16)

    empty = jnp.zeros(keys.shape, F32)
    (grad_keys, grad_values), grad_queries = lax.scan(
        one_block, (empty, empty), (queries, places, grads, tops, totals)
    )
    local, width = grad.shape
    both = jnp.concatenate([grad_keys.reshape(-1, width), grad_values.reshape(-1, width)], axis=1)
    parts = lax.axis_size("blk")
    both = both.reshape(local // rows_each, parts, rows_each, 2 * width).transpose(1, 0, 2, 3)
    own = lax.psum_scatter(both, "blk", scatter_dimension=0, tiled=False)
    own = own.reshape(local, 2 * width).astype(BF16)
    return jnp.concatenate([grad_queries.reshape(local, width), own], axis=1)


def on_device(
    inputs, w_qkv, w_dense, w_in, w_out, norm_gains, biases, in_bias, alibi_slopes, upstream
):
    dp_count, sp_count, blk_count = (lax.axis_size(axis) for axis in (DP, "sp", "blk"))
    dp_place = lax.axis_index(DP)
    ring = sp_count * blk_count
    devices = dp_count * ring
    rows, width = inputs.shape
    slice_rows = w_qkv.shape[0]
    head_dim = width // H
    dp_heads = H // dp_count
    dp_width = dp_heads * head_dim

    whole_pairs = ring % dp_count == 0 and dp_heads == 2 * (ring // dp_count)
    pair_axes = SEQ_AXES if whole_pairs else ("sp",)
    owners = ring if whole_pairs else sp_count
    groups = owners // dp_count
    pair_heads = dp_heads // groups
    pair_width = pair_heads * head_dim

    def spread(pieces):
        columns = pieces.shape[-1]
        sent = pieces.transpose(0, 2, 1, 3).reshape(owners * rows, columns)
        return lax.all_to_all(sent, pair_axes, split_axis=0, concat_axis=0, tiled=True)

    def collect(held):
        columns = held.shape[-1]
        got = lax.all_to_all(held, pair_axes, split_axis=0, concat_axis=0, tiled=True)
        return got.reshape(dp_count, groups, rows, columns).transpose(0, 2, 1, 3)

    def my_columns(pieces):
        return lax.all_to_all(pieces, DP, split_axis=0, concat_axis=0, tiled=True)

    split = w_qkv.reshape(slice_rows, 3, dp_count, groups, pair_heads, head_dim)

    def part_columns(query, key, value):
        lead = value.shape[:-3]
        all_values = value.reshape(lead + (groups, 1, pair_width))
        pairs = [
            jnp.concatenate([query[..., head, :], key[..., head, :]], axis=-1) for head in range(pair_heads)
        ]
        pairs[0] = jnp.concatenate([pairs[0], all_values[..., 0, :]], axis=-1)
        return [pair.reshape(lead + (-1,)) for pair in pairs]

    sizes = [2 * groups * head_dim + dp_width] + [2 * groups * head_dim] * (pair_heads - 1)
    starts = [sum(sizes[:place]) for place in range(len(sizes))]

    def cut(columns):
        return [columns[..., start : start + size] for start, size in zip(starts, sizes, strict=True)]

    qkv_split = jnp.concatenate(part_columns(split[:, 0], split[:, 1], split[:, 2]), axis=-1)
    qkv_part = my_columns(qkv_split.transpose(1, 0, 2))
    qkv_part, inputs_sent, upstream_sent, w_dense, w_in, w_out, in_bias = lax.optimization_barrier(
        (qkv_part, inputs, upstream, w_dense, w_in, w_out, in_bias)
    )
    tokens = jnp.concatenate(gather_dp(inputs_sent), axis=0)
    group_bits = bits_of("x") + [("core", 1)]
    x_count = dp_count // 2
    ff_rows = in_bias.shape[0]
    inner = ff_rows * ring
    grad_pieces = gather_group(upstream_sent, group_bits)
    small = jnp.concatenate([norm_gains.reshape(-1), biases.reshape(-1), in_bias])
    small = lax.all_to_all(
        jnp.broadcast_to(small[None], (devices, small.shape[0])), ALL, split_axis=0, concat_axis=0, tiled=True
    )
    gain_size, bias_size = norm_gains.size, biases.size
    gains_row = small[:, :gain_size].reshape(devices, 2, -1).transpose(1, 0, 2).reshape(2, width).astype(F32)
    offsets = small[:, gain_size : gain_size + bias_size].reshape(devices, 6, -1)
    offsets = offsets.transpose(1, 0, 2).reshape(6, width).astype(F32)
    in_offset = small[:, gain_size + bias_size :].reshape(dp_count, inner)
    in_offset = lax.dynamic_index_in_dim(in_offset, dp_place, 0, keepdims=False).astype(F32)

    def all_rows(gathered):
        columns = gathered.shape[-1]
        gathered = gathered.reshape(ring, dp_count, slice_rows, columns)
        return gathered.transpose(1, 0, 2, 3).reshape(width, columns)

    def by_owner(grad):
        return grad.reshape(dp_count, ring, slice_rows, -1).transpose(1, 0, 2, 3)

    def split_ring(parts):
        return parts.reshape((sp_count, blk_count) + parts.shape[1:])

    qkv_weight = all_rows(lax.all_gather(qkv_part, SEQ_AXES, axis=0, tiled=False))
    early = jnp.concatenate([w_dense, w_out], axis=0)
    early = lax.all_gather(early, SEQ_AXES, axis=0, tiled=False)
    dense_pieces = gather_dp(early[:, :slice_rows].reshape(dp_width, width))
    dense_weight = jnp.concatenate(dense_pieces, axis=0)
    out_weight = early[:, slice_rows:].reshape(inner, width)
    in_part = my_columns(w_in.reshape(slice_rows, dp_count, inner).transpose(1, 0, 2))
    in_weight = all_rows(lax.all_gather(in_part, SEQ_AXES, axis=0, tiled=False))

    rows_in = inputs.astype(F32)
    normed_one = norm_rows(tokens.astype(F32), gains_row[0], offsets[0]).astype(BF16)
    own_offset = lax.dynamic_slice_in_dim(offsets, dp_place * dp_width, dp_width, 1)
    own_offset = own_offset.reshape(6, groups, pair_heads, head_dim)
    part_offsets = part_columns(own_offset[1], jnp.zeros_like(own_offset[1]), own_offset[2])
    held = []
    for weight, offset in zip(cut(qkv_weight), part_offsets, strict=True):
        projected = (dot_nn(normed_one, weight) + offset).astype(BF16)
        held.append(spread(projected.reshape(dp_count, rows, groups, -1)))
    group = lax.axis_index(pair_axes) % groups
    slopes = lax.dynamic_slice_in_dim(alibi_slopes, dp_place * dp_heads + group * pair_heads, pair_heads)
    if whole_pairs:
        block = min(512, ring * rows // 2)
        contexts, lses = [], []
        for head in range(pair_heads):
            context_t, lse, *context = attend_forward(
                slopes, held[head], held[0], head, pair_heads, contexts, block
            )
            contexts.append(context_t)
            lses.append(lse)
        context = context[0]
    else:
        queries = [item[:, :head_dim] for item in held]
        keys = [item[:, head_dim : 2 * head_dim] for item in held]
        qkv = jnp.concatenate(queries + keys + [held[0][:, 2 * head_dim :]], axis=1)
        context, *kept = split_forward(slopes, qkv, pair_heads, rows)
    context_tok = collect(context).reshape(dp_count, rows, dp_width)
    context_tok = jnp.concatenate(swap_dp([context_tok[k] for k in range(dp_count)]), axis=1)
    middle = rows_in + (dot_nn(context_tok, dense_weight) + offsets[3])
    normed_two = norm_rows(middle, gains_row[1], offsets[4]).astype(BF16)

    grad_top = upstream.astype(F32)
    grad_in_offset, grad_out, grad_in = 0.0, 0.0, 0.0
    pieces = gather_group(normed_two, group_bits)
    branch, grad_two = [None] * len(pieces), [None] * len(pieces)
    for place in range(x_count):
        normed = jnp.concatenate(pieces[place::x_count], axis=0)
        grads = jnp.concatenate(grad_pieces[place::x_count], axis=0)
        hidden_pre = dot_nn(normed, in_weight) + in_offset
        hidden, gelu_pull = jax.vjp(jax.nn.gelu, hidden_pre)
        hidden = hidden.astype(BF16)
        grad_pre = gelu_pull(dot_nt(grads, out_weight))[0].astype(BF16)
        grad_two[place::x_count] = list(dot_nt(grad_pre, in_weight).reshape(2, rows, width))
        branch[place::x_count] = list(dot_nn(hidden, out_weight).reshape(2, rows, width))
        grad_in_offset += jnp.sum(grad_pre.astype(F32), axis=0)
        grad_out += dot_tn(hidden, grads)
        grad_in += dot_tn(normed, grad_pre)
    grad_normed_two = sum_group(grad_two, group_bits)
    grad_in = by_owner(grad_in.astype(BF16)).reshape(ring, -1, width)
    grad_out = grad_out.astype(BF16).reshape(ring, ff_rows, width)
    grad_both = jnp.concatenate([grad_in, grad_out], axis=1).reshape(-1, width)
    grad_normed_two, grad_both = lax.optimization_barrier((grad_normed_two, grad_both))
    grad_both = lax.psum_scatter(grad_both, SEQ_AXES, scatter_dimension=0, tiled=True)
    _, second_pull = jax.vjp(norm_rows, middle, gains_row[1], offsets[4])
    grad_mid_part, grad_gain_two, grad_shift_two = second_pull(grad_normed_two)
    grad_middle = grad_top + grad_mid_part
    grad_att = grad_middle.astype(BF16)
    grad_context = dot_nt(grad_att, dense_weight).astype(BF16)
    grad_context = swap_dp([grad_context[:, k * dp_width : (k + 1) * dp_width] for k in range(dp_count)])
    grad_held = spread(jnp.stack(grad_context).reshape(dp_count, rows, groups, pair_width))

    branch = sum_group(branch, group_bits)
    grad_dense = sum_dp(list(dot_tn(context_tok, grad_att).reshape(dp_count, dp_width, width)))
    grad_held, branch, grad_dense = lax.optimization_barrier((grad_held, branch, grad_dense))
    output = (middle + (branch + offsets[5])).astype(BF16)

    if whole_pairs:
        grad_qk, later = [], []
        for head in reversed(range(pair_heads)):
            grad_pair, *grad_value = attend_backward(
                slopes, held[head], held[0], grad_held, contexts[head], lses[head], head, pair_heads, later, block
            )
            grad_qk.append(grad_pair)
            later += grad_value
        grad_qk[:-1] = [collect(item) for item in grad_qk[:-1]]
        grad_qk[:-1], _ = lax.optimization_barrier((grad_qk[:-1], grad_qk[-1]))
        grad_qk[-1] = collect(grad_qk[-1])
    else:
        grad_qkv = split_backward(slopes, qkv, grad_held, *kept, pair_heads, rows)
        heads = [grad_qkv[:, start : start + head_dim] for start in range(0, 3 * pair_width, head_dim)]
        grad_qk = [
            jnp.concatenate([heads[head], heads[pair_heads + head]], axis=1)
            for head in reversed(range(pair_heads))
        ]
        grad_qk[-1] = jnp.concatenate([grad_qk[-1]] + heads[2 * pair_heads :], axis=1)
        grad_qk = [collect(item) for item in grad_qk]
    grad_parts = [item.reshape(dp_count * rows, -1) for item in grad_qk][::-1]
    later_cut = [sum_sequence(by_owner(dot_tn(normed_one, part).astype(BF16))) for part in grad_parts[1:]]
    grad_parts[0], grad_both, grad_dense = lax.optimization_barrier((grad_parts[0], grad_both, grad_dense))
    grad_dense = grad_dense.astype(BF16).reshape(ring, -1, width)
    grad_dense = lax.all_to_all(grad_dense, SEQ_AXES, split_axis=0, concat_axis=0, tiled=True)
    grad_w_dense = jnp.sum(grad_dense.astype(F32), axis=0)
    grad_one = sum(dot_nt(part, weight) for part, weight in zip(grad_parts, cut(qkv_weight), strict=True))
    grad_one = sum_bits_first(list(grad_one.reshape(dp_count, rows, width)))
    in_rows = dp_count * slice_rows * inner // width
    grad_w_out = grad_both[in_rows:].astype(F32)
    grad_in = to_places_dp(grad_both[:in_rows].reshape(dp_count, slice_rows, inner))
    grad_w_in = grad_in.transpose(1, 0, 2).reshape(slice_rows, -1).astype(F32)
    first_cut = split_ring(by_owner(dot_tn(normed_one, grad_parts[0]).astype(BF16)))
    first_cut = sum_bits(first_cut, bits_of("blk"), 1)
    first_cut, grad_one[0] = lax.optimization_barrier((first_cut, grad_one[0]))
    grad_normed_one = sum_bits_rest(grad_one)
    first_cut = sum_bits(first_cut, bits_of("sp"), 0)
    first_cut, grad_normed_one = lax.optimization_barrier((first_cut, grad_normed_one))
    grad_cut = [to_places_dp(item) for item in [first_cut] + later_cut]
    lead = (dp_count, slice_rows, groups)
    grad_cut = [item.reshape(lead + (-1, head_dim)) for item in grad_cut]
    grad_w_qkv = jnp.stack(
        [
            jnp.stack([item[..., 0, :] for item in grad_cut], axis=3),
            jnp.stack([item[..., 1, :] for item in grad_cut], axis=3),
            grad_cut[0][..., 2:, :],
        ]
    )
    grad_w_qkv = grad_w_qkv.transpose(2, 0, 1, 3, 4, 5).reshape(slice_rows, 3 * width).astype(F32)
    _, first_pull = jax.vjp(norm_rows, rows_in, gains_row[0], offsets[0])
    grad_rows_part, grad_gain_one, grad_shift_one = first_pull(grad_normed_one)
    grad_inputs = grad_middle + grad_rows_part

    part_sums = [jnp.sum(part.astype(F32), axis=0).reshape(groups, -1, head_dim) for part in grad_parts]
    query_sums = jnp.stack([item[:, 0] for item in part_sums], axis=1).reshape(-1)
    value_sums = part_sums[0][:, 2:].reshape(-1)

    def placed(part, size):
        return lax.dynamic_update_slice_in_dim(jnp.zeros(size, F32), part, dp_place * part.shape[0], 0)

    grad_vectors = jnp.stack(
        [
            grad_gain_one,
            grad_gain_two,
            grad_shift_one,
            placed(query_sums, width),
            placed(value_sums, width),
            jnp.sum(grad_att.astype(F32), axis=0),
            grad_shift_two,
            jnp.sum(grad_top, axis=0),
        ]
    )
    grad_in_part = placed(grad_in_offset, inner * dp_count)
    parts = jnp.concatenate(
        [
            grad_vectors.reshape(8, devices, -1).transpose(1, 0, 2).reshape(devices, -1),
            grad_in_part.reshape(devices, -1),
        ],
        axis=1,
    )
    parts = lax.all_to_all(parts, ALL, split_axis=0, concat_axis=0, tiled=True)
    summed = jnp.sum(parts, axis=0)
    vectors = summed[: gain_size + bias_size].reshape(8, -1)
    return (
        output,
        grad_inputs,
        grad_w_qkv,
        grad_w_dense,
        grad_w_in,
        grad_w_out,
        vectors[:2],
        vectors[2:],
        summed[gain_size + bias_size :],
    )


def solution(mesh):
    shape = mesh.devices.shape
    parted = jax.sharding.Mesh(mesh.devices.reshape((shape[0] // 2, 2) + shape[1:]), ALL)
    rows, columns, vector = P(ALL, None), P(None, ALL), P(ALL)
    in_specs = (rows, rows, rows, rows, rows, columns, columns, vector, P(), rows)
    out_specs = (rows, rows, rows, rows, rows, rows, columns, columns, vector)
    return jax.shard_map(
        on_device, mesh=parted, in_specs=in_specs, out_specs=out_specs, check_vma=False
    )
```

time: 498 us -> 477 us (0.958)
  waiting for transfers between devices: 233 us -> 180 us
  matrix products: 40.4 us -> 52.9 us
  other arithmetic: 30 us -> 41.9 us
  starting transfers between devices: 66.8 us -> 77 us
  blocking collectives: 17.9 us -> 9.45 us
  local copies, waits for them, and re-layouts: 53.6 us -> 59.3 us
    ppermute x48 -> x45, waiting for transfers between devices: 129 us -> 75.2 us  [exchange(): return lax.ppermute(value, axis, [(i, i ^ bit) for i in range(count)])]
    all_to_all x2 -> x3, waiting for transfers between devices: 79.2 us -> 58.3 us  [spread(): lax.all_to_all(sent, pair_axes, split_axis=0, concat_axis=0, tiled=True)]
    all_to_all x2 -> x3, waiting for transfers between devices: 0.01 us -> 14.6 us  [collect(): lax.all_to_all(held, pair_axes, split_axis=0, concat_axis=0, tiled=True)]
    all_to_all x2 -> x1, blocking collectives: 17.9 us -> 9.45 us  [my_columns(): return lax.all_to_all(pieces, DP, split_axis=0, concat_axis=0, tiled=True)]
    all_to_all x0 -> x2, starting transfers between devices: none -> 6.91 us  [the longest x1 3.51 us: on_device(): lax.all_to_all(grad_dense, SEQ_AXES, split_axis=0, concat_axis=0, tiled=T...]
    dot_general x4 -> x7, matrix products: 13.6 us -> 20.2 us  [dot_nt(): lax.dot_general(a, b, (((1,), (1,)), ((), ())), preferred_element_type=F32)]
    ppermute x48 -> x45, starting transfers between devices: 41.3 us -> 35.1 us  [exchange(): return lax.ppermute(value, axis, [(i, i ^ bit) for i in range(count)])]
    dot_general x4 -> x7, matrix products: 12.7 us -> 18.4 us  [dot_tn(): lax.dot_general(a, b, (((0,), (0,)), ((), ())), preferred_element_type=F32)]
  transfers between devices with their start and end apart: 56 -> 59, of which waited for: 24 -> 26; matrix products, arithmetic and copies ran while one was open for 21% -> 28% of each run, Pallas kernels for 6% -> 7%
where the time goes in v3:
time: 477 us; the launch traced here: 469 us
  waiting for transfers between devices  180 us (38%)
  starting transfers between devices  77 us (16%)
  local copies, waits for them, and re-layouts  59.3 us (12%)
  matrix products  52.9 us (11%)
  other arithmetic  41.9 us (9%)
  Pallas kernels  32.8 us (7%)
  between operations  15.3 us (3%)
  blocking collectives  9.45 us (2%)
    ppermute x45, waiting for transfers between devices, exchange(): return lax.ppermute(value, axis, [(i, i ^ bit) for i in range(count)])  75.2 us
    all_to_all x3, waiting for transfers between devices, spread(): lax.all_to_all(sent, pair_axes, split_axis=0, concat_axis=0, tiled=True)  58.3 us
    ppermute x45, starting transfers between devices, exchange(): return lax.ppermute(value, axis, [(i, i ^ bit) for i in range(count)])  35.1 us
    dot_general x7, matrix products, dot_nt(): lax.dot_general(a, b, (((1,), (1,)), ((), ())), preferred_element_type=F32)  20.2 us
    pallas_call x2, Pallas kernels, attend_backward(): pl.pallas_call(functools.partial(backward_kernel, head, head_dim, block),...  19.5 us
    dot_general x7, matrix products, dot_tn(): lax.dot_general(a, b, (((0,), (0,)), ((), ())), preferred_element_type=F32)  18.4 us
    all_gather x1, waiting for transfers between devices, on_device(): lax.all_gather(qkv_part, SEQ_AXES, axis=0, tiled=False)  16.7 us
    all_to_all x3, waiting for transfers between devices, collect(): lax.all_to_all(held, pair_axes, split_axis=0, concat_axis=0, tiled=True)  14.6 us
  transfers between devices with their start and end apart: 59, of which 26 were waited for; matrix products, arithmetic and copies ran while one was open for 28% of the time, Pallas kernels for 7%

profile of v3, /device:TPU:0, one launch (start us, length us, event | category | flops | bytes accessed | tf_op | source)
XLA Modules:
  0.0 468.8 jit_solution(2813482057715447385)
XLA Ops:
  9.7 9.4 %all_to_all.94 = bf16[4,32,768]{2,1,0:T(8,128)(2,1)} all-to-all(bf16[4,32,768]{2,1,0:T(8,128)(2,1)S(1)} %maximum_bitcast_fusion.1), channel_id=1, replica_groups=mesh['x'=2,'core'=2,'sp'=4,'blk'=2] {'x','core'}, dimensions={0} | all-to-all | bytes 393216 | tf_op jit(solution)/shard_map/all_to_all | solution.py:474
  22.0 6.5 %all-to-all-start.1 = ((bf16[32,2,192]{2,1,0:T(2,128)(2,1)}), bf16[32,2,192]{2,1,0:T(2,128)(2,1)S(1)}, u32[]{:S(2)}, u32[]{:S(2)}) async-start(bf16[32,2,192]{2,1,0:T(2,128)(2,1)} %reshape.501), calls=%async_computation.1 | async-start | bytes 65536 | tf_op jit(solution)/shard_map/all_to_all | solution.py:505
  30.3 5.4 %all-to-all-done.1 = bf16[32,2,192]{2,1,0:T(2,128)(2,1)S(1)} async-done(((bf16[32,2,192]{2,1,0:T(2,128)(2,1)}), bf16[32,2,192]{2,1,0:T(2,128)(2,1)S(1)}, u32[]{:S(2)}, u32[]{:S(2)}) %all-to-all-start.1) | async-done | bytes 24608 | tf_op jit(solution)/shard_map/all_to_all | solution.py:505
  47.7 16.7 %all-gather.7.cloned.1.call-done = bf16[32,32,768]{2,1,0:T(8,128)(2,1)} async-done(((bf16[4,32,768]{2,1,0:T(8,128)(2,1)}), bf16[32,32,768]{2,1,0:T(8,128)(2,1)}) %all-gather.7.cloned.1.call-update) | async-done | bytes 1572880 | tf_op jit(solution)/shard_map/all_gather | solution.py:526
  79.9 32.8 %all-to-all-done.3 = bf16[8,256,256]{2,1,0:T(8,128)(2,1)S(1)} async-done(((bf16[8,256,256]{2,1,0:T(8,128)(2,1)}), bf16[8,256,256]{2,1,0:T(8,128)(2,1)S(1)}, u32[]{:S(2)}, u32[]{:S(2)}) %all-to-all-start.3) | async-done | bytes 1048608 | tf_op jit(solution)/shard_map/all_to_all | solution.py:466
  117.5 6.2 %attend_forward.2 = (f32[64,2048]{1,0:T(8,128)S(1)}, f32[1,2048]{1,0:T(1,128)S(1)}) custom-call(f32[2]{0:T(128)S(1)} %dynamic_slice.80.slopes_ref, bf16[2048,256]{1,0:T(8,128)(2,1)S(1)} %bitcast.195, bf16[2048,256]{1,0:T(8,128)(2,1)S(1)} %bitcast.196), custom_call_target="tpu_custom_call" | custom-call | flops 8589934592 | bytes 2097152 | tf_op jit(solution)/shard_map/attend_forward/pallas_call | solution.py:311
  123.7 18.8 %all-to-all-done.2 = bf16[8,256,128]{2,1,0:T(8,128)(2,1)S(1)} async-done(((bf16[8,256,128]{2,1,0:T(8,128)(2,1)}), bf16[8,256,128]{2,1,0:T(8,128)(2,1)S(1)}, u32[]{:S(2)}, u32[]{:S(2)}) %all-to-all-start.2) | async-done | bytes 524320 | tf_op jit(solution)/shard_map/all_to_all | solution.py:466
  142.4 7.1 %attend_forward.3 = (f32[64,2048]{1,0:T(8,128)S(1)}, f32[1,2048]{1,0:T(1,128)S(1)}, bf16[2048,128]{1,0:T(8,128)(2,1)}) custom-call(f32[2]{0:T(128)S(1)} %dynamic_slice.80.slopes_ref, bf16[2048,128]{1,0:T(8,128)(2,1)S(1)} %bitcast.201, bf16[2048,256]{1,0:T(8,128)(2,1)S(1)} %bitcast.197, f32[64,2048]{1,0:T(8,128)S(1)} %get-tuple-element.39.refs_0_.ctx_t_ref), custom_call_target="tpu_custom_call" | custom-call | flops 8589934592 | bytes 2097152 | tf_op jit(solution)/shard_map/attend_forward/pallas_call | solution.py:311
  157.7 13.1 %collective-permute-done.7 = bf16[256,1024]{1,0:T(8,128)(2,1)} collective-permute-done((bf16[256,1024]{1,0:T(8,128)(2,1)}, bf16[256,1024]{1,0:T(8,128)(2,1)}, u32[]{:S(2)}, u32[]{:S(2)}) %collective-permute-start.7) | collective-permute-done | bytes 524320 | tf_op jit(solution)/shard_map/ppermute | solution.py:41
  195.5 7.4 %all-gather.11.cloned.1.call-done = bf16[32,32,1024]{2,1,0:T(8,128)(2,1)} async-done(((bf16[4,32,1024]{2,1,0:T(8,128)(2,1)}), bf16[32,32,1024]{2,1,0:T(8,128)(2,1)}) %all-gather.11.cloned.1.call-update) | async-done | bytes 2097168 | tf_op jit(solution)/shard_map/all_gather | solution.py:533
  214.1 6.3 %collective-permute-done.14 = bf16[256,1024]{1,0:T(8,128)(2,1)S(1)} collective-permute-done((bf16[256,1024]{1,0:T(8,128)(2,1)S(1)}, bf16[256,1024]{1,0:T(8,128)(2,1)S(1)}, u32[]{:S(2)}, u32[]{:S(2)}) %collective-permute-start.14) | collective-permute-done | bytes 524320 | tf_op jit(solution)/shard_map/ppermute | solution.py:41
  227.6 5.7 %convert_reduce_fusion.1 = (f32[1024]{0:T(1024)S(1)}, bf16[512,1024]{1,0:T(8,128)(2,1)S(1)}, f32[1024]{0:T(1024)S(1)}, bf16[512,1024]{1,0:T(8,128)(2,1)S(1)}) fusion(f32[512,1024]{1,0:T(8,128)S(1)} %fusion.88, f32[1024]{0:T(1024)S(1)} %bitcast.269, f32[512,1024]{1,0:T(8,128)S(1)} %fusion.86, f32[512,1024]{1,0:T(8,128)S(1)} %fusion.40, ...), kind=kOutput, calls=%fused_computation.32 | convolution fusion | flops 1097857024 | bytes 11546624 | tf_op jit(solution)/shard_map/dot_general | solution.py:32
  247.5 7.3 %collective-permute-done.17 = bf16[256,1024]{1,0:T(8,128)(2,1)S(1)} collective-permute-done((bf16[256,1024]{1,0:T(8,128)(2,1)S(1)}, bf16[256,1024]{1,0:T(8,128)(2,1)S(1)}, u32[]{:S(2)}, u32[]{:S(2)}) %collective-permute-start.17) | collective-permute-done | bytes 524320 | tf_op jit(solution)/shard_map/ppermute | solution.py:41
  292.6 8.9 %collective-permute-done.26 = bf16[256,1024]{1,0:T(8,128)(2,1)} collective-permute-done((bf16[256,1024]{1,0:T(8,128)(2,1)}, bf16[256,1024]{1,0:T(8,128)(2,1)}, u32[]{:S(2)}, u32[]{:S(2)}) %collective-permute-start.26) | collective-permute-done | bytes 524320 | tf_op jit(solution)/shard_map/ppermute | solution.py:41
  304.1 6.7 %all-to-all-done.6 = bf16[8,256,128]{2,1,0:T(8,128)(2,1)S(1)} async-done(((bf16[8,256,128]{2,1,0:T(8,128)(2,1)}), bf16[8,256,128]{2,1,0:T(8,128)(2,1)S(1)}, u32[]{:S(2)}, u32[]{:S(2)}) %all-to-all-start.6) | async-done | bytes 524320 | tf_op jit(solution)/shard_map/all_to_all | solution.py:466
  310.8 9.6 %attend_backward.2 = (bf16[2048,128]{1,0:T(8,128)(2,1)}, bf16[2048,128]{1,0:T(8,128)(2,1)S(1)}) custom-call(f32[2]{0:T(128)S(1)} %dynamic_slice.80.slopes_ref, bf16[2048,128]{1,0:T(8,128)(2,1)S(1)} %bitcast.202, bf16[2048,256]{1,0:T(8,128)(2,1)S(1)} %bitcast.198, bf16[2048,128]{1,0:T(8,128)(2,1)S(1)} %bitcast.203, ...), custom_call_target="tpu_custom_call" | custom-call | flops 10737418240 | bytes 4194304 | tf_op jit(solution)/shard_map/attend_backward/pallas_call | solution.py:339
  325.8 9.9 %attend_backward.3 = bf16[2048,256]{1,0:T(8,128)(2,1)} custom-call(f32[2]{0:T(128)S(1)} %dynamic_slice.80.slopes_ref, bf16[2048,256]{1,0:T(8,128)(2,1)S(1)} %bitcast.199, bf16[2048,256]{1,0:T(8,128)(2,1)S(1)} %bitcast.200, bf16[2048,128]{1,0:T(8,128)(2,1)S(1)} %bitcast.204, f32[64,2048]{1,0:T(8,128)S(1)} %get-tuple-element.39.refs_0_.ctx_t_ref, ...), custom_call_target="tpu_custom_call" | custom-call | flops 10737418240 | bytes 4194304 | tf_op jit(solution)/shard_map/attend_backward/pallas_call | solution.py:339
  335.7 10.7 %all-to-all-done.8 = bf16[8,256,128]{2,1,0:T(8,128)(2,1)S(1)} async-done(((bf16[8,256,128]{2,1,0:T(8,128)(2,1)}), bf16[8,256,128]{2,1,0:T(8,128)(2,1)S(1)}, u32[]{:S(2)}, u32[]{:S(2)}) %all-to-all-start.8) | async-done | bytes 524320 | tf_op jit(solution)/shard_map/all_to_all | solution.py:470
  353.1 4.6 all-to-all-start.7
  362.2 12.6 %collective-permute-done.37 = bf16[2,4,32,256]{3,1,2,0:T(4,128)(2,1)S(1)} collective-permute-done((bf16[2,4,32,256]{3,1,2,0:T(4,128)(2,1)S(1)}, bf16[2,4,32,256]{3,1,2,0:T(4,128)(2,1)S(1)}, u32[]{:S(2)}, u32[]{:S(2)}) %collective-permute-start.37) | collective-permute-done | bytes 131104 | tf_op jit(solution)/shard_map/ppermute | solution.py:41
  375.0 5.0 %collective-permute-start.38 = (bf16[1,4,32,256]{3,1,2,0:T(4,128)(2,1)S(1)}, bf16[1,4,32,256]{3,1,2,0:T(4,128)(2,1)S(1)}, u32[]{:S(2)}, u32[]{:S(2)}) collective-permute-start(bf16[1,4,32,256]{3,1,2,0:T(4,128)(2,1)S(1)} %constant_dynamic-slice_fusion.3), channel_id=1, source_target_pairs={{0,4},{2,6},{4,0},{6,2},{1,5},{3,7},{5,1},{7,3},{8,12},{10,14},{12... | collective-permute-start | bytes 196616 | tf_op jit(solution)/shard_map/ppermute | solution.py:41
  400.3 5.5 %fusion.85 = (bf16[1024,1024]{1,0:T(8,128)(2,1)S(1)}, f32[1024,1024]{1,0:T(8,128)}) fusion(f32[1024,1024]{1,0:T(8,128)} %fusion.44, bf16[1024,512]{1,0:T(8,128)(2,1)S(1)} %bitcast.208, bf16[1024,768]{1,0:T(8,128)(2,1)S(1)} %bitcast.214), kind=kOutput, calls=%fused_computation.219 | convolution fusion | flops 1075838976 | bytes 12582912 | tf_op jit(solution)/shard_map/dot_general | solution.py:32
  423.9 8.1 %collective-permute-done.29 = bf16[2,4,32,512]{3,1,2,0:T(4,128)(2,1)S(1)} collective-permute-done((bf16[2,4,32,512]{3,1,2,0:T(4,128)(2,1)S(1)}, bf16[2,4,32,512]{3,1,2,0:T(4,128)(2,1)S(1)}, u32[]{:S(2)}, u32[]{:S(2)}) %collective-permute-start.29) | collective-permute-done | bytes 262176 | tf_op jit(solution)/shard_map/ppermute | solution.py:41
  435.1 6.6 %collective-permute-done.30 = bf16[1,4,32,512]{3,1,2,0:T(4,128)(2,1)S(1)} collective-permute-done((bf16[1,4,32,512]{3,1,2,0:T(4,128)(2,1)S(1)}, bf16[1,4,32,512]{3,1,2,0:T(4,128)(2,1)S(1)}, u32[]{:S(2)}, u32[]{:S(2)}) %collective-permute-start.30) | collective-permute-done | bytes 131104 | tf_op jit(solution)/shard_map/ppermute | solution.py:41
  (404 shorter events, 222.5 us)
Async XLA Ops:
  7.2 57.3 %all-gather.7.cloned.1.call-start = ((), (), s32[]{:S(2)}) async-start(), calls=%async_computation.13 | async-start | bytes 1769472 | tf_op jit(solution)/shard_map/all_gather | solution.py:526
  19.5 20.3 %collective-permute-start.1 = (bf16[256,1024]{1,0:T(8,128)(2,1)S(1)}, bf16[256,1024]{1,0:T(8,128)(2,1)S(1)}, u32[]{:S(2)}, u32[]{:S(2)}) collective-permute-start(bf16[256,1024]{1,0:T(8,128)(2,1)S(1)} %copy-done.5), channel_id=1, source_target_pairs={{0,16},{8,24},{16,0},{24,8},{1,17},{9,25},{17,1},{25,9},{2,18},{10... | collective-permute-start | bytes 1572872 | tf_op jit(solution)/shard_map/ppermute | solution.py:41
  19.9 20.9 %collective-permute-start = (bf16[256,1024]{1,0:T(8,128)(2,1)S(1)}, bf16[256,1024]{1,0:T(8,128)(2,1)S(1)}, u32[]{:S(2)}, u32[]{:S(2)}) collective-permute-start(bf16[256,1024]{1,0:T(8,128)(2,1)S(1)} %copy-done.5), channel_id=1, source_target_pairs={{0,8},{8,0},{16,24},{24,16},{1,9},{9,1},{17,25},{25,17},{2,10},{10... | collective-permute-start | bytes 1572872 | tf_op jit(solution)/shard_map/ppermute | solution.py:41
  28.5 125.3 %all-gather.9.cloned.1.call-start = ((), (), s32[]{:S(2)}) async-start(), calls=%async_computation.14 | async-start | bytes 2949120 | tf_op jit(solution)/shard_map/all_gather | solution.py:528
  35.7 35.5 %all-to-all-start.5 = ((bf16[4,32,1024]{2,1,0:T(8,128)(2,1)}), bf16[4,32,1024]{2,1,0:T(8,128)(2,1)S(1)}, u32[]{:S(2)}, u32[]{:S(2)}) async-start(bf16[4,32,1024]{2,1,0:T(8,128)(2,1)} %copy.105), calls=%async_computation.5 | async-start | bytes 524288 | tf_op jit(solution)/shard_map/all_to_all | solution.py:474
  71.2 41.5 %all-to-all-start.3 = ((bf16[8,256,256]{2,1,0:T(8,128)(2,1)}), bf16[8,256,256]{2,1,0:T(8,128)(2,1)S(1)}, u32[]{:S(2)}, u32[]{:S(2)}) async-start(bf16[8,256,256]{2,1,0:T(8,128)(2,1)} %bitcast.217), calls=%async_computation.3 | async-start | bytes 2097152 | tf_op jit(solution)/shard_map/all_to_all | solution.py:466
  112.7 29.7 %all-to-all-start.2 = ((bf16[8,256,128]{2,1,0:T(8,128)(2,1)}), bf16[8,256,128]{2,1,0:T(8,128)(2,1)S(1)}, u32[]{:S(2)}, u32[]{:S(2)}) async-start(bf16[8,256,128]{2,1,0:T(8,128)(2,1)} %bitcast.15), calls=%async_computation.2 | async-start | bytes 1048576 | tf_op jit(solution)/shard_map/all_to_all | solution.py:466
  116.7 86.1 %all-gather.11.cloned.1.call-start = ((), (), s32[]{:S(2)}) async-start(), calls=%async_computation.15 | async-start | bytes 2359296 | tf_op jit(solution)/shard_map/all_gather | solution.py:533
  149.5 27.1 %all-to-all-start.4 = ((bf16[8,256,128]{2,1,0:T(8,128)(2,1)}), bf16[8,256,128]{2,1,0:T(8,128)(2,1)}, u32[]{:S(2)}, u32[]{:S(2)}) async-start(bf16[8,256,128]{2,1,0:T(8,128)(2,1)} %bitcast.22), calls=%async_computation.4 | async-start | bytes 1048576 | tf_op jit(solution)/shard_map/all_to_all | solution.py:470
  153.7 237.7 %reduce-scatter.2.cloned.1.call-start = ((), (), s32[]{:S(2)}) async-start(), calls=%async_computation.12 | async-start | bytes 4718592 | tf_op jit(solution)/shard_map/reduce_scatter | solution.py:587
  157.2 24.9 %collective-permute-start.12 = (bf16[256,1024]{1,0:T(8,128)(2,1)}, bf16[256,1024]{1,0:T(8,128)(2,1)}, u32[]{:S(2)}, u32[]{:S(2)}) collective-permute-start(bf16[256,1024]{1,0:T(8,128)(2,1)} %param.19), channel_id=1, source_target_pairs={{0,16},{16,0},{1,17},{17,1},{2,18},{18,2},{3,19},{19,3},{4,20},{20... | collective-permute-start | bytes 1572872 | tf_op jit(solution)/shard_map/ppermute | solution.py:41
  157.7 26.9 %collective-permute-start.6 = (bf16[256,1024]{1,0:T(8,128)(2,1)}, bf16[256,1024]{1,0:T(8,128)(2,1)}, u32[]{:S(2)}, u32[]{:S(2)}) collective-permute-start(bf16[256,1024]{1,0:T(8,128)(2,1)} %bitcast.31), channel_id=1, source_target_pairs={{0,8},{8,0},{16,24},{24,16},{1,9},{9,1},{17,25},{25,17},{2,10},{10... | collective-permute-start | bytes 1572872 | tf_op jit(solution)/shard_map/ppermute | solution.py:41
  214.1 75.7 %collective-permute-start.21 = (bf16[256,1024]{1,0:T(8,128)(2,1)}, bf16[256,1024]{1,0:T(8,128)(2,1)}, u32[]{:S(2)}, u32[]{:S(2)}) collective-permute-start(bf16[256,1024]{1,0:T(8,128)(2,1)} %unstack.123), channel_id=1, source_target_pairs={{0,8},{8,0},{1,9},{9,1},{2,10},{10,2},{3,11},{11,3},{4,12},{12,4},... | collective-permute-start | bytes 1572872 | tf_op jit(solution)/shard_map/ppermute | solution.py:41
  227.3 42.1 %collective-permute-start.22 = (bf16[256,1024]{1,0:T(8,128)(2,1)}, bf16[256,1024]{1,0:T(8,128)(2,1)}, u32[]{:S(2)}, u32[]{:S(2)}) collective-permute-start(bf16[256,1024]{1,0:T(8,128)(2,1)} %unstack.122), channel_id=1, source_target_pairs={{0,8},{8,0},{1,9},{9,1},{2,10},{10,2},{3,11},{11,3},{4,12},{12,4},... | collective-permute-start | bytes 1572872 | tf_op jit(solution)/shard_map/ppermute | solution.py:41
  264.2 20.6 %collective-permute-start.25 = (bf16[256,1024]{1,0:T(8,128)(2,1)}, bf16[256,1024]{1,0:T(8,128)(2,1)}, u32[]{:S(2)}, u32[]{:S(2)}) collective-permute-start(bf16[256,1024]{1,0:T(8,128)(2,1)} %get-tuple-element.90), channel_id=1, source_target_pairs={{0,8},{8,0},{16,24},{24,16},{1,9},{9,1},{17,25},{25,17},{2,10},{10... | collective-permute-start | bytes 1572872 | tf_op jit(solution)/shard_map/ppermute | solution.py:41
  273.0 16.9 %collective-permute-start.23 = (bf16[256,1024]{1,0:T(8,128)(2,1)}, bf16[256,1024]{1,0:T(8,128)(2,1)}, u32[]{:S(2)}, u32[]{:S(2)}) collective-permute-start(bf16[256,1024]{1,0:T(8,128)(2,1)} %fusion.32), channel_id=1, source_target_pairs={{0,16},{16,0},{1,17},{17,1},{2,18},{18,2},{3,19},{19,3},{4,20},{20... | collective-permute-start | bytes 1572872 | tf_op jit(solution)/shard_map/ppermute | solution.py:41
  276.2 16.4 %collective-permute-start.24 = (bf16[256,1024]{1,0:T(8,128)(2,1)}, bf16[256,1024]{1,0:T(8,128)(2,1)}, u32[]{:S(2)}, u32[]{:S(2)}) collective-permute-start(bf16[256,1024]{1,0:T(8,128)(2,1)} %get-tuple-element.89), channel_id=1, source_target_pairs={{0,8},{8,0},{16,24},{24,16},{1,9},{9,1},{17,25},{25,17},{2,10},{10... | collective-permute-start | bytes 1572872 | tf_op jit(solution)/shard_map/ppermute | solution.py:41
  280.4 30.4 %all-to-all-start.6 = ((bf16[8,256,128]{2,1,0:T(8,128)(2,1)}), bf16[8,256,128]{2,1,0:T(8,128)(2,1)S(1)}, u32[]{:S(2)}, u32[]{:S(2)}) async-start(bf16[8,256,128]{2,1,0:T(8,128)(2,1)} %bitcast.234), calls=%async_computation.6 | async-start | bytes 1048576 | tf_op jit(solution)/shard_map/all_to_all | solution.py:466
  321.2 25.2 %all-to-all-start.8 = ((bf16[8,256,128]{2,1,0:T(8,128)(2,1)}), bf16[8,256,128]{2,1,0:T(8,128)(2,1)S(1)}, u32[]{:S(2)}, u32[]{:S(2)}) async-start(bf16[8,256,128]{2,1,0:T(8,128)(2,1)} %bitcast.57), calls=%async_computation.9 | async-start | bytes 1048576 | tf_op jit(solution)/shard_map/all_to_all | solution.py:470
  353.1 35.7 %all-to-all-start.7 = ((bf16[8,256,256]{2,1,0:T(8,128)(2,1)}), bf16[8,256,256]{2,1,0:T(8,128)(2,1)}, u32[]{:S(2)}, u32[]{:S(2)}) async-start(bf16[8,256,256]{2,1,0:T(8,128)(2,1)} %bitcast.46), calls=%async_computation.7 | async-start | bytes 2097152 | tf_op jit(solution)/shard_map/all_to_all | solution.py:470
  358.0 16.9 %collective-permute-start.37 = (bf16[2,4,32,256]{3,1,2,0:T(4,128)(2,1)S(1)}, bf16[2,4,32,256]{3,1,2,0:T(4,128)(2,1)S(1)}, u32[]{:S(2)}, u32[]{:S(2)}) collective-permute-start(bf16[2,4,32,256]{3,1,2,0:T(4,128)(2,1)S(1)} %bitcast.263), channel_id=1, source_target_pairs={{0,2},{2,0},{4,6},{6,4},{1,3},{3,1},{5,7},{7,5},{8,10},{10,8},{12,... | collective-permute-start | bytes 393224 | tf_op jit(solution)/shard_map/ppermute | solution.py:41
  398.2 20.1 %collective-permute-start.27 = (bf16[4,1,4,32,512]{4,3,0,2,1:T(8,128)(2,1)}, bf16[4,1,4,32,512]{4,3,0,2,1:T(8,128)(2,1)}, u32[]{:S(2)}, u32[]{:S(2)}) collective-permute-start(bf16[4,1,4,32,512]{4,3,0,2,1:T(8,128)(2,1)} %dynamic-slice_bitcast_fusion), channel_id=1, source_target_pairs={{0,1},{1,0},{2,3},{3,2},{4,5},{5,4},{6,7},{7,6},{8,9},{9,8},{10,11... | collective-permute-start | bytes 1572872 | tf_op jit(solution)/shard_map/ppermute | solution.py:41
  411.4 23.0 %all-to-all-start.9 = ((bf16[8,32,1024]{2,1,0:T(8,128)(2,1)}), bf16[8,32,1024]{2,1,0:T(8,128)(2,1)S(1)}, u32[]{:S(2)}, u32[]{:S(2)}) async-start(bf16[8,32,1024]{2,1,0:T(8,128)(2,1)} %bitcast.84), calls=%async_computation.10 | async-start | bytes 1048576 | tf_op jit(solution)/shard_map/all_to_all | solution.py:625
  422.8 19.0 %collective-permute-start.32 = (bf16[256,1024]{1,0:T(8,128)(2,1)S(1)}, bf16[256,1024]{1,0:T(8,128)(2,1)}, u32[]{:S(2)}, u32[]{:S(2)}) collective-permute-start(bf16[256,1024]{1,0:T(8,128)(2,1)S(1)} %get-tuple-element.85), channel_id=1, source_target_pairs={{0,16},{8,24},{16,0},{24,8},{1,17},{9,25},{17,1},{25,9},{2,18},{10... | collective-permute-start | bytes 1572872 | tf_op jit(solution)/shard_map/ppermute | solution.py:41
  (80 other events, 609.6 us)
Sparse Core Ops, SparseCore 0:
  19.3 45.0 all-gather.6
  67.2 76.4 all-gather.8
  146.4 56.3 all-gather.10
  256.2 101.2 reduce-scatter.1

commit v4 on v3

--- a/solution.py
+++ b/solution.py
@@ -114,7 +114,7 @@
     return held, level
 
 
-def sum_bits(held, bits, level):
+def sum_bits(held, bits, level, last=True):
     for axis, bit in bits:
         shape = held.shape
         halves = held.reshape(shape[:level] + (shape[level] // 2, 2) + shape[level + 1 :])
@@ -123,7 +123,7 @@
         kept = lax.dynamic_index_in_dim(halves, side, level + 1, keepdims=False)
         arrived = exchange(sent.astype(BF16), bit, axis)
         held = (kept.astype(F32) + arrived.astype(F32)).astype(BF16)
-    return jnp.squeeze(held, level)
+    return jnp.squeeze(held, level) if last else held
 
 
 def sum_sequence(parts):
@@ -566,7 +566,7 @@
     grad_top = upstream.astype(F32)
     grad_in_offset, grad_out, grad_in = 0.0, 0.0, 0.0
     pieces = gather_group(normed_two, group_bits)
-    branch, grad_two = [None] * len(pieces), [None] * len(pieces)
+    branch, grad_two, hiddens = [None] * len(pieces), [None] * len(pieces), []
     for place in range(x_count):
         normed = jnp.concatenate(pieces[place::x_count], axis=0)
         grads = jnp.concatenate(grad_pieces[place::x_count], axis=0)
@@ -575,7 +575,7 @@
         hidden = hidden.astype(BF16)
         grad_pre = gelu_pull(dot_nt(grads, out_weight))[0].astype(BF16)
         grad_two[place::x_count] = list(dot_nt(grad_pre, in_weight).reshape(2, rows, width))
-        branch[place::x_count] = list(dot_nn(hidden, out_weight).reshape(2, rows, width))
+        hiddens.append(hidden)
         grad_in_offset += jnp.sum(grad_pre.astype(F32), axis=0)
         grad_out += dot_tn(hidden, grads)
         grad_in += dot_tn(normed, grad_pre)
@@ -593,10 +593,11 @@
     grad_context = swap_dp([grad_context[:, k * dp_width : (k + 1) * dp_width] for k in range(dp_count)])
     grad_held = spread(jnp.stack(grad_context).reshape(dp_count, rows, groups, pair_width))
 
-    branch = sum_group(branch, group_bits)
-    grad_dense = sum_dp(list(dot_tn(context_tok, grad_att).reshape(dp_count, dp_width, width)))
-    grad_held, branch, grad_dense = lax.optimization_barrier((grad_held, branch, grad_dense))
-    output = (middle + (branch + offsets[5])).astype(BF16)
+    grad_held, hiddens, grad_late = lax.optimization_barrier((grad_held, hiddens, grad_att))
+    for place, hidden in enumerate(hiddens):
+        branch[place::x_count] = list(dot_nn(hidden, out_weight).reshape(2, rows, width))
+    output = (middle + (sum_group(branch, group_bits) + offsets[5])).astype(BF16)
+    grad_dense = sum_dp(list(dot_tn(context_tok, grad_late).reshape(dp_count, dp_width, width)))
 
     if whole_pairs:
         grad_qk, later = [], []
@@ -619,24 +620,27 @@
         grad_qk[-1] = jnp.concatenate([grad_qk[-1]] + heads[2 * pair_heads :], axis=1)
         grad_qk = [collect(item) for item in grad_qk]
     grad_parts = [item.reshape(dp_count * rows, -1) for item in grad_qk][::-1]
-    later_cut = [sum_sequence(by_owner(dot_tn(normed_one, part).astype(BF16))) for part in grad_parts[1:]]
-    grad_parts[0], grad_both, grad_dense = lax.optimization_barrier((grad_parts[0], grad_both, grad_dense))
+    later_sent = [by_owner(dot_tn(normed_one, part).astype(BF16)) for part in grad_parts[1:]]
+    grad_parts[0], later_sent, grad_both, grad_dense = lax.optimization_barrier(
+        (grad_parts[0], later_sent, grad_both, grad_dense)
+    )
     grad_dense = grad_dense.astype(BF16).reshape(ring, -1, width)
     grad_dense = lax.all_to_all(grad_dense, SEQ_AXES, split_axis=0, concat_axis=0, tiled=True)
-    grad_w_dense = jnp.sum(grad_dense.astype(F32), axis=0)
-    grad_one = sum(dot_nt(part, weight) for part, weight in zip(grad_parts, cut(qkv_weight), strict=True))
-    grad_one = sum_bits_first(list(grad_one.reshape(dp_count, rows, width)))
     in_rows = dp_count * slice_rows * inner // width
     grad_w_out = grad_both[in_rows:].astype(F32)
     grad_in = to_places_dp(grad_both[:in_rows].reshape(dp_count, slice_rows, inner))
     grad_w_in = grad_in.transpose(1, 0, 2).reshape(slice_rows, -1).astype(F32)
-    first_cut = split_ring(by_owner(dot_tn(normed_one, grad_parts[0]).astype(BF16)))
-    first_cut = sum_bits(first_cut, bits_of("blk"), 1)
-    first_cut, grad_one[0] = lax.optimization_barrier((first_cut, grad_one[0]))
-    grad_normed_one = sum_bits_rest(grad_one)
-    first_cut = sum_bits(first_cut, bits_of("sp"), 0)
-    first_cut, grad_normed_one = lax.optimization_barrier((first_cut, grad_normed_one))
-    grad_cut = [to_places_dp(item) for item in [first_cut] + later_cut]
+    grad_one = sum(dot_nt(part, weight) for part, weight in zip(grad_parts, cut(qkv_weight), strict=True))
+    grad_one = list(grad_one.reshape(dp_count, rows, width))
+    first_part, grad_one = lax.optimization_barrier((grad_parts[0], grad_one))
+    grad_sent = [by_owner(dot_tn(normed_one, first_part).astype(BF16))] + later_sent
+    grad_sent = jnp.concatenate(grad_sent, axis=-1)
+    grad_sent, grad_dense = lax.optimization_barrier((grad_sent, grad_dense))
+    grad_cut = lax.all_to_all(grad_sent, SEQ_AXES, split_axis=0, concat_axis=0, tiled=True)
+    grad_normed_one = sum_dp(grad_one)
+    grad_cut, grad_normed_one = lax.optimization_barrier((grad_cut, grad_normed_one))
+    grad_w_dense = jnp.sum(grad_dense.astype(F32), axis=0)
+    grad_cut = cut(to_places_dp(jnp.sum(grad_cut.astype(F32), axis=0).astype(BF16)))
     lead = (dp_count, slice_rows, groups)
     grad_cut = [item.reshape(lead + (-1, head_dim)) for item in grad_cut]
     grad_w_qkv = jnp.stack(

time: 477 us -> 468 us (0.981)
  starting transfers between devices: 77 us -> 64 us
  waiting for transfers between devices: 180 us -> 193 us
  local copies, waits for them, and re-layouts: 59.3 us -> 53.9 us
    all_to_all x3, waiting for transfers between devices: 58.3 us -> 78.8 us  [spread(): lax.all_to_all(sent, pair_axes, split_axis=0, concat_axis=0, tiled=True)]
    ppermute x45 -> x36, waiting for transfers between devices: 75.2 us -> 54.8 us  [exchange(): return lax.ppermute(value, axis, [(i, i ^ bit) for i in range(count)])]
    ppermute x45 -> x36, starting transfers between devices: 35.1 us -> 18.6 us  [exchange(): return lax.ppermute(value, axis, [(i, i ^ bit) for i in range(count)])]
    all_to_all x0 -> x1, waiting for transfers between devices: none -> 10.5 us  [on_device(): lax.all_to_all(grad_sent, SEQ_AXES, split_axis=0, concat_axis=0, tiled=True)]
    all_gather x1, waiting for transfers between devices: 7.41 us -> 0.93 us  [on_device(): in_weight = all_rows(lax.all_gather(in_part, SEQ_AXES, axis=0, tiled=False))]
    unnamed x96 -> x90, local copies, waits for them, and re-layouts: 12.7 us -> 12.1 us
  transfers between devices with their start and end apart: 59 -> 51, of which waited for: 26 -> 23; matrix products, arithmetic and copies ran while one was open for 28% -> 25% of each run, Pallas kernels for 7% -> 7%
where the time goes in v4:
time: 468 us; the launch traced here: 459 us
  waiting for transfers between devices  193 us (41%)
  starting transfers between devices  64 us (14%)
  local copies, waits for them, and re-layouts  53.9 us (12%)
  matrix products  51.6 us (11%)
  other arithmetic  39.4 us (8%)
  Pallas kernels  32.9 us (7%)
  between operations  15.3 us (3%)
  blocking collectives  9.45 us (2%)
    all_to_all x3, waiting for transfers between devices, spread(): lax.all_to_all(sent, pair_axes, split_axis=0, concat_axis=0, tiled=True)  78.8 us
    ppermute x36, waiting for transfers between devices, exchange(): return lax.ppermute(value, axis, [(i, i ^ bit) for i in range(count)])  54.8 us
    dot_general x7, matrix products, dot_nt(): lax.dot_general(a, b, (((1,), (1,)), ((), ())), preferred_element_type=F32)  19.9 us
    pallas_call x2, Pallas kernels, attend_backward(): pl.pallas_call(functools.partial(backward_kernel, head, head_dim, block),...  19.5 us
    ppermute x36, starting transfers between devices, exchange(): return lax.ppermute(value, axis, [(i, i ^ bit) for i in range(count)])  18.6 us
    all_to_all x3, waiting for transfers between devices, collect(): lax.all_to_all(held, pair_axes, split_axis=0, concat_axis=0, tiled=True)  17.9 us
    dot_general x7, matrix products, dot_nn(): lax.dot_general(a, b, (((1,), (0,)), ((), ())), preferred_element_type=F32)  17.8 us
    all_gather x1, waiting for transfers between devices, on_device(): lax.all_gather(qkv_part, SEQ_AXES, axis=0, tiled=False)  16.4 us
  transfers between devices with their start and end apart: 51, of which 23 were waited for; matrix products, arithmetic and copies ran while one was open for 25% of the time, Pallas kernels for 7%

profile of v4, /device:TPU:0, one launch (start us, length us, event | category | flops | bytes accessed | tf_op | source)
XLA Modules:
  0.0 459.4 jit_solution(7183106278275388543)
XLA Ops:
  9.7 9.4 %all_to_all.99 = bf16[4,32,768]{2,1,0:T(8,128)(2,1)} all-to-all(bf16[4,32,768]{2,1,0:T(8,128)(2,1)S(1)} %maximum_bitcast_fusion.1), channel_id=1, replica_groups=mesh['x'=2,'core'=2,'sp'=4,'blk'=2] {'x','core'}, dimensions={0} | all-to-all | bytes 393216 | tf_op jit(solution)/shard_map/all_to_all | solution.py:474
  22.0 6.5 %all-to-all-start.1 = ((bf16[32,2,192]{2,1,0:T(2,128)(2,1)}), bf16[32,2,192]{2,1,0:T(2,128)(2,1)S(1)}, u32[]{:S(2)}, u32[]{:S(2)}) async-start(bf16[32,2,192]{2,1,0:T(2,128)(2,1)} %reshape.444), calls=%async_computation.1 | async-start | bytes 65536 | tf_op jit(solution)/shard_map/all_to_all | solution.py:505
  30.3 5.4 %all-to-all-done.1 = bf16[32,2,192]{2,1,0:T(2,128)(2,1)S(1)} async-done(((bf16[32,2,192]{2,1,0:T(2,128)(2,1)}), bf16[32,2,192]{2,1,0:T(2,128)(2,1)S(1)}, u32[]{:S(2)}, u32[]{:S(2)}) %all-to-all-start.1) | async-done | bytes 24608 | tf_op jit(solution)/shard_map/all_to_all | solution.py:505
  48.1 16.4 %all-gather.7.cloned.1.call-done = bf16[32,32,768]{2,1,0:T(8,128)(2,1)} async-done(((bf16[4,32,768]{2,1,0:T(8,128)(2,1)}), bf16[32,32,768]{2,1,0:T(8,128)(2,1)}) %all-gather.7.cloned.1.call-update) | async-done | bytes 1572880 | tf_op jit(solution)/shard_map/all_gather | solution.py:526
  79.9 32.8 %all-to-all-done.3 = bf16[8,256,256]{2,1,0:T(8,128)(2,1)S(1)} async-done(((bf16[8,256,256]{2,1,0:T(8,128)(2,1)}), bf16[8,256,256]{2,1,0:T(8,128)(2,1)S(1)}, u32[]{:S(2)}, u32[]{:S(2)}) %all-to-all-start.3) | async-done | bytes 1048608 | tf_op jit(solution)/shard_map/all_to_all | solution.py:466
  117.5 6.2 %attend_forward.2 = (f32[64,2048]{1,0:T(8,128)S(1)}, f32[1,2048]{1,0:T(1,128)S(1)}) custom-call(f32[2]{0:T(128)S(1)} %dynamic_slice.30.slopes_ref, bf16[2048,256]{1,0:T(8,128)(2,1)S(1)} %bitcast.150, bf16[2048,256]{1,0:T(8,128)(2,1)S(1)} %bitcast.151), custom_call_target="tpu_custom_call" | custom-call | flops 8589934592 | bytes 2097152 | tf_op jit(solution)/shard_map/attend_forward/pallas_call | solution.py:311
  123.7 18.7 %all-to-all-done.2 = bf16[8,256,128]{2,1,0:T(8,128)(2,1)S(1)} async-done(((bf16[8,256,128]{2,1,0:T(8,128)(2,1)}), bf16[8,256,128]{2,1,0:T(8,128)(2,1)S(1)}, u32[]{:S(2)}, u32[]{:S(2)}) %all-to-all-start.2) | async-done | bytes 524320 | tf_op jit(solution)/shard_map/all_to_all | solution.py:466
  142.4 7.1 %attend_forward.3 = (f32[64,2048]{1,0:T(8,128)S(1)}, f32[1,2048]{1,0:T(1,128)S(1)}, bf16[2048,128]{1,0:T(8,128)(2,1)}) custom-call(f32[2]{0:T(128)S(1)} %dynamic_slice.30.slopes_ref, bf16[2048,128]{1,0:T(8,128)(2,1)S(1)} %bitcast.156, bf16[2048,256]{1,0:T(8,128)(2,1)S(1)} %bitcast.152, f32[64,2048]{1,0:T(8,128)S(1)} %get-tuple-element.46.refs_0_.ctx_t_ref), custom_call_target="tpu_custom_call" | custom-call | flops 8589934592 | bytes 2097152 | tf_op jit(solution)/shard_map/attend_forward/pallas_call | solution.py:311
  149.5 4.2 all-to-all-start.4
  157.9 13.1 %collective-permute-done.7 = bf16[256,1024]{1,0:T(8,128)(2,1)} collective-permute-done((bf16[256,1024]{1,0:T(8,128)(2,1)}, bf16[256,1024]{1,0:T(8,128)(2,1)}, u32[]{:S(2)}, u32[]{:S(2)}) %collective-permute-start.7) | collective-permute-done | bytes 524320 | tf_op jit(solution)/shard_map/ppermute | solution.py:41
  171.0 5.7 %all-to-all-done.4 = bf16[8,256,128]{2,1,0:T(8,128)(2,1)} async-done(((bf16[8,256,128]{2,1,0:T(8,128)(2,1)}), bf16[8,256,128]{2,1,0:T(8,128)(2,1)}, u32[]{:S(2)}, u32[]{:S(2)}) %all-to-all-start.4) | async-done | bytes 524320 | tf_op jit(solution)/shard_map/all_to_all | solution.py:470
  214.6 6.0 %convert_reduce_fusion.1 = (f32[1024]{0:T(1024)S(1)}, bf16[512,1024]{1,0:T(8,128)(2,1)S(1)}, bf16[512,1024]{1,0:T(8,128)(2,1)S(1)}, bf16[512,1024]{1,0:T(8,128)(...) fusion(f32[512,1024]{1,0:T(8,128)S(1)} %fusion.80, f32[1024]{0:T(1024)S(1)} %bitcast.217, ...), kind=kOutput, calls=%fused_computation.32 | convolution fusion | flops 1099954176 | bytes 13643776 | tf_op jit(solution)/shard_map/dot_general | solution.py:32
  236.2 7.8 %collective-permute-done.17 = bf16[256,1024]{1,0:T(8,128)(2,1)S(1)} collective-permute-done((bf16[256,1024]{1,0:T(8,128)(2,1)S(1)}, bf16[256,1024]{1,0:T(8,128)(2,1)S(1)}, u32[]{:S(2)}, u32[]{:S(2)}) %collective-permute-start.17) | collective-permute-done | bytes 524320 | tf_op jit(solution)/shard_map/ppermute | solution.py:41
  254.3 4.6 collective-permute-done.19
  269.0 27.3 %all-to-all-done.6 = bf16[8,256,128]{2,1,0:T(8,128)(2,1)S(1)} async-done(((bf16[8,256,128]{2,1,0:T(8,128)(2,1)}), bf16[8,256,128]{2,1,0:T(8,128)(2,1)S(1)}, u32[]{:S(2)}, u32[]{:S(2)}) %all-to-all-start.6) | async-done | bytes 524320 | tf_op jit(solution)/shard_map/all_to_all | solution.py:466
  301.8 9.6 %attend_backward.2 = (bf16[2048,128]{1,0:T(8,128)(2,1)}, bf16[2048,128]{1,0:T(8,128)(2,1)S(1)}) custom-call(f32[2]{0:T(128)S(1)} %dynamic_slice.30.slopes_ref, bf16[2048,128]{1,0:T(8,128)(2,1)S(1)} %bitcast.157, bf16[2048,256]{1,0:T(8,128)(2,1)S(1)} %bitcast.153, bf16[2048,128]{1,0:T(8,128)(2,1)S(1)} %bitcast.158, ...), custom_call_target="tpu_custom_call" | custom-call | flops 10737418240 | bytes 4194304 | tf_op jit(solution)/shard_map/attend_backward/pallas_call | solution.py:339
  321.2 9.9 %attend_backward.3 = bf16[2048,256]{1,0:T(8,128)(2,1)} custom-call(f32[2]{0:T(128)S(1)} %dynamic_slice.30.slopes_ref, bf16[2048,256]{1,0:T(8,128)(2,1)S(1)} %bitcast.154, bf16[2048,256]{1,0:T(8,128)(2,1)S(1)} %bitcast.155, bf16[2048,128]{1,0:T(8,128)(2,1)S(1)} %bitcast.159, f32[64,2048]{1,0:T(8,128)S(1)} %get-tuple-element.46.refs_0_.ctx_t_ref, ...), custom_call_target="tpu_custom_call" | custom-call | flops 10737418240 | bytes 4194304 | tf_op jit(solution)/shard_map/attend_backward/pallas_call | solution.py:339
  331.1 6.8 %all-to-all-done.8 = bf16[8,256,128]{2,1,0:T(8,128)(2,1)S(1)} async-done(((bf16[8,256,128]{2,1,0:T(8,128)(2,1)}), bf16[8,256,128]{2,1,0:T(8,128)(2,1)S(1)}, u32[]{:S(2)}, u32[]{:S(2)}) %all-to-all-start.8) | async-done | bytes 524320 | tf_op jit(solution)/shard_map/all_to_all | solution.py:470
  357.5 4.8 %collective-permute-done.26 = bf16[256,1024]{1,0:T(8,128)(2,1)S(1)} collective-permute-done((bf16[256,1024]{1,0:T(8,128)(2,1)S(1)}, bf16[256,1024]{1,0:T(8,128)(2,1)S(1)}, u32[]{:S(2)}, u32[]{:S(2)}) %collective-permute-start.26) | collective-permute-done | bytes 524320 | tf_op jit(solution)/shard_map/ppermute | solution.py:41
  364.4 5.4 %all-to-all-done.7 = bf16[8,256,256]{2,1,0:T(8,128)(2,1)S(1)} async-done(((bf16[8,256,256]{2,1,0:T(8,128)(2,1)}), bf16[8,256,256]{2,1,0:T(8,128)(2,1)S(1)}, u32[]{:S(2)}, u32[]{:S(2)}) %all-to-all-start.7) | async-done | bytes 1048608 | tf_op jit(solution)/shard_map/all_to_all | solution.py:470
  389.4 4.5 all-to-all-start.10
  406.9 10.8 %collective-permute-done.35 = bf16[1,32,1024]{2,1,0:T(8,128)(2,1)S(1)} collective-permute-done((bf16[1,32,1024]{2,1,0:T(8,128)(2,1)S(1)}, bf16[1,32,1024]{2,1,0:T(8,128)(2,1)S(1)}, u32[]{:S(2)}, u32[]{:S(2)}) %collective-permute-start.35) | collective-permute-done | bytes 65568 | tf_op jit(solution)/shard_map/ppermute | solution.py:41
  420.0 10.5 %all-to-all-done.10 = bf16[8,4,32,768]{3,2,1,0:T(8,128)(2,1)} async-done(((bf16[8,4,32,768]{3,2,1,0:T(8,128)(2,1)}), bf16[8,4,32,768]{3,2,1,0:T(8,128)(2,1)}, u32[]{:S(2)}, u32[]{:S(2)}) %all-to-all-start.10) | async-done | bytes 1572896 | tf_op jit(solution)/shard_map/all_to_all | solution.py:639
  442.1 4.6 %all-to-all-done.11 = f32[32,1,384]{2,1,0:T(1,128)S(1)} async-done(((f32[32,1,384]{2,1,0:T(1,128)}), f32[32,1,384]{2,1,0:T(1,128)S(1)}, u32[]{:S(2)}, u32[]{:S(2)}) %all-to-all-start.11) | async-done | bytes 49184 | tf_op jit(solution)/shard_map/all_to_all | solution.py:685
  (370 shorter events, 205.9 us)
Async XLA Ops:
  7.2 57.3 %all-gather.7.cloned.1.call-start = ((), (), s32[]{:S(2)}) async-start(), calls=%async_computation.14 | async-start | bytes 1769472 | tf_op jit(solution)/shard_map/all_gather | solution.py:526
  19.5 20.6 %collective-permute-start.1 = (bf16[256,1024]{1,0:T(8,128)(2,1)S(1)}, bf16[256,1024]{1,0:T(8,128)(2,1)S(1)}, u32[]{:S(2)}, u32[]{:S(2)}) collective-permute-start(bf16[256,1024]{1,0:T(8,128)(2,1)S(1)} %copy-done.5), channel_id=1, source_target_pairs={{0,16},{8,24},{16,0},{24,8},{1,17},{9,25},{17,1},{25,9},{2,18},{10... | collective-permute-start | bytes 1572872 | tf_op jit(solution)/shard_map/ppermute | solution.py:41
  19.9 20.9 %collective-permute-start = (bf16[256,1024]{1,0:T(8,128)(2,1)S(1)}, bf16[256,1024]{1,0:T(8,128)(2,1)S(1)}, u32[]{:S(2)}, u32[]{:S(2)}) collective-permute-start(bf16[256,1024]{1,0:T(8,128)(2,1)S(1)} %copy-done.5), channel_id=1, source_target_pairs={{0,8},{8,0},{16,24},{24,16},{1,9},{9,1},{17,25},{25,17},{2,10},{10... | collective-permute-start | bytes 1572872 | tf_op jit(solution)/shard_map/ppermute | solution.py:41
  28.5 125.5 %all-gather.9.cloned.1.call-start = ((), (), s32[]{:S(2)}) async-start(), calls=%async_computation.15 | async-start | bytes 2949120 | tf_op jit(solution)/shard_map/all_gather | solution.py:528
  35.7 35.5 %all-to-all-start.5 = ((bf16[4,32,1024]{2,1,0:T(8,128)(2,1)}), bf16[4,32,1024]{2,1,0:T(8,128)(2,1)S(1)}, u32[]{:S(2)}, u32[]{:S(2)}) async-start(bf16[4,32,1024]{2,1,0:T(8,128)(2,1)} %copy.89), calls=%async_computation.5 | async-start | bytes 524288 | tf_op jit(solution)/shard_map/all_to_all | solution.py:474
  71.2 41.5 %all-to-all-start.3 = ((bf16[8,256,256]{2,1,0:T(8,128)(2,1)}), bf16[8,256,256]{2,1,0:T(8,128)(2,1)S(1)}, u32[]{:S(2)}, u32[]{:S(2)}) async-start(bf16[8,256,256]{2,1,0:T(8,128)(2,1)} %bitcast.175), calls=%async_computation.3 | async-start | bytes 2097152 | tf_op jit(solution)/shard_map/all_to_all | solution.py:466
  112.7 29.7 %all-to-all-start.2 = ((bf16[8,256,128]{2,1,0:T(8,128)(2,1)}), bf16[8,256,128]{2,1,0:T(8,128)(2,1)S(1)}, u32[]{:S(2)}, u32[]{:S(2)}) async-start(bf16[8,256,128]{2,1,0:T(8,128)(2,1)} %bitcast.15), calls=%async_computation.2 | async-start | bytes 1048576 | tf_op jit(solution)/shard_map/all_to_all | solution.py:466
  116.7 86.1 %all-gather.11.cloned.1.call-start = ((), (), s32[]{:S(2)}) async-start(), calls=%async_computation.16 | async-start | bytes 2359296 | tf_op jit(solution)/shard_map/all_gather | solution.py:533
  149.5 27.2 %all-to-all-start.4 = ((bf16[8,256,128]{2,1,0:T(8,128)(2,1)}), bf16[8,256,128]{2,1,0:T(8,128)(2,1)}, u32[]{:S(2)}, u32[]{:S(2)}) async-start(bf16[8,256,128]{2,1,0:T(8,128)(2,1)} %bitcast.22), calls=%async_computation.4 | async-start | bytes 1048576 | tf_op jit(solution)/shard_map/all_to_all | solution.py:470
  153.7 217.5 %reduce-scatter.2.cloned.1.call-start = ((), (), s32[]{:S(2)}) async-start(), calls=%async_computation.13 | async-start | bytes 4718592 | tf_op jit(solution)/shard_map/reduce_scatter | solution.py:587
  157.3 24.7 %collective-permute-start.12 = (bf16[256,1024]{1,0:T(8,128)(2,1)}, bf16[256,1024]{1,0:T(8,128)(2,1)}, u32[]{:S(2)}, u32[]{:S(2)}) collective-permute-start(bf16[256,1024]{1,0:T(8,128)(2,1)} %param.19), channel_id=1, source_target_pairs={{0,16},{16,0},{1,17},{17,1},{2,18},{18,2},{3,19},{19,3},{4,20},{20... | collective-permute-start | bytes 1572872 | tf_op jit(solution)/shard_map/ppermute | solution.py:41
  157.9 24.8 %collective-permute-start.6 = (bf16[256,1024]{1,0:T(8,128)(2,1)}, bf16[256,1024]{1,0:T(8,128)(2,1)}, u32[]{:S(2)}, u32[]{:S(2)}) collective-permute-start(bf16[256,1024]{1,0:T(8,128)(2,1)} %bitcast.31), channel_id=1, source_target_pairs={{0,8},{8,0},{16,24},{24,16},{1,9},{9,1},{17,25},{25,17},{2,10},{10... | collective-permute-start | bytes 1572872 | tf_op jit(solution)/shard_map/ppermute | solution.py:41
  183.0 17.1 %collective-permute-start.13 = (bf16[256,1024]{1,0:T(8,128)(2,1)}, bf16[256,1024]{1,0:T(8,128)(2,1)}, u32[]{:S(2)}, u32[]{:S(2)}) collective-permute-start(bf16[256,1024]{1,0:T(8,128)(2,1)} %collective-permute-done.12), channel_id=1, source_target_pairs={{0,8},{8,0},{1,9},{9,1},{2,10},{10,2},{3,11},{11,3},{4,12},{12,4},... | collective-permute-start | bytes 1572872 | tf_op jit(solution)/shard_map/ppermute | solution.py:41
  263.7 32.6 %all-to-all-start.6 = ((bf16[8,256,128]{2,1,0:T(8,128)(2,1)}), bf16[8,256,128]{2,1,0:T(8,128)(2,1)S(1)}, u32[]{:S(2)}, u32[]{:S(2)}) async-start(bf16[8,256,128]{2,1,0:T(8,128)(2,1)} %bitcast.191), calls=%async_computation.6 | async-start | bytes 1048576 | tf_op jit(solution)/shard_map/all_to_all | solution.py:466
  301.3 44.2 %collective-permute-start.25 = (bf16[256,1024]{1,0:T(8,128)(2,1)}, bf16[256,1024]{1,0:T(8,128)(2,1)}, u32[]{:S(2)}, u32[]{:S(2)}) collective-permute-start(bf16[256,1024]{1,0:T(8,128)(2,1)} %get-tuple-element.106), channel_id=1, source_target_pairs={{0,8},{8,0},{16,24},{24,16},{1,9},{9,1},{17,25},{25,17},{2,10},{10... | collective-permute-start | bytes 1572872 | tf_op jit(solution)/shard_map/ppermute | solution.py:41
  301.3 56.2 %collective-permute-start.24 = (bf16[256,1024]{1,0:T(8,128)(2,1)}, bf16[256,1024]{1,0:T(8,128)(2,1)}, u32[]{:S(2)}, u32[]{:S(2)}) collective-permute-start(bf16[256,1024]{1,0:T(8,128)(2,1)} %get-tuple-element.105), channel_id=1, source_target_pairs={{0,8},{8,0},{16,24},{24,16},{1,9},{9,1},{17,25},{25,17},{2,10},{10... | collective-permute-start | bytes 1572872 | tf_op jit(solution)/shard_map/ppermute | solution.py:41
  312.2 25.6 %all-to-all-start.8 = ((bf16[8,256,128]{2,1,0:T(8,128)(2,1)}), bf16[8,256,128]{2,1,0:T(8,128)(2,1)S(1)}, u32[]{:S(2)}, u32[]{:S(2)}) async-start(bf16[8,256,128]{2,1,0:T(8,128)(2,1)} %bitcast.49), calls=%async_computation.8 | async-start | bytes 1048576 | tf_op jit(solution)/shard_map/all_to_all | solution.py:470
  321.1 27.5 %collective-permute-start.22 = (bf16[256,1024]{1,0:T(8,128)(2,1)}, bf16[256,1024]{1,0:T(8,128)(2,1)}, u32[]{:S(2)}, u32[]{:S(2)}) collective-permute-start(bf16[256,1024]{1,0:T(8,128)(2,1)} %unstack.124), channel_id=1, source_target_pairs={{0,8},{8,0},{1,9},{9,1},{2,10},{10,2},{3,11},{11,3},{4,12},{12,4},... | collective-permute-start | bytes 1572872 | tf_op jit(solution)/shard_map/ppermute | solution.py:41
  337.8 32.0 %all-to-all-start.7 = ((bf16[8,256,256]{2,1,0:T(8,128)(2,1)}), bf16[8,256,256]{2,1,0:T(8,128)(2,1)S(1)}, u32[]{:S(2)}, u32[]{:S(2)}) async-start(bf16[8,256,256]{2,1,0:T(8,128)(2,1)} %bitcast.46), calls=%async_computation.7 | async-start | bytes 2097152 | tf_op jit(solution)/shard_map/all_to_all | solution.py:470
  345.5 49.0 %collective-permute-start.21 = (bf16[256,1024]{1,0:T(8,128)(2,1)}, bf16[256,1024]{1,0:T(8,128)(2,1)}, u32[]{:S(2)}, u32[]{:S(2)}) collective-permute-start(bf16[256,1024]{1,0:T(8,128)(2,1)} %unstack.125), channel_id=1, source_target_pairs={{0,8},{8,0},{1,9},{9,1},{2,10},{10,2},{3,11},{11,3},{4,12},{12,4},... | collective-permute-start | bytes 1572872 | tf_op jit(solution)/shard_map/ppermute | solution.py:41
  350.6 43.9 %collective-permute-start.23 = (bf16[256,1024]{1,0:T(8,128)(2,1)}, bf16[256,1024]{1,0:T(8,128)(2,1)}, u32[]{:S(2)}, u32[]{:S(2)}) collective-permute-start(bf16[256,1024]{1,0:T(8,128)(2,1)} %fusion.31), channel_id=1, source_target_pairs={{0,16},{16,0},{1,17},{17,1},{2,18},{18,2},{3,19},{19,3},{4,20},{20... | collective-permute-start | bytes 1572872 | tf_op jit(solution)/shard_map/ppermute | solution.py:41
  371.2 18.2 %all-to-all-start.9 = ((bf16[8,32,1024]{2,1,0:T(8,128)(2,1)}), bf16[8,32,1024]{2,1,0:T(8,128)(2,1)S(1)}, u32[]{:S(2)}, u32[]{:S(2)}) async-start(bf16[8,32,1024]{2,1,0:T(8,128)(2,1)} %bitcast.56), calls=%async_computation.10 | async-start | bytes 1048576 | tf_op jit(solution)/shard_map/all_to_all | solution.py:628
  389.4 41.1 %all-to-all-start.10 = ((bf16[8,4,32,768]{3,2,1,0:T(8,128)(2,1)}), bf16[8,4,32,768]{3,2,1,0:T(8,128)(2,1)}, u32[]{:S(2)}, u32[]{:S(2)}) async-start(bf16[8,4,32,768]{3,2,1,0:T(8,128)(2,1)} %pad_maximum_fusion.3), calls=%async_computation.11 | async-start | bytes 3145728 | tf_op jit(solution)/shard_map/all_to_all | solution.py:639
  397.6 21.1 %collective-permute-start.27 = (bf16[256,1024]{1,0:T(8,128)(2,1)}, bf16[256,1024]{1,0:T(8,128)(2,1)}, u32[]{:S(2)}, u32[]{:S(2)}) collective-permute-start(bf16[256,1024]{1,0:T(8,128)(2,1)} %get-tuple-element.70), channel_id=1, source_target_pairs={{0,8},{8,0},{16,24},{24,16},{1,9},{9,1},{17,25},{25,17},{2,10},{10... | collective-permute-start | bytes 1572872 | tf_op jit(solution)/shard_map/ppermute | solution.py:41
  (68 other events, 558.0 us)
Sparse Core Ops, SparseCore 0:
  19.3 45.0 all-gather.6
  67.2 76.4 all-gather.8
  146.4 56.3 all-gather.10
  245.4 107.5 reduce-scatter.1

commit v5 on v4

--- a/solution.py
+++ b/solution.py
@@ -560,6 +560,9 @@
         context, *kept = split_forward(slopes, qkv, pair_heads, rows)
     context_tok = collect(context).reshape(dp_count, rows, dp_width)
     context_tok = jnp.concatenate(swap_dp([context_tok[k] for k in range(dp_count)]), axis=1)
+    grads_of = [jnp.concatenate(grad_pieces[place::x_count], axis=0) for place in range(x_count)]
+    grad_hidden = [dot_nt(grads, out_weight) for grads in grads_of]
+    context_tok, grads_of, grad_hidden = lax.optimization_barrier((context_tok, grads_of, grad_hidden))
     middle = rows_in + (dot_nn(context_tok, dense_weight) + offsets[3])
     normed_two = norm_rows(middle, gains_row[1], offsets[4]).astype(BF16)
 
@@ -569,11 +572,11 @@
     branch, grad_two, hiddens = [None] * len(pieces), [None] * len(pieces), []
     for place in range(x_count):
         normed = jnp.concatenate(pieces[place::x_count], axis=0)
-        grads = jnp.concatenate(grad_pieces[place::x_count], axis=0)
+        grads = grads_of[place]
         hidden_pre = dot_nn(normed, in_weight) + in_offset
         hidden, gelu_pull = jax.vjp(jax.nn.gelu, hidden_pre)
         hidden = hidden.astype(BF16)
-        grad_pre = gelu_pull(dot_nt(grads, out_weight))[0].astype(BF16)
+        grad_pre = gelu_pull(grad_hidden[place])[0].astype(BF16)
         grad_two[place::x_count] = list(dot_nt(grad_pre, in_weight).reshape(2, rows, width))
         hiddens.append(hidden)
         grad_in_offset += jnp.sum(grad_pre.astype(F32), axis=0)

time: 468 us -> 467 us (level)
  waiting for transfers between devices: 193 us -> 185 us
  other arithmetic: 39.4 us -> 44.2 us
    unnamed x90 -> x96, local copies, waits for them, and re-layouts: 12.1 us -> 15.8 us
  transfers between devices with their start and end apart: 51 -> 51, of which waited for: 23 -> 21; matrix products, arithmetic and copies ran while one was open for 25% -> 26% of each run, Pallas kernels for 7% -> 7%
where the time goes in v5:
time: 467 us; the launch traced here: 459 us
  waiting for transfers between devices  185 us (40%)
  starting transfers between devices  64.3 us (14%)
  local copies, waits for them, and re-layouts  57 us (12%)
  matrix products  50.3 us (11%)
  other arithmetic  44.2 us (9%)
  Pallas kernels  32.8 us (7%)
  between operations  15.4 us (3%)
  blocking collectives  9.45 us (2%)
    all_to_all x3, waiting for transfers between devices, spread(): lax.all_to_all(sent, pair_axes, split_axis=0, concat_axis=0, tiled=True)  77 us
    ppermute x36, waiting for transfers between devices, exchange(): return lax.ppermute(value, axis, [(i, i ^ bit) for i in range(count)])  52.1 us
    dot_general x7, matrix products, dot_nt(): lax.dot_general(a, b, (((1,), (1,)), ((), ())), preferred_element_type=F32)  20.2 us
    ppermute x36, starting transfers between devices, exchange(): return lax.ppermute(value, axis, [(i, i ^ bit) for i in range(count)])  19.7 us
    pallas_call x2, Pallas kernels, attend_backward(): pl.pallas_call(functools.partial(backward_kernel, head, head_dim, block),...  19.5 us
    dot_general x7, matrix products, dot_nn(): lax.dot_general(a, b, (((1,), (0,)), ((), ())), preferred_element_type=F32)  17.7 us
    all_gather x1, waiting for transfers between devices, on_device(): lax.all_gather(qkv_part, SEQ_AXES, axis=0, tiled=False)  16.4 us
    unnamed x96, local copies, waits for them, and re-layouts  15.8 us
  transfers between devices with their start and end apart: 51, of which 21 were waited for; matrix products, arithmetic and copies ran while one was open for 26% of the time, Pallas kernels for 7%

profile of v5, /device:TPU:0, one launch (start us, length us, event | category | flops | bytes accessed | tf_op | source)
XLA Modules:
  0.0 458.7 jit_solution(983313277978621863)
XLA Ops:
  9.7 9.4 %all_to_all.99 = bf16[4,32,768]{2,1,0:T(8,128)(2,1)} all-to-all(bf16[4,32,768]{2,1,0:T(8,128)(2,1)S(1)} %maximum_bitcast_fusion.1), channel_id=1, replica_groups=mesh['x'=2,'core'=2,'sp'=4,'blk'=2] {'x','core'}, dimensions={0} | all-to-all | bytes 393216 | tf_op jit(solution)/shard_map/all_to_all | solution.py:474
  22.0 6.5 %all-to-all-start.1 = ((bf16[32,2,192]{2,1,0:T(2,128)(2,1)}), bf16[32,2,192]{2,1,0:T(2,128)(2,1)S(1)}, u32[]{:S(2)}, u32[]{:S(2)}) async-start(bf16[32,2,192]{2,1,0:T(2,128)(2,1)} %reshape.444), calls=%async_computation.1 | async-start | bytes 65536 | tf_op jit(solution)/shard_map/all_to_all | solution.py:505
  30.3 5.4 %all-to-all-done.1 = bf16[32,2,192]{2,1,0:T(2,128)(2,1)S(1)} async-done(((bf16[32,2,192]{2,1,0:T(2,128)(2,1)}), bf16[32,2,192]{2,1,0:T(2,128)(2,1)S(1)}, u32[]{:S(2)}, u32[]{:S(2)}) %all-to-all-start.1) | async-done | bytes 24608 | tf_op jit(solution)/shard_map/all_to_all | solution.py:505
  48.1 16.4 %all-gather.7.cloned.1.call-done = bf16[32,32,768]{2,1,0:T(8,128)(2,1)} async-done(((bf16[4,32,768]{2,1,0:T(8,128)(2,1)}), bf16[32,32,768]{2,1,0:T(8,128)(2,1)}) %all-gather.7.cloned.1.call-update) | async-done | bytes 1572880 | tf_op jit(solution)/shard_map/all_gather | solution.py:526
  81.5 31.3 %all-to-all-done.3 = bf16[8,256,256]{2,1,0:T(8,128)(2,1)S(1)} async-done(((bf16[8,256,256]{2,1,0:T(8,128)(2,1)}), bf16[8,256,256]{2,1,0:T(8,128)(2,1)S(1)}, u32[]{:S(2)}, u32[]{:S(2)}) %all-to-all-start.3) | async-done | bytes 1048608 | tf_op jit(solution)/shard_map/all_to_all | solution.py:466
  118.0 6.2 %attend_forward.2 = (f32[64,2048]{1,0:T(8,128)S(1)}, f32[1,2048]{1,0:T(1,128)S(1)}) custom-call(f32[2]{0:T(128)S(1)} %dynamic_slice.30.slopes_ref, bf16[2048,256]{1,0:T(8,128)(2,1)S(1)} %bitcast.152, bf16[2048,256]{1,0:T(8,128)(2,1)S(1)} %bitcast.153), custom_call_target="tpu_custom_call" | custom-call | flops 8589934592 | bytes 2097152 | tf_op jit(solution)/shard_map/attend_forward/pallas_call | solution.py:311
  124.2 18.2 %all-to-all-done.2 = bf16[8,256,128]{2,1,0:T(8,128)(2,1)S(1)} async-done(((bf16[8,256,128]{2,1,0:T(8,128)(2,1)}), bf16[8,256,128]{2,1,0:T(8,128)(2,1)S(1)}, u32[]{:S(2)}, u32[]{:S(2)}) %all-to-all-start.2) | async-done | bytes 524320 | tf_op jit(solution)/shard_map/all_to_all | solution.py:466
  142.4 7.1 %attend_forward.3 = (f32[64,2048]{1,0:T(8,128)S(1)}, f32[1,2048]{1,0:T(1,128)S(1)}, bf16[2048,128]{1,0:T(8,128)(2,1)}) custom-call(f32[2]{0:T(128)S(1)} %dynamic_slice.30.slopes_ref, bf16[2048,128]{1,0:T(8,128)(2,1)S(1)} %bitcast.158, bf16[2048,256]{1,0:T(8,128)(2,1)S(1)} %bitcast.154, f32[64,2048]{1,0:T(8,128)S(1)} %get-tuple-element.51.refs_0_.ctx_t_ref), custom_call_target="tpu_custom_call" | custom-call | flops 8589934592 | bytes 2097152 | tf_op jit(solution)/shard_map/attend_forward/pallas_call | solution.py:311
  149.5 4.1 all-to-all-start.4
  169.3 4.4 collective-permute-done.10
  181.5 4.5 fusion.76
  193.7 12.7 %collective-permute-done.14 = bf16[256,1024]{1,0:T(8,128)(2,1)} collective-permute-done((bf16[256,1024]{1,0:T(8,128)(2,1)S(1)}, bf16[256,1024]{1,0:T(8,128)(2,1)}, u32[]{:S(2)}, u32[]{:S(2)}) %collective-permute-start.14) | collective-permute-done | bytes 524320 | tf_op jit(solution)/shard_map/ppermute | solution.py:41
  233.6 8.6 %collective-permute-done.17 = bf16[256,1024]{1,0:T(8,128)(2,1)S(1)} collective-permute-done((bf16[256,1024]{1,0:T(8,128)(2,1)S(1)}, bf16[256,1024]{1,0:T(8,128)(2,1)S(1)}, u32[]{:S(2)}, u32[]{:S(2)}) %collective-permute-start.17) | collective-permute-done | bytes 524320 | tf_op jit(solution)/shard_map/ppermute | solution.py:41
  253.7 4.6 collective-permute-done.19
  267.3 27.5 %all-to-all-done.6 = bf16[8,256,128]{2,1,0:T(8,128)(2,1)S(1)} async-done(((bf16[8,256,128]{2,1,0:T(8,128)(2,1)}), bf16[8,256,128]{2,1,0:T(8,128)(2,1)S(1)}, u32[]{:S(2)}, u32[]{:S(2)}) %all-to-all-start.6) | async-done | bytes 524320 | tf_op jit(solution)/shard_map/all_to_all | solution.py:466
  300.4 9.6 %attend_backward.2 = (bf16[2048,128]{1,0:T(8,128)(2,1)}, bf16[2048,128]{1,0:T(8,128)(2,1)S(1)}) custom-call(f32[2]{0:T(128)S(1)} %dynamic_slice.30.slopes_ref, bf16[2048,128]{1,0:T(8,128)(2,1)S(1)} %bitcast.159, bf16[2048,256]{1,0:T(8,128)(2,1)S(1)} %bitcast.155, bf16[2048,128]{1,0:T(8,128)(2,1)S(1)} %bitcast.160, ...), custom_call_target="tpu_custom_call" | custom-call | flops 10737418240 | bytes 4194304 | tf_op jit(solution)/shard_map/attend_backward/pallas_call | solution.py:339
  319.8 9.9 %attend_backward.3 = bf16[2048,256]{1,0:T(8,128)(2,1)} custom-call(f32[2]{0:T(128)S(1)} %dynamic_slice.30.slopes_ref, bf16[2048,256]{1,0:T(8,128)(2,1)S(1)} %bitcast.156, bf16[2048,256]{1,0:T(8,128)(2,1)S(1)} %bitcast.157, bf16[2048,128]{1,0:T(8,128)(2,1)S(1)} %bitcast.161, f32[64,2048]{1,0:T(8,128)S(1)} %get-tuple-element.51.refs_0_.ctx_t_ref, ...), custom_call_target="tpu_custom_call" | custom-call | flops 10737418240 | bytes 4194304 | tf_op jit(solution)/shard_map/attend_backward/pallas_call | solution.py:339
  329.7 6.4 %all-to-all-done.8 = bf16[8,256,128]{2,1,0:T(8,128)(2,1)S(1)} async-done(((bf16[8,256,128]{2,1,0:T(8,128)(2,1)}), bf16[8,256,128]{2,1,0:T(8,128)(2,1)S(1)}, u32[]{:S(2)}, u32[]{:S(2)}) %all-to-all-start.8) | async-done | bytes 524320 | tf_op jit(solution)/shard_map/all_to_all | solution.py:470
  355.8 4.8 %collective-permute-done.26 = bf16[256,1024]{1,0:T(8,128)(2,1)S(1)} collective-permute-done((bf16[256,1024]{1,0:T(8,128)(2,1)S(1)}, bf16[256,1024]{1,0:T(8,128)(2,1)S(1)}, u32[]{:S(2)}, u32[]{:S(2)}) %collective-permute-start.26) | collective-permute-done | bytes 524320 | tf_op jit(solution)/shard_map/ppermute | solution.py:41
  362.7 5.8 %all-to-all-done.7 = bf16[8,256,256]{2,1,0:T(8,128)(2,1)S(1)} async-done(((bf16[8,256,256]{2,1,0:T(8,128)(2,1)}), bf16[8,256,256]{2,1,0:T(8,128)(2,1)S(1)}, u32[]{:S(2)}, u32[]{:S(2)}) %all-to-all-start.7) | async-done | bytes 1048608 | tf_op jit(solution)/shard_map/all_to_all | solution.py:470
  388.1 4.5 all-to-all-start.10
  405.4 10.7 %collective-permute-done.35 = bf16[1,32,1024]{2,1,0:T(8,128)(2,1)S(1)} collective-permute-done((bf16[1,32,1024]{2,1,0:T(8,128)(2,1)S(1)}, bf16[1,32,1024]{2,1,0:T(8,128)(2,1)S(1)}, u32[]{:S(2)}, u32[]{:S(2)}) %collective-permute-start.35) | collective-permute-done | bytes 65568 | tf_op jit(solution)/shard_map/ppermute | solution.py:41
  418.3 11.0 %all-to-all-done.10 = bf16[8,4,32,768]{3,2,1,0:T(8,128)(2,1)} async-done(((bf16[8,4,32,768]{3,2,1,0:T(8,128)(2,1)}), bf16[8,4,32,768]{3,2,1,0:T(8,128)(2,1)}, u32[]{:S(2)}, u32[]{:S(2)}) %all-to-all-start.10) | async-done | bytes 1572896 | tf_op jit(solution)/shard_map/all_to_all | solution.py:642
  441.3 4.6 %all-to-all-done.11 = f32[32,1,384]{2,1,0:T(1,128)S(1)} async-done(((f32[32,1,384]{2,1,0:T(1,128)}), f32[32,1,384]{2,1,0:T(1,128)S(1)}, u32[]{:S(2)}, u32[]{:S(2)}) %all-to-all-start.11) | async-done | bytes 49184 | tf_op jit(solution)/shard_map/all_to_all | solution.py:688
  (378 shorter events, 209.0 us)
Async XLA Ops:
  7.2 57.3 %all-gather.7.cloned.1.call-start = ((), (), s32[]{:S(2)}) async-start(), calls=%async_computation.14 | async-start | bytes 1769472 | tf_op jit(solution)/shard_map/all_gather | solution.py:526
  19.5 20.6 %collective-permute-start.1 = (bf16[256,1024]{1,0:T(8,128)(2,1)S(1)}, bf16[256,1024]{1,0:T(8,128)(2,1)S(1)}, u32[]{:S(2)}, u32[]{:S(2)}) collective-permute-start(bf16[256,1024]{1,0:T(8,128)(2,1)S(1)} %copy-done.5), channel_id=1, source_target_pairs={{0,16},{8,24},{16,0},{24,8},{1,17},{9,25},{17,1},{25,9},{2,18},{10... | collective-permute-start | bytes 1572872 | tf_op jit(solution)/shard_map/ppermute | solution.py:41
  19.9 20.9 %collective-permute-start = (bf16[256,1024]{1,0:T(8,128)(2,1)S(1)}, bf16[256,1024]{1,0:T(8,128)(2,1)S(1)}, u32[]{:S(2)}, u32[]{:S(2)}) collective-permute-start(bf16[256,1024]{1,0:T(8,128)(2,1)S(1)} %copy-done.5), channel_id=1, source_target_pairs={{0,8},{8,0},{16,24},{24,16},{1,9},{9,1},{17,25},{25,17},{2,10},{10... | collective-permute-start | bytes 1572872 | tf_op jit(solution)/shard_map/ppermute | solution.py:41
  28.5 129.4 %all-gather.9.cloned.1.call-start = ((), (), s32[]{:S(2)}) async-start(), calls=%async_computation.15 | async-start | bytes 2949120 | tf_op jit(solution)/shard_map/all_gather | solution.py:528
  35.7 35.5 %all-to-all-start.5 = ((bf16[4,32,1024]{2,1,0:T(8,128)(2,1)}), bf16[4,32,1024]{2,1,0:T(8,128)(2,1)S(1)}, u32[]{:S(2)}, u32[]{:S(2)}) async-start(bf16[4,32,1024]{2,1,0:T(8,128)(2,1)} %copy.89), calls=%async_computation.5 | async-start | bytes 524288 | tf_op jit(solution)/shard_map/all_to_all | solution.py:474
  71.2 41.5 %all-to-all-start.3 = ((bf16[8,256,256]{2,1,0:T(8,128)(2,1)}), bf16[8,256,256]{2,1,0:T(8,128)(2,1)S(1)}, u32[]{:S(2)}, u32[]{:S(2)}) async-start(bf16[8,256,256]{2,1,0:T(8,128)(2,1)} %bitcast.177), calls=%async_computation.3 | async-start | bytes 2097152 | tf_op jit(solution)/shard_map/all_to_all | solution.py:466
  74.8 42.7 %collective-permute-start.7 = (bf16[256,1024]{1,0:T(8,128)(2,1)}, bf16[256,1024]{1,0:T(8,128)(2,1)}, u32[]{:S(2)}, u32[]{:S(2)}) collective-permute-start(bf16[256,1024]{1,0:T(8,128)(2,1)} %param.19), channel_id=1, source_target_pairs={{0,16},{16,0},{1,17},{17,1},{2,18},{18,2},{3,19},{19,3},{4,20},{20... | collective-permute-start | bytes 1572872 | tf_op jit(solution)/shard_map/ppermute | solution.py:41
  112.7 29.7 %all-to-all-start.2 = ((bf16[8,256,128]{2,1,0:T(8,128)(2,1)}), bf16[8,256,128]{2,1,0:T(8,128)(2,1)S(1)}, u32[]{:S(2)}, u32[]{:S(2)}) async-start(bf16[8,256,128]{2,1,0:T(8,128)(2,1)} %bitcast.15), calls=%async_computation.2 | async-start | bytes 1048576 | tf_op jit(solution)/shard_map/all_to_all | solution.py:466
  116.7 89.7 %all-gather.11.cloned.1.call-start = ((), (), s32[]{:S(2)}) async-start(), calls=%async_computation.16 | async-start | bytes 2359296 | tf_op jit(solution)/shard_map/all_gather | solution.py:533
  117.4 44.0 %collective-permute-start.6 = (bf16[256,1024]{1,0:T(8,128)(2,1)}, bf16[256,1024]{1,0:T(8,128)(2,1)}, u32[]{:S(2)}, u32[]{:S(2)}) collective-permute-start(bf16[256,1024]{1,0:T(8,128)(2,1)} %param.19), channel_id=1, source_target_pairs={{0,8},{8,0},{1,9},{9,1},{2,10},{10,2},{3,11},{11,3},{4,12},{12,4},... | collective-permute-start | bytes 1572872 | tf_op jit(solution)/shard_map/ppermute | solution.py:41
  117.5 45.8 %collective-permute-start.8 = (bf16[256,1024]{1,0:T(8,128)(2,1)}, bf16[256,1024]{1,0:T(8,128)(2,1)}, u32[]{:S(2)}, u32[]{:S(2)}) collective-permute-start(bf16[256,1024]{1,0:T(8,128)(2,1)} %collective-permute-done.7), channel_id=1, source_target_pairs={{0,8},{8,0},{1,9},{9,1},{2,10},{10,2},{3,11},{11,3},{4,12},{12,4},... | collective-permute-start | bytes 1572872 | tf_op jit(solution)/shard_map/ppermute | solution.py:41
  149.5 26.8 %all-to-all-start.4 = ((bf16[8,256,128]{2,1,0:T(8,128)(2,1)}), bf16[8,256,128]{2,1,0:T(8,128)(2,1)}, u32[]{:S(2)}, u32[]{:S(2)}) async-start(bf16[8,256,128]{2,1,0:T(8,128)(2,1)} %bitcast.22), calls=%async_computation.4 | async-start | bytes 1048576 | tf_op jit(solution)/shard_map/all_to_all | solution.py:470
  153.7 216.2 %reduce-scatter.2.cloned.1.call-start = ((), (), s32[]{:S(2)}) async-start(), calls=%async_computation.13 | async-start | bytes 4718592 | tf_op jit(solution)/shard_map/reduce_scatter | solution.py:590
  165.3 22.7 %collective-permute-start.9 = (bf16[256,1024]{1,0:T(8,128)(2,1)}, bf16[256,1024]{1,0:T(8,128)(2,1)}, u32[]{:S(2)}, u32[]{:S(2)}) collective-permute-start(bf16[256,1024]{1,0:T(8,128)(2,1)} %bitcast.32), channel_id=1, source_target_pairs={{0,8},{8,0},{16,24},{24,16},{1,9},{9,1},{17,25},{25,17},{2,10},{10... | collective-permute-start | bytes 1572872 | tf_op jit(solution)/shard_map/ppermute | solution.py:41
  262.2 32.7 %all-to-all-start.6 = ((bf16[8,256,128]{2,1,0:T(8,128)(2,1)}), bf16[8,256,128]{2,1,0:T(8,128)(2,1)S(1)}, u32[]{:S(2)}, u32[]{:S(2)}) async-start(bf16[8,256,128]{2,1,0:T(8,128)(2,1)} %bitcast.193), calls=%async_computation.6 | async-start | bytes 1048576 | tf_op jit(solution)/shard_map/all_to_all | solution.py:466
  299.9 43.9 %collective-permute-start.25 = (bf16[256,1024]{1,0:T(8,128)(2,1)}, bf16[256,1024]{1,0:T(8,128)(2,1)}, u32[]{:S(2)}, u32[]{:S(2)}) collective-permute-start(bf16[256,1024]{1,0:T(8,128)(2,1)} %get-tuple-element.116), channel_id=1, source_target_pairs={{0,8},{8,0},{16,24},{24,16},{1,9},{9,1},{17,25},{25,17},{2,10},{10... | collective-permute-start | bytes 1572872 | tf_op jit(solution)/shard_map/ppermute | solution.py:41
  300.0 55.9 %collective-permute-start.24 = (bf16[256,1024]{1,0:T(8,128)(2,1)}, bf16[256,1024]{1,0:T(8,128)(2,1)}, u32[]{:S(2)}, u32[]{:S(2)}) collective-permute-start(bf16[256,1024]{1,0:T(8,128)(2,1)} %get-tuple-element.115), channel_id=1, source_target_pairs={{0,8},{8,0},{16,24},{24,16},{1,9},{9,1},{17,25},{25,17},{2,10},{10... | collective-permute-start | bytes 1572872 | tf_op jit(solution)/shard_map/ppermute | solution.py:41
  310.8 25.3 %all-to-all-start.8 = ((bf16[8,256,128]{2,1,0:T(8,128)(2,1)}), bf16[8,256,128]{2,1,0:T(8,128)(2,1)S(1)}, u32[]{:S(2)}, u32[]{:S(2)}) async-start(bf16[8,256,128]{2,1,0:T(8,128)(2,1)} %bitcast.49), calls=%async_computation.8 | async-start | bytes 1048576 | tf_op jit(solution)/shard_map/all_to_all | solution.py:470
  319.8 26.7 %collective-permute-start.22 = (bf16[256,1024]{1,0:T(8,128)(2,1)}, bf16[256,1024]{1,0:T(8,128)(2,1)}, u32[]{:S(2)}, u32[]{:S(2)}) collective-permute-start(bf16[256,1024]{1,0:T(8,128)(2,1)} %unstack.124), channel_id=1, source_target_pairs={{0,8},{8,0},{1,9},{9,1},{2,10},{10,2},{3,11},{11,3},{4,12},{12,4},... | collective-permute-start | bytes 1572872 | tf_op jit(solution)/shard_map/ppermute | solution.py:41
  336.1 32.5 %all-to-all-start.7 = ((bf16[8,256,256]{2,1,0:T(8,128)(2,1)}), bf16[8,256,256]{2,1,0:T(8,128)(2,1)S(1)}, u32[]{:S(2)}, u32[]{:S(2)}) async-start(bf16[8,256,256]{2,1,0:T(8,128)(2,1)} %bitcast.46), calls=%async_computation.7 | async-start | bytes 2097152 | tf_op jit(solution)/shard_map/all_to_all | solution.py:470
  343.8 49.5 %collective-permute-start.21 = (bf16[256,1024]{1,0:T(8,128)(2,1)}, bf16[256,1024]{1,0:T(8,128)(2,1)}, u32[]{:S(2)}, u32[]{:S(2)}) collective-permute-start(bf16[256,1024]{1,0:T(8,128)(2,1)} %unstack.125), channel_id=1, source_target_pairs={{0,8},{8,0},{1,9},{9,1},{2,10},{10,2},{3,11},{11,3},{4,12},{12,4},... | collective-permute-start | bytes 1572872 | tf_op jit(solution)/shard_map/ppermute | solution.py:41
  348.5 44.8 %collective-permute-start.23 = (bf16[256,1024]{1,0:T(8,128)(2,1)}, bf16[256,1024]{1,0:T(8,128)(2,1)}, u32[]{:S(2)}, u32[]{:S(2)}) collective-permute-start(bf16[256,1024]{1,0:T(8,128)(2,1)} %fusion.31), channel_id=1, source_target_pairs={{0,16},{16,0},{1,17},{17,1},{2,18},{18,2},{3,19},{19,3},{4,20},{20... | collective-permute-start | bytes 1572872 | tf_op jit(solution)/shard_map/ppermute | solution.py:41
  388.1 41.1 %all-to-all-start.10 = ((bf16[8,4,32,768]{3,2,1,0:T(8,128)(2,1)}), bf16[8,4,32,768]{3,2,1,0:T(8,128)(2,1)}, u32[]{:S(2)}, u32[]{:S(2)}) async-start(bf16[8,4,32,768]{3,2,1,0:T(8,128)(2,1)} %pad_maximum_fusion.3), calls=%async_computation.11 | async-start | bytes 3145728 | tf_op jit(solution)/shard_map/all_to_all | solution.py:642
  396.4 20.6 %collective-permute-start.27 = (bf16[256,1024]{1,0:T(8,128)(2,1)}, bf16[256,1024]{1,0:T(8,128)(2,1)}, u32[]{:S(2)}, u32[]{:S(2)}) collective-permute-start(bf16[256,1024]{1,0:T(8,128)(2,1)} %get-tuple-element.80), channel_id=1, source_target_pairs={{0,8},{8,0},{16,24},{24,16},{1,9},{9,1},{17,25},{25,17},{2,10},{10... | collective-permute-start | bytes 1572872 | tf_op jit(solution)/shard_map/ppermute | solution.py:41
  (71 other events, 561.9 us)
Sparse Core Ops, SparseCore 0:
  19.3 45.0 all-gather.6
  67.2 76.4 all-gather.8
  145.9 56.1 all-gather.10
  243.5 108.2 reduce-scatter.1
